TPU v7x, 32 devices: a whole 2x2x4 slice. The times are simulated.
32 devices in a mesh: batch: 4 (over y, x), node: 8 (over z, core).
Axes of the slice: x: 2, y: 2, z: 4, core: 2. Of those that a mesh axis runs over, the one named last changes fastest.
Arguments:
- params: float32 [360448], P(('batch', 'node'))
- moment1: float32 [360448], P(('batch', 'node')), may hold values from -0.0234375 to 0.0234375
- moment2: float32 [360448], P(('batch', 'node')), may hold values from 1.9e-06 to 0.00015
- memory: float32 [4, 65536, 100], P('batch', 'node'), may hold values from -4 to 4
- mailbox: bfloat16 [4, 65536, 386], P('batch', 'node'), may hold values from -4 to 4
- mail_time: int32 [4, 65536], P('batch', 'node'), may hold values from 2048 to 4095
- update_time: int32 [4, 65536], P('batch', 'node'), may hold values from 0 to 2047
- node_feat: bfloat16 [65536, 413], P('node'), may hold values from -4 to 4
- req_rows: int32 [4, 8, 8, 1024], P('batch', 'node'), may hold values from 0 to 8191, as said below
- req_count: int32 [4, 8, 8], P('batch', 'node'), may hold values from 1 to 1024, 4096 in all within a row
- root_live: int32 [4, 8, 3, 512], P('batch', 'node'), may hold values from 0 to 4095, as said below
- nbr_live: int32 [4, 8, 1536, 10], P('batch', 'node'), may hold values from 0 to 4095
- nbr_dt: int32 [4, 8, 1536, 10], P('batch', 'node'), may hold values from 0 to 4095
- nbr_edge: bfloat16 [4, 8, 1536, 10, 186], P('batch', 'node'), may hold values from -4 to 4
- ev_edge: bfloat16 [4, 8, 512, 186], P('batch', 'node'), may hold values from -4 to 4
- ev_time: int32 [4, 8, 512], P('batch', 'node'), may hold values from 4096 to 8191
- neg_count: int32 [4, 8, 512], P('batch', 'node'), may hold values from 1 to 8
Outputs:
- loss_sum: float32 [], replicated
- loss_weight: float32 [], replicated
- grad_norm: float32 [], replicated
- params_new: float32 [360448], P(('batch', 'node'))
- moment1_new: float32 [360448], P(('batch', 'node'))
- moment2_new: float32 [360448], P(('batch', 'node'))
- params_low: bfloat16 [360448], P(('batch', 'node'))
- memory_new: float32 [4, 65536, 100], P('batch', 'node')
- mailbox_new: bfloat16 [4, 65536, 386], P('batch', 'node')
- mail_time_new: int32 [4, 65536], P('batch', 'node')
- update_time_new: int32 [4, 65536], P('batch', 'node')
- memory_grad: float32 [4, 65536, 100], P('batch', 'node')
Inputs may be any that keep to these rules, and one draw needn't show every extreme that they name: `req_rows`: within one batch group, the rows that all devices and slots request of one owner are all distinct. `req_count`: live requests of a device to each owner; a device's counts sum to 4096. `root_live`: the 1536 entries of one device are distinct live request indices.
All inputs are finite; a program needn't handle non-finite values.
Results may differ from a plain program's by a relative error of at most 0.012.
The roundings to bfloat16 on the way count: a program that leaves them out, or rounds other values in their place, can miss the bound.
Values may be sent and summed in bfloat16 or wider, within the bound.
No kernel may reach another device: no remote copies, remote signals or barrier semaphores. Data moves between devices by JAX's collectives and lax.ppermute only.
A program may use at most 256 MiB of HBM per device.

v0:
```python
import jax
import jax.numpy as jnp
from jax import lax
from jax.sharding import PartitionSpec as P

MEM = 100
TENC = 100
EDGE = 186
NFEAT = 413
HEADS = 2
NBR = 10
STEP = 5
EV = 512
LIVE = 4096
MAIL = 386
FLAT = 360448


clip_limit = 1.0
learn_rate = 0.02
beta_first = 0.5
beta_second = 0.6
adam_floor = 1e-08
decay_rate = 0.01


def pieces():
    return [
        ("w_ih", (2 * MEM + EDGE + TENC, 3 * MEM)),
        ("w_hh", (MEM, 3 * MEM)),
        ("w_nf", (NFEAT, MEM)),
        ("w_q", (MEM + TENC, MEM)),
        ("w_kv", (MEM + EDGE + TENC, 2 * MEM)),
        ("w_o", (2 * MEM, MEM)),
        ("w_src", (MEM, MEM)),
        ("w_dst", (MEM, MEM)),
        ("w_out", (MEM, 1)),
        ("b_ih", (3 * MEM,)),
        ("b_hh", (3 * MEM,)),
        ("b_o", (MEM,)),
        ("ln_gain", (MEM,)),
        ("ln_bias", (MEM,)),
        ("b_pred", (MEM,)),
        ("b_out", (1,)),
    ]


def unpack(flat):
    table = {}
    offset = 0
    for piece_name, shape_dims in pieces():
        amount = 1
        for extent in shape_dims:
            amount = amount * extent
        table[piece_name] = flat[offset : offset + amount].reshape(shape_dims)
        offset = offset + amount
    return table


def widen_cols(array):
    extra = -array.shape[-1] % 128
    return jnp.concatenate([array, jnp.zeros(array.shape[:-1] + (extra,), array.dtype)], -1)


def matmul(left, right):
    return jnp.dot(left, right, preferred_element_type=jnp.float32)


def outer_sum(left, grad_low):
    return lax.dot_general(
        left, grad_low, (((0,), (0,)), ((), ())), preferred_element_type=jnp.float32
    )


def through(grad_low, right):
    return lax.dot_general(
        grad_low, right, (((1,), (1,)), ((), ())), preferred_element_type=jnp.float32
    )


def encode(delta):
    freqs = 10.0 ** (-9.0 * jnp.arange(TENC, dtype=jnp.float32) / (TENC - 1))
    return jnp.cos(delta.astype(jnp.float32)[..., None] * freqs)


def gru_gates(gate_in, gate_hid, memory_rows):
    reset = jax.nn.sigmoid(gate_in[:, :MEM] + gate_hid[:, :MEM])
    update = jax.nn.sigmoid(gate_in[:, MEM : 2 * MEM] + gate_hid[:, MEM : 2 * MEM])
    candidate = jnp.tanh(gate_in[:, 2 * MEM :] + reset * gate_hid[:, 2 * MEM :])
    return (1.0 - update) * candidate + update * memory_rows


def gru_forward(x_rows, mem_rows, feat_rows, wts, bias):
    gate_in = matmul(x_rows, wts["w_ih"]) + bias["b_ih"]
    gate_hid = matmul(mem_rows, wts["w_hh"]) + bias["b_hh"]
    renewed, gate_back = jax.vjp(gru_gates, gate_in, gate_hid, mem_rows.astype(jnp.float32))
    hidden = (renewed + matmul(feat_rows, wts["w_nf"])).astype(jnp.bfloat16)
    return (renewed, hidden, gate_back)


def gru_backward(gate_back, d_hidden, x_rows, mem_rows, feat_rows, wts, grads):
    grads["w_nf"] = outer_sum(feat_rows, d_hidden.astype(jnp.bfloat16))
    d_gate_in, d_gate_hid, d_memory = gate_back(d_hidden)
    d_gin_low = d_gate_in.astype(jnp.bfloat16)
    d_ghid_low = d_gate_hid.astype(jnp.bfloat16)
    grads["w_ih"] = outer_sum(x_rows, d_gin_low)
    grads["w_hh"] = outer_sum(mem_rows, d_ghid_low)
    grads["b_ih"] = jnp.sum(d_gate_in, 0)
    grads["b_hh"] = jnp.sum(d_gate_hid, 0)
    return d_memory + through(d_ghid_low, wts["w_hh"])


def attend(query, keyval):
    rows = query.shape[0]
    width = MEM // HEADS
    keys = keyval[..., :MEM].reshape(rows, NBR, HEADS, width)
    values = keyval[..., MEM:].reshape(rows, NBR, HEADS, width)
    scores = jnp.einsum(
        "nhd,nkhd->nhk", query.reshape(rows, HEADS, width), keys, precision=lax.Precision.HIGHEST
    ) * width ** (-0.5)
    scores = scores - jnp.max(scores, -1, keepdims=True)
    weights = jnp.exp(scores)
    weights = weights / jnp.sum(weights, -1, keepdims=True)
    return jnp.einsum("nhk,nkhd->nhd", weights, values, precision=lax.Precision.HIGHEST).reshape(
        rows, MEM
    )


def norm_act(pre, gain, shift):
    active = jax.nn.gelu(pre)
    centre = active - jnp.mean(active, -1, keepdims=True)
    spread = jnp.mean(centre * centre, -1, keepdims=True)
    return centre * lax.rsqrt(spread + 1e-05) * gain + shift


def link_loss(pos_logit, neg_logit, weight):
    return jnp.sum(jax.nn.softplus(-pos_logit)) + jnp.sum(weight * jax.nn.softplus(neg_logit))


def locate(counts, slots):
    index = jnp.arange(LIVE, dtype=jnp.int32)
    upper = jnp.cumsum(counts)
    lower = upper - counts
    owner = jnp.sum((index[:, None] >= upper[None, :]).astype(jnp.int32), 1)
    match = owner[:, None] == jnp.arange(counts.shape[0], dtype=jnp.int32)[None, :]
    start = jnp.sum(jnp.where(match, lower[None, :], 0), 1)
    return owner * slots + index - start


def body(
    params,
    moment1,
    moment2,
    memory,
    mailbox,
    mail_time,
    update_time,
    node_feat,
    req_rows,
    req_count,
    root_live,
    nbr_live,
    nbr_dt,
    nbr_edge,
    ev_edge,
    ev_time,
    neg_count,
):
    single = jnp.float32
    halfw = jnp.bfloat16
    shards = lax.axis_size("node")
    slots = req_rows.shape[3]
    table_rows = memory.shape[1]
    wts = unpack(lax.all_gather(params.astype(halfw), ("batch", "node"), axis=0, tiled=True))
    bias = {
        name: wts[name].astype(single)
        for name in ["b_ih", "b_hh", "b_o", "ln_gain", "ln_bias", "b_pred", "b_out"]
    }
    got_rows, got_counts = (
        lax.all_to_all(req_rows[0], "node", split_axis=1, concat_axis=1, tiled=True),
        lax.all_to_all(req_count[0][..., None], "node", split_axis=1, concat_axis=1, tiled=True),
    )
    flat_rows = got_rows[0].reshape(-1)
    own_mem = memory[0][flat_rows].astype(halfw)
    own_in = jnp.concatenate(
        [
            mailbox[0][flat_rows],
            encode(mail_time[0][flat_rows] - update_time[0][flat_rows]).astype(halfw),
        ],
        -1,
    )
    own_feat = node_feat[flat_rows]
    live_slot = locate(req_count[0, 0], slots)
    packed = widen_cols(jnp.concatenate([own_mem, own_in, own_feat], -1))
    fetched = lax.all_to_all(
        packed.reshape(1, shards, slots, packed.shape[-1]),
        "node",
        split_axis=1,
        concat_axis=1,
        tiled=True,
    )
    live_rows = fetched.reshape(shards * slots, -1)[live_slot]
    mem_low = live_rows[:, :MEM]
    x_low = live_rows[:, MEM : 3 * MEM + EDGE + TENC]
    feat_low = live_rows[:, 3 * MEM + EDGE + TENC : 3 * MEM + EDGE + TENC + NFEAT]
    renewed, hid_low, gate_back = gru_forward(x_low, mem_low, feat_low, wts, bias)
    hid_wide = widen_cols(hid_low)
    roots = root_live[0, 0].reshape(-1)
    neighbors = nbr_live[0, 0]
    count_rows = roots.shape[0]
    root_low = hid_wide[roots][:, :MEM]
    neigh_low = hid_wide[neighbors][..., :MEM]
    key_in = jnp.concatenate([neigh_low, nbr_edge[0, 0], encode(nbr_dt[0, 0]).astype(halfw)], -1)
    key_flat = key_in.reshape(count_rows * NBR, -1)
    query_in = jnp.concatenate([root_low, jnp.ones((count_rows, TENC), halfw)], -1)
    query = matmul(query_in, wts["w_q"])

    def key_values():
        return matmul(key_flat, wts["w_kv"]).reshape(count_rows, NBR, 2 * MEM)

    attended = attend(query, key_values())
    out_in = jnp.concatenate([attended.astype(halfw), root_low], -1)
    out_pre = matmul(out_in, wts["w_o"]) + bias["b_o"]
    embed, norm_back = jax.vjp(norm_act, out_pre, bias["ln_gain"], bias["ln_bias"])
    emb_low = embed.astype(halfw)
    src_low = emb_low[:EV]
    dst_low = emb_low[EV : 2 * EV]
    negs_low = emb_low[2 * EV :]
    src_proj = matmul(src_low, wts["w_src"])
    pos_pre = src_proj + matmul(dst_low, wts["w_dst"]) + bias["b_pred"]
    neg_pre = src_proj + matmul(negs_low, wts["w_dst"]) + bias["b_pred"]
    pos_act, pos_back = jax.vjp(jax.nn.gelu, pos_pre)
    neg_act, neg_back = jax.vjp(jax.nn.gelu, neg_pre)
    pos_low = pos_act.astype(halfw)
    neg_low = neg_act.astype(halfw)
    pos_logit = matmul(pos_low, wts["w_out"])[:, 0] + bias["b_out"][0]
    neg_logit = matmul(neg_low, wts["w_out"])[:, 0] + bias["b_out"][0]
    weight = neg_count[0, 0].astype(single)
    loss_local, loss_back = jax.vjp(lambda a, b: link_loss(a, b, weight), pos_logit, neg_logit)
    local_weight = jnp.sum(1.0 + weight)
    loss_sum, loss_weight = lax.psum((loss_local, local_weight), ("batch", "node"))
    d_pos, d_neg = loss_back(jnp.ones((), single))
    d_pos_low = d_pos[:, None].astype(halfw)
    d_neg_low = d_neg[:, None].astype(halfw)
    grads = {}
    grads["w_out"] = outer_sum(pos_low, d_pos_low) + outer_sum(neg_low, d_neg_low)
    grads["b_out"] = (jnp.sum(d_pos) + jnp.sum(d_neg))[None]
    d_ppre = pos_back(through(d_pos_low, wts["w_out"]))[0]
    d_npre = neg_back(through(d_neg_low, wts["w_out"]))[0]
    grads["b_pred"] = jnp.sum(d_ppre + d_npre, 0)
    d_src_low = (d_ppre + d_npre).astype(halfw)
    d_dst_low = d_ppre.astype(halfw)
    d_negp_low = d_npre.astype(halfw)
    grads["w_src"] = outer_sum(src_low, d_src_low)
    grads["w_dst"] = outer_sum(dst_low, d_dst_low) + outer_sum(negs_low, d_negp_low)
    d_embed = jnp.concatenate(
        [
            through(d_src_low, wts["w_src"]),
            through(d_dst_low, wts["w_dst"]),
            through(d_negp_low, wts["w_dst"]),
        ],
        0,
    )
    d_out_pre, grads["ln_gain"], grads["ln_bias"] = norm_back(d_embed)
    grads["b_o"] = jnp.sum(d_out_pre, 0)
    d_out_low = d_out_pre.astype(halfw)
    grads["w_o"] = outer_sum(out_in, d_out_low)
    d_out_in = through(d_out_low, wts["w_o"])
    attended_again, attend_back = jax.vjp(attend, query, key_values())
    d_query, d_keyval = attend_back(d_out_in[:, :MEM])
    d_query_low = d_query.astype(halfw)
    grads["w_q"] = outer_sum(query_in, d_query_low)
    d_root = d_out_in[:, MEM:] + through(d_query_low, wts["w_q"])[:, :MEM]
    d_kv_low = d_keyval.reshape(count_rows * NBR, 2 * MEM).astype(halfw)
    grads["w_kv"] = outer_sum(key_flat, d_kv_low)
    d_neigh = through(d_kv_low, wts["w_kv"])[:, :MEM]
    d_hidden = (
        jnp.zeros((LIVE, MEM), single).at[roots].add(d_root).at[neighbors.reshape(-1)].add(d_neigh)
    )
    src_slot = root_live[0, 0, 0]
    dst_slot = root_live[0, 0, 1]
    edge_float = ev_edge[0, 0].astype(single)
    mail_src = jnp.concatenate([renewed[src_slot], renewed[dst_slot], edge_float], -1).astype(halfw)
    mail_dst = jnp.concatenate([renewed[dst_slot], renewed[src_slot], edge_float], -1).astype(halfw)
    mail_live = jnp.zeros((LIVE, MAIL), halfw).at[src_slot].set(mail_src).at[dst_slot].set(mail_dst)
    mail_back = (
        jnp.zeros((shards * slots, MAIL), halfw)
        .at[live_slot]
        .set(mail_live)
        .reshape(1, shards, slots, MAIL)
    )
    stamp_rows = jnp.stack([ev_time[0, 0].astype(single), jnp.ones((EV,), single)], -1)
    tag_live = (
        jnp.zeros((LIVE, 2), single).at[src_slot].set(stamp_rows).at[dst_slot].set(stamp_rows)
    )
    tags_back = (
        jnp.zeros((shards * slots, 2), single)
        .at[live_slot]
        .set(tag_live)
        .reshape(1, shards, slots, 2)
    )
    d_memory = gru_backward(gate_back, d_hidden, x_low, mem_low, feat_low, wts, grads)
    rows_live = widen_cols(jnp.concatenate([renewed, d_memory], -1))
    wide_back = rows_live.shape[-1]
    slots_back = jnp.zeros((shards * slots, wide_back), single).at[live_slot].set(rows_live)
    got_back, got_mail, got_tags = (
        lax.all_to_all(
            slots_back.reshape(1, shards, slots, wide_back),
            "node",
            split_axis=1,
            concat_axis=1,
            tiled=True,
        ),
        lax.all_to_all(
            mail_back.astype(jnp.float32), "node", split_axis=1, concat_axis=1, tiled=True
        ).astype(mail_back.dtype),
        lax.all_to_all(tags_back, "node", split_axis=1, concat_axis=1, tiled=True),
    )
    got_back = got_back.reshape(shards * slots, -1)
    new_rows = got_back[:, :MEM]
    grad_rows = got_back[:, MEM : 2 * MEM]
    ordered = [grads[piece_name].reshape(-1) for piece_name, shape_dims in pieces()]
    flat_grad = jnp.concatenate(ordered)
    flat_grad = jnp.concatenate([flat_grad, jnp.zeros((FLAT - flat_grad.shape[0],), single)])
    grad_shard = lax.psum_scatter(flat_grad, ("batch", "node"), scatter_dimension=0, tiled=True)
    squares = jnp.sum(grad_shard * grad_shard)
    norm_sq = lax.psum(squares, ("batch", "node"))
    grad_norm = jnp.sqrt(norm_sq)
    clipped = grad_shard * jnp.minimum(1.0, clip_limit / (grad_norm + 1e-06))
    moment1_new = beta_first * moment1 + (1.0 - beta_first) * clipped
    moment2_new = beta_second * moment2 + (1.0 - beta_second) * clipped * clipped
    ratio = (
        moment1_new
        / (1.0 - beta_first**STEP)
        / (jnp.sqrt(moment2_new / (1.0 - beta_second**STEP)) + adam_floor)
    )
    params_new = params - learn_rate * (ratio + decay_rate * params)
    mail_rows = got_mail.reshape(shards * slots, MAIL)
    got_tags = got_tags.reshape(shards * slots, 2)
    live_mask = (jnp.arange(slots, dtype=jnp.int32)[None, :] < got_counts[0]).reshape(-1)
    target = jnp.where(live_mask, flat_rows, table_rows)
    mail_target = jnp.where(live_mask & (got_tags[:, 1] > 0.5), flat_rows, table_rows)
    memory_new = memory[0].at[target].set(new_rows, mode="drop")[None]
    memory_grad = jnp.zeros_like(memory[0]).at[target].add(grad_rows, mode="drop")[None]
    mailbox_new = mailbox[0].at[mail_target].set(mail_rows, mode="drop")[None]
    mail_time_new = (
        mail_time[0].at[mail_target].set(got_tags[:, 0].astype(jnp.int32), mode="drop")[None]
    )
    update_time_new = update_time[0].at[target].set(mail_time[0][flat_rows], mode="drop")[None]
    return (
        loss_sum,
        loss_weight,
        grad_norm,
        params_new,
        moment1_new,
        moment2_new,
        params_new.astype(halfw),
        memory_new,
        mailbox_new,
        mail_time_new,
        update_time_new,
        memory_grad,
    )


def solution(mesh):
    in_specs = (
        P(("batch", "node")),
        P(("batch", "node")),
        P(("batch", "node")),
        P("batch", "node", None),
        P("batch", "node", None),
        P("batch", "node"),
        P("batch", "node"),
        P("node", None),
        P("batch", "node", None, None),
        P("batch", "node", None),
        P("batch", "node", None, None),
        P("batch", "node", None, None),
        P("batch", "node", None, None),
        P("batch", "node", None, None, None),
        P("batch", "node", None, None),
        P("batch", "node", None),
        P("batch", "node", None),
    )
    out_specs = (
        P(),
        P(),
        P(),
        P(("batch", "node")),
        P(("batch", "node")),
        P(("batch", "node")),
        P(("batch", "node")),
        P("batch", "node", None),
        P("batch", "node", None),
        P("batch", "node"),
        P("batch", "node"),
        P("batch", "node", None),
    )
    return jax.shard_map(body, mesh=mesh, in_specs=in_specs, out_specs=out_specs, check_vma=False)
```

profile of v0, /device:TPU:0, one launch (start us, length us, event | category | flops | bytes accessed | tf_op | source)
XLA Modules:
  0.0 1959.4 jit_solution(3285260228358963641)
XLA Ops:
  10.0 6.3 all-to-all-start.2
  24.5 12.8 scatter_custom_fusion.6
  41.4 10.8 copy.302
  52.2 5.9 copy.301
  58.0 10.7 copy.303
  74.1 5.5 all-to-all-done
  83.6 5.7 all-to-all-done.4
  90.1 45.5 %gather_fusion.2 = s32[8192]{0:T(1024)S(1)} fusion(s32[8192]{0:T(1024)S(1)} %bitcast.157, s32[8192]{0:T(1024)S(1)} %broadcast_clamp_fusion.1), kind=kCustom, calls=%fused_computation.2 | custom fusion | bytes 98304 | tf_op jit(solution)/shard_map/gather | solution.py:188
  135.7 45.5 %gather_fusion.3 = s32[8192]{0:T(1024)S(1)} fusion(s32[8192]{0:T(1024)S(1)} %bitcast.160, s32[8192]{0:T(1024)S(1)} %broadcast_clamp_fusion.1), kind=kCustom, calls=%fused_computation.3 | custom fusion | bytes 98304 | tf_op jit(solution)/shard_map/gather | solution.py:188
  181.3 38.2 %gather_fusion.1 = bf16[8192,386]{1,0:T(8,128)(2,1)} fusion(bf16[8192,386]{1,0:T(8,128)(2,1)} %bitcast.163, s32[8192]{0:T(1024)S(1)} %broadcast_clamp_fusion.1), kind=kCustom, calls=%fused_computation.1 | custom fusion | bytes 12681216 | tf_op jit(solution)/shard_map/gather | solution.py:187
  219.5 24.1 %gather_fusion = bf16[8192,100]{1,0:T(8,128)(2,1)S(1)} fusion(f32[8192,100]{1,0:T(8,128)} %bitcast.166, s32[8192]{0:T(1024)S(1)} %broadcast_clamp_fusion.1), kind=kCustom, calls=%fused_computation | custom fusion | bytes 3309568 | tf_op jit(solution)/shard_map/gather | solution.py:184
  243.6 38.3 %gather_fusion.4 = bf16[8192,413]{1,0:T(8,128)(2,1)} fusion(bf16[8192,413]{1,0:T(8,128)(2,1)} %copy.303, s32[8192]{0:T(1024)S(1)} %broadcast_clamp_fusion.1), kind=kCustom, calls=%fused_computation.4 | custom fusion | bytes 13565952 | tf_op jit(solution)/shard_map/gather | solution.py:192
  281.9 15.7 cosine_convert_fusion.2
  299.1 32.1 %concatenate.47 = bf16[1,8,1024,1024]{3,2,0,1:T(8,128)(2,1)} concatenate(bf16[1,8,1024,100]{3,2,0,1:T(8,128)(2,1)S(1)} %bitcast.181, bf16[1,8,1024,386]{3,2,0,1:T(8,128)(2,1)} %bitcast.173, bf16[1,8,1024,100]{3,2,0,1:T(8,128)(2,1)} %cosine_convert_fusion.2, bf16[1,8,1024,413]{3,2,0,1:T(8,128)(2,1)} %bitcast.174, bf16[1,8,1024,25]{3,2,0,1:T(8,128)(2,1)} %broadcast_in_dim.56), dimensions={3} | concatenate | bytes 33554432 | tf_op jit(solution)/shard_map/concatenate | solution.py:62
  331.3 5.9 all-to-all-start.1
  337.2 396.5 %all_gather.3 = bf16[360448]{0:T(1024)(128)(2,1)S(1)} all-gather(bf16[11264]{0:T(1024)(128)(2,1)S(1)} %convert_element_type.203), channel_id=1, replica_groups=mesh['batch'=4,'node'=8] {'batch','node'}, dimensions={0}, use_global_device_ids=true | all-gather | bytes 743424 | tf_op jit(solution)/shard_map/all_gather | solution.py:174
  750.0 22.0 %cosine_convert_fusion.1 = bf16[1536,10,100]{0,2,1:T(8,128)(2,1)} fusion(f32[100]{0:T(128)S(1)} %multiply_power_fusion, f32[1536,10]{0,1:T(8,128)S(1)} %bitcast.183), kind=kLoop, calls=%fused_computation.45 | loop fusion | flops 3072000 | bytes 3133840 | tf_op jit(solution)/shard_map/convert_element_type | solution.py:213
  772.7 28.8 %gather_fusion.5 = bf16[4096,1024]{1,0:T(8,128)(2,1)} fusion(bf16[8192,1024]{1,0:T(8,128)(2,1)} %bitcast.16, s32[4096]{0:T(1024)S(1)} %broadcast_clamp_fusion.2), kind=kCustom, calls=%fused_computation.5 | custom fusion | bytes 16793600 | tf_op jit(solution)/shard_map/gather | solution.py:202
  805.9 6.4 convolution_add_fusion.1
  823.0 54.0 %gather_fusion.7 = bf16[15360,100]{1,0:T(8,128)(2,1)} fusion(bf16[4096,100]{1,0:T(8,128)(2,1)S(1)} %copy.308, s32[15360]{0:T(1024)S(1)} %broadcast_clamp_fusion), kind=kCustom, calls=%fused_computation.7 | custom fusion | bytes 6205440 | tf_op jit(solution)/shard_map/gather | solution.py:212
  876.9 8.4 reshape.688
  885.4 9.0 copy.313
  894.4 10.3 fusion.6
  904.7 11.6 fusion.159
  916.2 7.4 reshape.608
  934.0 7.9 reshape.609
  958.0 5.3 scatter_custom_fusion.7
  963.5 7.6 scatter_fusion.1
  971.1 23.6 %scatter_custom_fusion.9 = bf16[8192,386]{1,0:T(8,128)(2,1)} fusion(s32[4096]{0:T(1024)} %bitcast.200, bf16[4096,386]{1,0:T(8,128)(2,1)} %scatter_fusion.1, bf16[]{:T(256)} %constant.36.clone.1), kind=kCustom, calls=%fused_computation.60 | custom fusion | bytes 6324736 | tf_op jit(solution)/shard_map/scatter | solution.py:289
  994.7 10.6 copy.339
  1005.3 10.2 copy.377
  1016.2 32.8 %copy.381 = bf16[1,8,1024,386]{2,0,3,1:T(2,128)(2,1)} copy(bf16[1,8,1024,386]{2,1,3,0:T(8,128)(2,1)S(1)} %slice_bitcast_fusion) | data formatting | bytes 12648448 | tf_op jit(solution)/shard_map/convert_element_type | solution.py:315
  1049.5 136.6 %reduce.14 = bf16[8,386,1024]{2,1,0:T(8,128)(2,1)} reduce(bf16[8,386,1,1024]{3,2,1,0:T(2,128)(2,1)} %bitcast.172, bf16[]{:T(256)} %broadcast.579), dimensions={2}, to_apply=%bitcast.156.reduce_sub_computation | reduce | bytes 12648450
  1186.2 9.6 reshape.864
  1209.9 7.8 multiply_bitcast_fusion.1
  1222.4 7.4 reshape.615
  1229.9 7.4 reshape.614
  1237.3 8.5 add_convert_fusion
  1245.9 18.7 copy.317
  1264.6 16.4 convert_element_type.232
  1282.1 9.5 scatter_custom_fusion
  1291.7 8.7 fusion.102
  1300.4 83.0 %scatter_fusion = f32[4096,100]{1,0:T(8,128)S(1)} fusion(f32[4096,100]{1,0:T(8,128)S(1)} %scatter_custom_fusion, s32[15360]{0:T(1024)S(1)} %bitcast.189, f32[15360,100]{1,0:T(8,128)} %fusion.102), kind=kCustom, calls=%fused_computation.11 | custom fusion | flops 1536000 | bytes 18493440 | tf_op jit(solution)/shard_map/scatter-add | solution.py:278
  1399.5 5.6 copy.328
  1405.1 21.6 %scatter_custom_fusion.2 = f32[8192,256]{1,0:T(8,128)} fusion(s32[4096]{0:T(1024)} %bitcast.201, f32[4096,256]{1,0:T(8,128)} %copy.328, f32[]{:T(128)} %constant.42.clone.1), kind=kCustom, calls=%fused_computation.62 | custom fusion | bytes 8389120 | tf_op jit(solution)/shard_map/scatter | solution.py:305
  1426.6 5.1 all-to-all-start.3
  1432.3 18.5 copy.324
  1451.4 16.4 concatenate.54
  1467.8 29.1 %cosine_convert_fusion = bf16[15360,100]{1,0:T(8,128)(2,1)} fusion(f32[100]{0:T(128)S(1)} %copy-done.86, f32[15360]{0:T(1024)S(1)} %convert_element_type.236), kind=kLoop, calls=%fused_computation.38 | loop fusion | flops 3072000 | bytes 3133840 | tf_op jit(solution)/shard_map/convert_element_type | solution.py:213
  1502.1 16.5 fusion
  1531.1 8.0 fusion.24
  1547.5 29.3 %concatenate.56 = f32[360448]{0:T(1024)} concatenate(f32[145800]{0:T(1024)} %reshape.616, f32[30000]{0:T(1024)} %reshape.617, f32[41300]{0:T(1024)} %reshape.618, f32[20000]{0:T(1024)} %reshape.619, f32[77200]{0:T(1024)} %reshape.620, f32[20000]{0:T(1024)S(1)} %copy-done.39, f32[10000]{0:T(1024)} %reshape.622, f32[10000]{0:T(1024)} %reshape.623, f32[100]{0:T(128)} %fusion.53, ...), dimensions={0} | concatenate | bytes 2883584 | tf_op jit(solution)/shard_map/concatenate | solution.py:324
  1576.9 30.5 %scatter_fusion.4 = s32[8192]{0:T(1024)S(1)} fusion(s32[8192]{0:T(1024)S(1)} %bitcast.161, s32[8192]{0:T(1024)S(1)} %bitcast.192, s32[8192]{0:T(1024)S(1)} %copy-done.44), kind=kCustom, calls=%fused_computation.22 | custom fusion | bytes 131072 | tf_op jit(solution)/shard_map/scatter | solution.py:349
  1607.5 30.7 %scatter_fusion.3 = s32[8192]{0:T(1024)S(1)} fusion(s32[8192]{0:T(1024)S(1)} %bitcast.158, s32[8192]{0:T(1024)S(1)} %bitcast.185, s32[8192]{0:T(1024)S(1)} %bitcast.191), kind=kCustom, calls=%fused_computation.21 | custom fusion | bytes 131072 | tf_op jit(solution)/shard_map/scatter | solution.py:347
  1639.5 74.6 %all-reduce.12.cloned.1.call-done = f32[360448]{0:T(1024)} async-done(((f32[360448]{0:T(1024)}), f32[360448]{0:T(1024)}) %all-reduce.12.cloned.1.call-update) | async-done | bytes 1441808
  1715.5 39.4 %all-reduce.9 = (f32[]{:T(128)}, f32[]{:T(128)}, f32[]{:T(128)}) all-reduce(f32[]{:T(128)S(6)} %add.353, f32[]{:T(128)} %get-tuple-element.177, f32[]{:T(128)} %multiply_reduce_fusion.9), channel_id=1, replica_groups=mesh['batch'=4,'node'=8] {'batch','node'}, use_global_device_ids=true, to_apply=%region_9.11 | all-reduce | flops 3 | bytes 24 | tf_op jit(solution)/shard_map/psum | solution.py:241
  1757.1 10.7 reshape.865
  1767.8 38.0 %copy.341 = bf16[1,8,1024,386]{3,2,1,0:T(8,128)(2,1)} copy(bf16[1,8,1024,386]{2,0,3,1:T(2,128)(2,1)} %bitcast.171) | data formatting | bytes 12648448 | tf_op jit(solution)/shard_map/convert_element_type | solution.py:316
  1805.8 44.2 %scatter_fusion.2 = bf16[8192,386]{1,0:T(8,128)(2,1)} fusion(bf16[8192,386]{1,0:T(8,128)(2,1)} %bitcast.164, s32[8192]{0:T(1024)S(1)} %bitcast.186, bf16[8192,386]{1,0:T(8,128)(2,1)} %bitcast.175), kind=kCustom, calls=%fused_computation.20 | custom fusion | bytes 19005440 | tf_op jit(solution)/shard_map/scatter | solution.py:345
  1850.0 10.5 copy.343
  1860.5 48.7 %scatter_custom_fusion.13 = f32[8192,100]{1,0:T(8,128)} fusion(s32[8192]{0:T(1024)S(1)} %bitcast.193, f32[8192,256]{1,0:T(8,128)} %bitcast.44, f32[]{:T(128)} %constant.42.clone.1), kind=kCustom, calls=%fused_computation.55 | custom fusion | flops 819200 | bytes 7471616 | tf_op jit(solution)/shard_map/scatter-add | solution.py:344
  1909.2 25.2 %scatter_custom_fusion.3 = f32[8192,100]{1,0:T(8,128)} fusion(f32[8192,100]{1,0:T(8,128)} %bitcast.167, s32[8192]{0:T(1024)S(1)} %bitcast.194, f32[8192,256]{1,0:T(8,128)} %bitcast.44), kind=kCustom, calls=%fused_computation.57 | custom fusion | bytes 7471104 | tf_op jit(solution)/shard_map/scatter | solution.py:343
  1934.4 8.4 copy.344
  1942.8 8.4 copy.342
  (361 shorter events, 150.0 us)
Async XLA Ops:
  7.9 82.2 %copy-start = (s32[1,8192]{1,0:T(1,128)}, s32[1,8192]{1,0:T(1,128)S(1)}, u32[]{:S(2)}) copy-start(s32[1,8192]{1,0:T(1,128)S(1)} %copy.392) | copy-start | bytes 98308
  8.7 127.0 %copy-start.3 = (s32[1,8192]{1,0:T(1,128)}, s32[1,8192]{1,0:T(1,128)S(1)}, u32[]{:S(2)}) copy-start(s32[1,8192]{1,0:T(1,128)S(1)} %copy.393) | copy-start | bytes 98308
  10.0 58.7 %all-to-all-start.2 = ((s32[1,8,1]{2,0,1:T(1,128)}), s32[1,8,1]{2,0,1:T(1,128)S(1)}, u32[]{:S(2)}, u32[]{:S(2)}) async-start(s32[1,8,1]{2,0,1:T(1,128)} %copy.326), calls=%async_computation.2 | async-start | bytes 8192 | tf_op jit(solution)/shard_map/all_to_all | solution.py:181
  17.1 20.2 %copy-start.82 = (s32[512,1]{0,1:T(1,128)}, s32[512,1]{0,1:T(1,128)S(1)}, u32[]{:S(2)}) copy-start(s32[512,1]{0,1:T(1,128)S(1)} %get-tuple-element.175) | copy-start | bytes 6148
  17.1 731.0 %copy-start.75 = (s32[512,1]{0,1:T(1,128)}, s32[512,1]{0,1:T(1,128)S(1)}, u32[]{:S(2)}) copy-start(s32[512,1]{0,1:T(1,128)S(1)} %get-tuple-element.174) | copy-start | bytes 6148
  24.5 725.6 %copy-start.68 = (s32[4096,1]{0,1:T(1,128)}, s32[4096,1]{0,1:T(1,128)S(1)}, u32[]{:S(2)}) copy-start(s32[4096,1]{0,1:T(1,128)S(1)} %compare_select_fusion.5) | copy-start | bytes 49156
  24.5 16.3 copy-start.74
  41.4 10.8 copy-start.20
  68.8 10.8 all-to-all-start
  73.9 676.1 %copy-start.85 = (f32[100]{0:T(128)}, f32[100]{0:T(128)S(1)}, u32[]{:S(2)}) copy-start(f32[100]{0:T(128)S(1)} %multiply_power_fusion) | copy-start | bytes 1204
  79.6 9.7 all-to-all-start.4
  135.7 45.6 %copy-start.43 = (s32[8192]{0:T(1024)}, s32[8192]{0:T(1024)S(1)}, u32[]{:S(2)}) copy-start(s32[8192]{0:T(1024)S(1)} %gather_fusion.2) | copy-start | bytes 98308
  331.3 408.9 %copy-start.48 = (s32[1,1,1536,10]{2,1,3,0:T(1,128)S(1)}, s32[1,1,1536,10]{2,1,3,0:T(1,128)}, u32[]{:S(2)}) copy-start(s32[1,1,1536,10]{2,1,3,0:T(1,128)} %param.29) | copy-start | bytes 184324
  331.3 441.4 %all-to-all-start.1 = ((bf16[1,8,1024,1024]{3,2,0,1:T(8,128)(2,1)}), bf16[1,8,1024,1024]{3,2,0,1:T(8,128)(2,1)}, u32[]{:S(2)}, u32[]{:S(2)}) async-start(bf16[1,8,1024,1024]{3,2,0,1:T(8,128)(2,1)} %concatenate.47), calls=%async_computation.1 | async-start | bytes 33554432 | tf_op jit(solution)/shard_map/all_to_all | solution.py:195
  337.2 404.2 %copy-start.69 = (s32[1,1,1536,10]{2,1,3,0:T(1,128)S(1)}, s32[1,1,1536,10]{2,1,3,0:T(1,128)}, u32[]{:S(2)}) copy-start(s32[1,1,1536,10]{2,1,3,0:T(1,128)} %param.30) | copy-start | bytes 184324
  337.2 408.5 %copy-start.90 = (s32[1,1,512]{2,1,0:T(1,128)S(1)}, s32[1,1,512]{2,1,0:T(1,128)}, u32[]{:S(2)}) copy-start(s32[1,1,512]{2,1,0:T(1,128)} %param.34) | copy-start | bytes 6148
  337.2 410.3 %copy-start.83 = (s32[512,1]{0,1:T(1,128)S(1)}, s32[512,1]{0,1:T(1,128)}, u32[]{:S(2)}) copy-start(s32[512,1]{0,1:T(1,128)} %copy-done.82) | copy-start | bytes 6148
  337.2 411.5 %copy-start.77 = (s32[1,1,3,512]{3,1,2,0:T(1,128)S(1)}, s32[1,1,3,512]{3,1,2,0:T(1,128)}, u32[]{:S(2)}) copy-start(s32[1,1,3,512]{3,1,2,0:T(1,128)} %param.28) | copy-start | bytes 18436
  737.4 66.0 %copy-start.32 = (bf16[100,300]{1,0:T(8,128)(2,1)}, bf16[100,300]{1,0:T(8,128)(2,1)S(1)}, u32[]{:S(2)}) copy-start(bf16[100,300]{1,0:T(8,128)(2,1)S(1)} %reshape.604) | copy-start | bytes 180004
  741.4 31.3 %copy-start.34 = (f32[1,1,1536,10]{2,1,3,0:T(1,128)}, f32[1,1,1536,10]{2,1,3,0:T(1,128)S(1)}, u32[]{:S(2)}) copy-start(f32[1,1,1536,10]{2,1,3,0:T(1,128)S(1)} %convert_element_type.208) | copy-start | bytes 184324
  741.8 30.9 %copy-start.40 = (bf16[200,100]{1,0:T(8,128)(2,1)}, bf16[200,100]{1,0:T(8,128)(2,1)S(1)}, u32[]{:S(2)}) copy-start(bf16[200,100]{1,0:T(8,128)(2,1)S(1)} %reshape.606) | copy-start | bytes 120004
  803.5 8.8 copy-start.18
  805.9 6.4 copy-start.6
  885.4 9.0 copy-start.57
  916.2 7.4 copy-start.72
  933.9 8.0 copy-start.58
  934.0 7.9 copy-start.30
  942.0 6.6 copy-start.55
  945.9 7.9 copy-start.81
  946.6 8.6 copy-start.80
  956.6 6.9 copy-start.76
  1195.7 6.1 copy-start.53
  1195.8 7.0 copy-start.52
  1195.8 7.8 copy-start.50
  1195.8 9.4 copy-start.79
  1195.8 230.8 %all-to-all-start.5 = ((bf16[8,2,197632]{2,1,0:T(2,128)(2,1)}), bf16[8,2,197632]{2,1,0:T(2,128)(2,1)}, u32[]{:S(2)}, u32[]{:S(2)}) async-start(bf16[8,2,197632]{2,1,0:T(2,128)(2,1)} %reshape.864), calls=%async_computation.5 | async-start | bytes 12648448 | tf_op jit(solution)/shard_map/all_to_all | solution.py:314
  1200.7 7.9 copy-start.56
  1209.9 8.4 slice-start
  1209.9 8.3 slice-start.1
  1264.6 16.5 copy-start.41
  1291.6 8.7 copy-start.47
  1426.6 433.9 %all-to-all-start.3 = ((f32[1,8,1024,256]{3,2,0,1:T(8,128)}), f32[1,8,1024,256]{3,2,0,1:T(8,128)}, u32[]{:S(2)}, u32[]{:S(2)}) async-start(f32[1,8,1024,256]{3,2,0,1:T(8,128)} %bitcast.176), calls=%async_computation.3 | async-start | bytes 16777216 | tf_op jit(solution)/shard_map/all_to_all | solution.py:307
  1431.8 282.3 %all-reduce.12.cloned.1.call-start = ((), (), s32[]{:S(2)}) async-start(), calls=%async_computation.6 | async-start | bytes 2883584
  1451.4 16.5 copy-start.86
  1451.4 46.2 %copy-start.22 = (bf16[1536,100]{0,1:T(8,128)(2,1)S(1)}, bf16[1536,100]{0,1:T(8,128)(2,1)}, u32[]{:S(2)}) copy-start(bf16[1536,100]{0,1:T(8,128)(2,1)} %copy-done.21) | copy-start | bytes 921604
  1467.8 31.7 %copy-start.24 = (bf16[1536,100]{1,0:T(8,128)(2,1)S(1)}, bf16[1536,100]{1,0:T(8,128)(2,1)}, u32[]{:S(2)}) copy-start(bf16[1536,100]{1,0:T(8,128)(2,1)} %copy-done.23) | copy-start | bytes 921604
  1502.1 17.7 copy-start.26
  1502.1 17.7 copy-start.29
  1531.1 11.3 copy-start.37
  1531.1 11.4 copy-start.89
  1531.1 11.4 copy-start.92
  1531.1 11.4 copy-start.93
  1531.1 13.5 copy-start.10
  1544.6 32.2 %copy-start.4 = (s32[1,8192]{1,0:T(1,128)S(1)}, s32[1,8192]{1,0:T(1,128)}, u32[]{:S(2)}) copy-start(s32[1,8192]{1,0:T(1,128)} %copy-done.3) | copy-start | bytes 98308
  1544.6 32.2 %copy-start.44 = (s32[8192]{0:T(1024)S(1)}, s32[8192]{0:T(1024)}, u32[]{:S(2)}) copy-start(s32[8192]{0:T(1024)} %copy-done.43) | copy-start | bytes 98308
  1547.5 29.4 %copy-start.46 = (f32[1,8,1024,2]{2,3,0,1:T(2,128)S(1)}, f32[1,8,1024,2]{2,3,0,1:T(2,128)}, u32[]{:S(2)}) copy-start(f32[1,8,1024,2]{2,3,0,1:T(2,128)} %copy-done.45) | copy-start | bytes 196612
  1547.5 29.4 %copy-start.62 = (s32[8192,1]{0,1:T(1,128)S(1)}, s32[8192,1]{0,1:T(1,128)}, u32[]{:S(2)}) copy-start(s32[8192,1]{0,1:T(1,128)} %get-tuple-element.172) | copy-start | bytes 98308
  1576.9 30.6 %copy-start.1 = (s32[1,8192]{1,0:T(1,128)S(1)}, s32[1,8192]{1,0:T(1,128)}, u32[]{:S(2)}) copy-start(s32[1,8192]{1,0:T(1,128)} %copy-done) | copy-start | bytes 98308
  1576.9 30.6 %copy-start.42 = (s32[8192,1]{0,1:T(1,128)S(1)}, s32[8192,1]{0,1:T(1,128)}, u32[]{:S(2)}) copy-start(s32[8192,1]{0,1:T(1,128)} %get-tuple-element.171) | copy-start | bytes 98308
  1607.4 30.8 %copy-start.5 = (s32[8192]{0:T(1024)}, s32[8192]{0:T(1024)S(1)}, u32[]{:S(2)}) copy-start(s32[8192]{0:T(1024)S(1)} %scatter_fusion.4) | copy-start | bytes 98308
  1607.5 148.1 %copy-start.61 = (f32[11264]{0:T(1024)S(1)}, f32[11264]{0:T(1024)}, u32[]{:S(2)}) copy-start(f32[11264]{0:T(1024)} %param.18) | copy-start | bytes 135172
  1607.5 148.1 %copy-start.70 = (f32[11264]{0:T(1024)S(1)}, f32[11264]{0:T(1024)}, u32[]{:S(2)}) copy-start(f32[11264]{0:T(1024)} %param.19) | copy-start | bytes 135172
  1607.5 148.1 %copy-start.71 = (f32[11264]{0:T(1024)S(1)}, f32[11264]{0:T(1024)}, u32[]{:S(2)}) copy-start(f32[11264]{0:T(1024)} %param.20) | copy-start | bytes 135172
  1638.2 129.6 %copy-start.2 = (s32[8192]{0:T(1024)}, s32[8192]{0:T(1024)S(1)}, u32[]{:S(2)}) copy-start(s32[8192]{0:T(1024)S(1)} %scatter_fusion.3) | copy-start | bytes 98308
  (40 other events, 147.6 us)
Sparse Core Ops, SparseCore 0:
  1576.9 137.0 all-reduce.11
where the time goes:
time: 1980 us; the launch traced here: 1960 us
  local copies, waits for them, and re-layouts  897 us (45%)
  blocking collectives  436 us (22%)
  other arithmetic  409 us (21%)
  waiting for transfers between devices  85.8 us (4%)
  matrix products  78.9 us (4%)
  starting transfers between devices  31.4 us (2%)
  between operations  20.8 us (1%)
    all_gather x1, blocking collectives, body(): lax.all_gather(params.astype(halfw), ('batch', 'node'), axis=0, tiled=True)  397 us
    unnamed x3, other arithmetic  137 us
    unnamed x213, local copies, waits for them, and re-layouts  113 us
    scatter-add x2, other arithmetic, body(): jnp.zeros((LIVE, MEM), single).at[roots].add(d_root)  92.5 us
    unnamed x2, waiting for transfers between devices  74.6 us
    gather x3, local copies, waits for them, and re-layouts, body(): neigh_low = hid_wide[neighbors][..., :MEM]  71.4 us
    convert_element_type x2, other arithmetic, body(): encode(nbr_dt[0, 0]).astype(halfw)  51.1 us
    scatter-add x1, other arithmetic, body(): jnp.zeros_like(memory[0]).at[target].add(grad_rows, mode='drop')[None]  48.7 us
  transfers between devices with their start and end apart: 7, of which 3 were waited for; matrix products, arithmetic and copies ran while one was open for 32% of the time, Pallas kernels for 0%

commit v1 on v0

v1 whole, which is shorter than its diff:
```python
import functools
import math

import jax
import jax.numpy as jnp
import numpy as np
from jax import lax
from jax.experimental import pallas as pl
from jax.experimental.pallas import tpu as pltpu
from jax.sharding import PartitionSpec as P

MEM = 100
TENC = 100
EDGE = 186
NFEAT = 413
NBR = 10
STEP = 5
EV = 512
MAIL = 386
FLAT = 360448

clip_limit = 1.0
learn_rate = 0.02
beta_first = 0.5
beta_second = 0.6
adam_floor = 1e-08
decay_rate = 0.01

F32 = jnp.float32
BF16 = jnp.bfloat16
LANES = 128
PAD = 112
HALF = 56
GATES = 3 * PAD
KV = 4 * HALF
EB = 128
SECT = 3 * EB
STREAMS = 8
VMEM_LIMIT = 60 * 2**20

ROW_HH = 1458
ROW_NF = 1758
ROW_Q = 2171
ROW_KV = 2371
ROW_O = 3143
ROW_SRC = 3343
ROW_DST = 3443
ROW_OUT = 3543
ROW_BIH = 3544
ROW_BHH = 3547
ROW_BO = 3550
ROW_GAIN = 3551
ROW_SHIFT = 3552
ROW_BPRED = 3553
ROW_BOUT = 3554
USED = 355401
FLAT_ROWS = FLAT // LANES
PERIODS = 113
WROWS = 32 * PERIODS
GRU_ROWS = 2176
ATT_BASE = 2168
ATT_ROWS = 1448

FREQS = np.float32(10.0 ** (-9.0 * np.arange(TENC) / (TENC - 1)))

VMEM = pl.BlockSpec(memory_space=pltpu.VMEM)
SMEM = pl.BlockSpec(memory_space=pltpu.SMEM)


def params_of(limit=VMEM_LIMIT):
    return pltpu.CompilerParams(vmem_limit_bytes=limit)


def dot(left, right, left_dim=1, right_dim=0):
    return lax.dot_general(
        left, right, (((left_dim,), (right_dim,)), ((), ())), preferred_element_type=F32
    )


def fit_cosine():
    u = np.cos(np.pi * (np.arange(4000) + 0.5) / 4000) * 0.5 + 0.5
    u = u * (np.pi**2 * 1.002)
    fit = np.polynomial.chebyshev.Chebyshev.fit(u, np.cos(np.sqrt(u)), 7, domain=[0, np.pi**2 * 1.002])
    return [float(np.float32(c)) for c in fit.convert(kind=np.polynomial.Polynomial).coef]


COSINE = fit_cosine()


def cosine(x):
    turns = jnp.floor(x * np.float32(0.5 / np.pi) + 0.5)
    x = x - turns * np.float32(6.28125)
    x = x - turns * np.float32(2 * np.pi - 6.28125)
    u = x * x
    total = jnp.full_like(u, COSINE[-1])
    for c in COSINE[-2::-1]:
        total = total * u + np.float32(c)
    return total


def sigmoid(x):
    return 0.5 * jnp.tanh(0.5 * x) + 0.5


GELU_C = math.sqrt(2.0 / math.pi)


def gelu(x):
    t = jnp.tanh(GELU_C * (x + 0.044715 * (x * x * x)))
    return 0.5 * x * (1.0 + t)


def gelu_slope(x):
    x2 = x * x
    t = jnp.tanh(GELU_C * (x + 0.044715 * (x2 * x)))
    return 0.5 * (1.0 + t) + 0.5 * x * (1.0 - t * t) * (GELU_C * (1.0 + 3 * 0.044715 * x2))


def lane_of(shape):
    return lax.broadcasted_iota(jnp.int32, shape, len(shape) - 1)


def row_of(shape):
    return lax.broadcasted_iota(jnp.int32, shape, len(shape) - 2)


def roll_left(x, amount):
    amount = amount % LANES
    return x if amount == 0 else pltpu.roll(x, LANES - amount, 1)


def spread_heads(x):
    lane = lane_of(x.shape)
    moved = roll_left(x, -6)
    return jnp.where(lane < 50, x, jnp.where((lane >= 56) & (lane < 106), moved, 0.0))


def join_heads(x):
    lane = lane_of(x.shape)
    return jnp.where(lane < 50, x, jnp.where(lane < 100, roll_left(x, 6), 0.0))


def codes_kernel(dt, delta, freq, phi_n, phi_m):
    freqs = freq[...]
    for k in range(NBR):

        def one(i, carry, k=k):
            at = pl.ds(pl.multiple_of(i * LANES, LANES), LANES)
            phi_n[k, :, at] = cosine(dt[k : k + 1, at].astype(F32) * freqs).astype(BF16)
            return carry

        lax.fori_loop(0, dt.shape[1] // LANES, one, 0)

    def other(i, carry):
        at = pl.ds(pl.multiple_of(i * LANES, LANES), LANES)
        phi_m[:, at] = cosine(delta[:, at].astype(F32) * freqs).astype(BF16)
        return carry

    lax.fori_loop(0, delta.shape[1] // LANES, other, 0)


def time_codes(dt, delta):
    freq = jnp.asarray(np.tile(FREQS[:, None], (1, LANES)))
    return pl.pallas_call(
        codes_kernel,
        out_shape=(
            jax.ShapeDtypeStruct((NBR, TENC, dt.shape[1]), BF16),
            jax.ShapeDtypeStruct((TENC, delta.shape[1]), BF16),
        ),
        in_specs=[VMEM] * 3,
        out_specs=(VMEM, VMEM),
        compiler_params=params_of(24 * 2**20),
        cost_estimate=pl.CostEstimate(flops=60_000_000, bytes_accessed=5_000_000, transcendentals=0),
    )(dt, delta, freq)


def weights_kernel(
    flat,
    w_mail,
    w_time,
    w_hid,
    w_feat,
    gate_bias,
    kv_h,
    kv_e,
    kv_t,
    q_h,
    q_one,
    o_att,
    o_att_n,
    o_h,
    src_t,
    src_n,
    dst_t,
    dst_n,
    cols,
    wide,
    rows,
):
    wide[0:FLAT_ROWS, :] = flat[...].astype(F32)
    wide[FLAT_ROWS:, :] = jnp.zeros((wide.shape[0] - FLAT_ROWS, LANES), F32)
    lane = lane_of((PERIODS, LANES))
    for j in range(32):
        first, shift = divmod(100 * j, LANES)
        out = roll_left(wide[pl.ds(first, PERIODS, stride=25), :], shift)
        if shift + 100 > LANES:
            after = roll_left(wide[pl.ds(first + 1, PERIODS, stride=25), :], shift)
            out = jnp.where(lane < LANES - shift, out, after)
        rows[pl.ds(j, PERIODS, stride=32), :] = jnp.where(lane < 100, out, 0.0)

    def turned(start, count, stride=1):
        size = -(-count // LANES) * LANES
        if stride == 1:
            block = rows[start : start + size, :]
        else:
            block = rows[pl.ds(start, size, stride=stride), :]
        return jnp.where(row_of((size, LANES)) < count, block, 0.0).T

    for g in range(3):
        to = slice(PAD * g, PAD * g + PAD)
        w_mail[to, :] = turned(g, MAIL, 3)[:PAD, :MAIL].astype(BF16)
        w_time[to, :] = turned(3 * MAIL + g, TENC, 3)[:PAD, :TENC].astype(BF16)
        w_hid[to, :] = turned(ROW_HH + g, MEM, 3)[:PAD, :MEM].astype(BF16)
    w_feat[...] = turned(ROW_NF, NFEAT)[:PAD, :NFEAT].astype(BF16)

    def column(r):
        return jnp.broadcast_to(rows[r : r + 1, :], (LANES, LANES)).T[:PAD, :]

    for g in range(3):
        gate_bias[0, PAD * g : PAD * g + PAD, :] = column(ROW_BIH + g)
        gate_bias[1, PAD * g : PAD * g + PAD, :] = column(ROW_BHH + g)
    for part in range(2):
        to = slice(PAD * part, PAD * part + PAD)

        def heads(start, count, part=part):
            size = -(-count // LANES) * LANES
            block = spread_heads(rows[pl.ds(ROW_KV + 2 * start + part, size, stride=2), :])
            return jnp.where(row_of((size, LANES)) < count, block, 0.0).T[:PAD]

        kv_h[to, :] = heads(0, MEM).astype(BF16)
        kv_e[to, :] = heads(MEM, EDGE)[:, :EDGE].astype(BF16)
        kv_t[to, :] = heads(MEM + EDGE, TENC)[:, :TENC].astype(BF16)
    q_rows = spread_heads(rows[ROW_Q : ROW_Q + LANES, :])
    keep = row_of((LANES, LANES)) < 100
    q_h[...] = jnp.where(keep, q_rows, 0.0).T[:PAD].astype(BF16)
    q_two = spread_heads(rows[ROW_Q + 100 : ROW_Q + 100 + LANES, :])
    q_sum = jnp.sum(jnp.where(keep, q_two, 0.0), 0, keepdims=True)
    q_one[...] = jnp.broadcast_to(q_sum, (LANES, LANES)).T[:PAD]
    att = spread_heads(turned(ROW_O, 100))
    o_att[...] = att[:PAD, :PAD].astype(BF16)
    o_att_n[...] = att.T[:PAD, :PAD].astype(BF16)
    o_h[...] = turned(ROW_O + 100, 100)[:PAD].astype(BF16)
    for start, out_t, out_n in ((ROW_SRC, src_t, src_n), (ROW_DST, dst_t, dst_n)):
        block = turned(start, 100)
        out_t[...] = block[:PAD, :PAD].astype(BF16)
        out_n[...] = block.T[:PAD, :PAD].astype(BF16)
    for i, r in enumerate((ROW_BO, ROW_GAIN, ROW_SHIFT, ROW_BPRED, ROW_OUT)):
        cols[i, :, :] = column(r)
    first = rows[ROW_BOUT : ROW_BOUT + 1, :]
    value = jnp.sum(jnp.where(lane_of((1, LANES)) == 0, first, 0.0), 1, keepdims=True)
    cols[5, :, :] = jnp.broadcast_to(value, (PAD, LANES))


def weights_of(flat):
    shapes = [
        ((GATES, MAIL), BF16),
        ((GATES, TENC), BF16),
        ((GATES, MEM), BF16),
        ((PAD, NFEAT), BF16),
        ((2, GATES, LANES), F32),
        ((KV, LANES), BF16),
        ((KV, EDGE), BF16),
        ((KV, TENC), BF16),
        ((PAD, LANES), BF16),
        ((PAD, LANES), F32),
        ((PAD, PAD), BF16),
        ((PAD, PAD), BF16),
        ((PAD, LANES), BF16),
        ((PAD, PAD), BF16),
        ((PAD, PAD), BF16),
        ((PAD, PAD), BF16),
        ((PAD, PAD), BF16),
        ((6, PAD, LANES), F32),
    ]
    return pl.pallas_call(
        weights_kernel,
        out_shape=[jax.ShapeDtypeStruct(s, d) for s, d in shapes],
        in_specs=[VMEM],
        out_specs=[VMEM] * len(shapes),
        scratch_shapes=[pltpu.VMEM((FLAT_ROWS + 16, LANES), F32), pltpu.VMEM((WROWS + 512, LANES), F32)],
        compiler_params=params_of(24 * 2**20),
        cost_estimate=pl.CostEstimate(flops=4_000_000, bytes_accessed=2_000_000, transcendentals=0),
    )(flat)


def gather_loop(index, table, out, count, base=0, to=0):
    group = 32

    def step(i, carry):
        for g in range(group // 16):
            at = pl.multiple_of(i * group + g * 16, 16)
            picked = [table[pl.ds(index[base + at + u], 1), :] for u in range(16)]
            out[pl.ds(to + at, 16), :] = jnp.concatenate(picked, 0).astype(out.dtype)
        return carry

    lax.fori_loop(0, count // group, step, 0)


def gru_products(mail, phi, feat, w_mail, w_time, w_hid, w_feat, low, gi, gh, nf):
    gi[...] = dot(w_mail[...], mail[...]) + dot(w_time[...], phi[...])
    gh[...] = dot(w_hid[...], low)
    if nf is not None:
        nf[...] = dot(w_feat[...], feat[...])


def gates_at(at, gi, gh, bias, kept):
    gr, gz, gn = (gi[PAD * g : PAD * g + PAD, at] + bias[0, PAD * g : PAD * g + PAD, :] for g in range(3))
    hr, hz, hn = (gh[PAD * g : PAD * g + PAD, at] + bias[1, PAD * g : PAD * g + PAD, :] for g in range(3))
    r = sigmoid(gr + hr)
    z = sigmoid(gz + hz)
    n = jnp.tanh(gn + r * hn)
    s = kept[:, at]
    return r, z, n, hn, s, (1.0 - z) * n + z * s


def to_rows(block):
    full = jnp.concatenate([block, jnp.zeros((LANES - PAD, LANES), F32)], 0)
    return full.T


def load_memory(mem, kept):
    low = mem[...].astype(BF16)
    kept[0:MEM, :] = low.astype(F32)
    kept[MEM:, :] = jnp.zeros((PAD - MEM, kept.shape[1]), F32)
    return low


def gru_kernel(
    index, mail, phi, mem, feat, w_mail, w_time, w_hid, w_feat, bias, sent, s_rows, s_cols, table, kept, gi, gh, nf
):
    block = mail.shape[1]
    step = pl.program_id(0)
    low = load_memory(mem, kept)
    gru_products(mail, phi, feat, w_mail, w_time, w_hid, w_feat, low, gi, gh, nf)

    def piece(i, carry):
        start = pl.multiple_of(i * LANES, LANES)
        at = pl.ds(start, LANES)
        _, _, _, _, _, renewed = gates_at(at, gi, gh, bias, kept)
        hidden = (renewed + nf[:, at]).astype(BF16).astype(F32)
        table[pl.ds(pl.multiple_of(step * block + start, LANES), LANES), :] = to_rows(hidden)
        s_rows[at, :] = to_rows(renewed)
        s_cols[:, at] = renewed[:MEM].astype(BF16)
        return carry

    lax.fori_loop(0, block // LANES, piece, 0)

    @pl.when(step == pl.num_programs(0) - 1)
    def _():
        gather_loop(index, table, sent, sent.shape[0])


def gru_specs(block):
    def cols(rows):
        return pl.BlockSpec((rows, block), lambda i: (0, i))

    return [cols(MAIL), cols(TENC), cols(MEM), cols(NFEAT)]


def gru_forward(index, mail, phi, mem, feat, wts, count):
    rows = mail.shape[1]
    block = 1024
    return pl.pallas_call(
        gru_kernel,
        grid=(rows // block,),
        out_shape=(
            jax.ShapeDtypeStruct((count, LANES), BF16),
            jax.ShapeDtypeStruct((rows, LANES), F32),
            jax.ShapeDtypeStruct((MEM, rows), BF16),
        ),
        in_specs=[SMEM] + gru_specs(block) + [VMEM] * 5,
        out_specs=(
            VMEM,
            pl.BlockSpec((block, LANES), lambda i: (i, 0)),
            pl.BlockSpec((MEM, block), lambda i: (0, i)),
        ),
        scratch_shapes=[
            pltpu.VMEM((rows, LANES), F32),
            pltpu.VMEM((PAD, block), F32),
            pltpu.VMEM((GATES, block), F32),
            pltpu.VMEM((GATES, block), F32),
            pltpu.VMEM((PAD, block), F32),
        ],
        compiler_params=params_of(48 * 2**20),
        cost_estimate=pl.CostEstimate(flops=4_000_000_000, bytes_accessed=24_000_000, transcendentals=3_000_000),
    )(index, mail, phi, mem, feat, *wts[:5])


def gather_kernel(index, table, out, wide):
    if table.dtype != F32:
        wide[...] = table[...].astype(F32)
        table = wide
    gather_loop(index, table, out, out.shape[0])


def gather_rows(table, index):
    return pl.pallas_call(
        gather_kernel,
        out_shape=jax.ShapeDtypeStruct((index.shape[0], LANES), BF16),
        in_specs=[SMEM, VMEM],
        out_specs=VMEM,
        scratch_shapes=[pltpu.VMEM(table.shape if table.dtype != F32 else (8, LANES), F32)],
        compiler_params=params_of(24 * 2**20),
        cost_estimate=pl.CostEstimate(
            flops=index.shape[0] * 1000, bytes_accessed=6_000_000, transcendentals=0
        ),
    )(index, table)


def gru_back_kernel(
    index,
    got,
    mail,
    phi,
    mem,
    feat,
    mail_time,
    update_time,
    w_mail,
    w_time,
    w_hid,
    bias,
    mem_new,
    mem_grad,
    time_new,
    grads,
    biases,
    wide,
    placed,
    kept,
    gi,
    gh,
    d_in,
    d_hid,
    d_low,
    direct,
    a_mail,
    a_time,
    a_hid,
    a_feat,
    a_bin,
    a_bhid,
):
    block = mail.shape[1]
    step = pl.program_id(0)

    @pl.when(step == 0)
    def _():
        wide[...] = got[...].astype(F32)
        if got.shape[0] != placed.shape[0]:
            placed[...] = jnp.zeros_like(placed)
        group = 32

        def move(i, carry):
            for u in range(group):
                at = i * group + u
                placed[pl.ds(index[at], 1), :] = wide[pl.ds(at, 1), :]
            return carry

        lax.fori_loop(0, got.shape[0] // group, move, 0)
        for ref in (a_mail, a_time, a_hid, a_feat, a_bin, a_bhid):
            ref[...] = jnp.zeros_like(ref)

    low = load_memory(mem, kept)
    gru_products(mail, phi, None, w_mail, w_time, w_hid, None, low, gi, gh, None)
    real = row_of((PAD, LANES)) < MEM

    def piece(i, carry):
        start = pl.multiple_of(i * LANES, LANES)
        at = pl.ds(start, LANES)
        r, z, n, hn, s, renewed = gates_at(at, gi, gh, bias, kept)
        turned = placed[pl.ds(pl.multiple_of(step * block + start, LANES), LANES), :].T
        live = turned[MEM : MEM + 1, :] > 0.5
        d = jnp.where(real, turned[:PAD], 0.0)
        d_low[:, at] = d.astype(BF16)
        dn = d * (1.0 - z) * (1.0 - n * n)
        dr = dn * hn * r * (1.0 - r)
        dz = d * (s - n) * z * (1.0 - z)
        dhn = dn * r
        direct[:, at] = d * z
        low_r, low_z = dr.astype(BF16), dz.astype(BF16)
        d_in[0:PAD, at] = low_r
        d_in[PAD : 2 * PAD, at] = low_z
        d_in[2 * PAD : 3 * PAD, at] = dn.astype(BF16)
        d_hid[0:PAD, at] = low_r
        d_hid[PAD : 2 * PAD, at] = low_z
        d_hid[2 * PAD : 3 * PAD, at] = dhn.astype(BF16)
        a_bin[0:PAD, :] += dr
        a_bin[PAD : 2 * PAD, :] += dz
        a_bin[2 * PAD : 3 * PAD, :] += dn
        a_bhid[...] += dhn
        mem_new[:, at] = jnp.where(live, renewed[:MEM], mem[:, at])
        time_new[:, at] = jnp.where(live, mail_time[:, at], update_time[:, at])
        return carry

    lax.fori_loop(0, block // LANES, piece, 0)
    din, dhid = d_in[...], d_hid[...]
    a_mail[:, :MAIL] += dot(din, mail[...], 1, 1)
    a_time[:, :TENC] += dot(din, phi[...], 1, 1)
    a_hid[:, :MEM] += dot(dhid, low, 1, 1)
    a_feat[:, :NFEAT] += dot(d_low[...], feat[...], 1, 1)
    mem_grad[...] = direct[0:MEM, :] + dot(w_hid[...], dhid, 0, 0)

    @pl.when(step == pl.num_programs(0) - 1)
    def _():
        def turned_back(ref, g):
            part = ref[PAD * g : PAD * g + PAD, :]
            return jnp.concatenate([part, jnp.zeros((LANES - PAD, part.shape[1]), F32)], 0).T

        grads[ROW_Q:GRU_ROWS, :] = jnp.zeros((GRU_ROWS - ROW_Q, LANES), F32)
        for g in range(3):
            grads[pl.ds(g, MAIL, stride=3), :] = turned_back(a_mail, g)[:MAIL]
            grads[pl.ds(3 * MAIL + g, TENC, stride=3), :] = turned_back(a_time, g)[:TENC]
            grads[pl.ds(ROW_HH + g, MEM, stride=3), :] = turned_back(a_hid, g)[:MEM]
        grads[ROW_NF:ROW_Q, :] = turned_back(a_feat, 0)[:NFEAT]
        sums = []
        for ref, g in ((a_bin, 0), (a_bin, 1), (a_bin, 2), (a_bin, 0), (a_bin, 1), (a_bhid, 0)):
            sums.append(jnp.sum(turned_back(ref, g), 0, keepdims=True))
        biases[...] = jnp.concatenate(sums + [jnp.zeros((2, LANES), F32)], 0)


def gru_backward(index, got, mail, phi, mem, feat, mail_time, update_time, wts):
    rows = mail.shape[1]
    block = 1024
    one = pl.BlockSpec((1, block), lambda i: (0, i))
    hundred = pl.BlockSpec((MEM, block), lambda i: (0, i))
    return pl.pallas_call(
        gru_back_kernel,
        grid=(rows // block,),
        out_shape=(
            jax.ShapeDtypeStruct((MEM, rows), F32),
            jax.ShapeDtypeStruct((MEM, rows), F32),
            jax.ShapeDtypeStruct((1, rows), jnp.int32),
            jax.ShapeDtypeStruct((GRU_ROWS, LANES), F32),
            jax.ShapeDtypeStruct((8, LANES), F32),
        ),
        in_specs=[SMEM, VMEM] + gru_specs(block) + [one, one] + [VMEM] * 4,
        out_specs=(hundred, hundred, one, VMEM, VMEM),
        scratch_shapes=[
            pltpu.VMEM(got.shape, F32),
            pltpu.VMEM((rows, LANES), F32),
            pltpu.VMEM((PAD, block), F32),
            pltpu.VMEM((GATES, block), F32),
            pltpu.VMEM((GATES, block), F32),
            pltpu.VMEM((GATES, block), BF16),
            pltpu.VMEM((GATES, block), BF16),
            pltpu.VMEM((PAD, block), BF16),
            pltpu.VMEM((PAD, block), F32),
            pltpu.VMEM((GATES, 512), F32),
            pltpu.VMEM((GATES, LANES), F32),
            pltpu.VMEM((GATES, LANES), F32),
            pltpu.VMEM((PAD, 512), F32),
            pltpu.VMEM((GATES, LANES), F32),
            pltpu.VMEM((PAD, LANES), F32),
        ],
        compiler_params=params_of(),
        cost_estimate=pl.CostEstimate(flops=7_000_000_000, bytes_accessed=28_000_000, transcendentals=3_000_000),
    )(index, got, mail, phi, mem, feat, mail_time, update_time, wts[0], wts[1], wts[2], wts[4])


def attention_kernel(
    index,
    counts,
    got,
    e0,
    e1,
    e2,
    p0,
    p1,
    p2,
    weight,
    kv_h,
    kv_e,
    kv_t,
    q_h,
    q_one,
    o_att,
    o_att_n,
    o_h,
    src_t,
    src_n,
    dst_t,
    dst_n,
    cols,
    sent,
    grads,
    losses,
    table,
    picked,
    kv,
    d_rows,
    a_kvh,
    a_kve,
    a_kvt,
    a_qh,
    a_q1,
    a_oa,
    a_oh,
    a_src,
    a_dst,
    a_col,
    a_one,
    *lanes,
):
    step = pl.program_id(0)
    near = NBR * SECT
    total = near + SECT
    scale = 50 ** (-0.5)
    sums = (a_kvh, a_kve, a_kvt, a_qh, a_q1, a_oa, a_oh, a_src, a_dst, a_col, a_one)

    @pl.when(step == 0)
    def _():
        table[...] = got[...].astype(F32)
        for ref in sums + lanes:
            ref[...] = jnp.zeros_like(ref)

    gather_loop(index, table, picked, total, step * total)
    roots = picked[near:total, :]

    def edge_of(k):
        return jnp.concatenate([e0[k], e1[k], e2[k]], 1)

    def code_of(k):
        return jnp.concatenate([p0[k], p1[k], p2[k]], 1)

    for k in range(NBR):
        kv[k] = (
            dot(kv_h[...], picked[k * SECT : k * SECT + SECT, :], 1, 1)
            + dot(kv_e[...], edge_of(k))
            + dot(kv_t[...], code_of(k))
        )
    query = dot(q_h[...], roots, 1, 1)
    o_root = dot(o_h[...], roots, 1, 1)
    bo, gain, shift, bpred, wout = (cols[i] for i in range(5))
    bout = cols[5, 0:1, :]
    real = row_of((PAD, LANES)) < MEM
    queries, probs, atts, pres, embs, norms = [], [], [], [], [], []
    for t in range(3):
        at = slice(t * EB, t * EB + EB)
        q = query[:, at] + q_one[...]
        scores = [[], []]
        for k in range(NBR):
            both = q * kv[k, 0:PAD, at]
            for h in range(2):
                scores[h].append(jnp.sum(both[h * HALF : h * HALF + HALF], 0, keepdims=True) * scale)
        weights = []
        for h in range(2):
            top = functools.reduce(jnp.maximum, scores[h])
            parts = [jnp.exp(x - top) for x in scores[h]]
            whole = functools.reduce(jnp.add, parts)
            weights.append([x / whole for x in parts])
        heads = []
        for h in range(2):
            rows = slice(PAD + h * HALF, PAD + h * HALF + HALF)
            heads.append(
                functools.reduce(jnp.add, [weights[h][k] * kv[k, rows, at] for k in range(NBR)])
            )
        att = jnp.concatenate(heads, 0).astype(BF16)
        pre = dot(o_att[...], att) + o_root[:, at] + bo
        active = gelu(pre)
        mean = jnp.sum(active, 0, keepdims=True) * (1.0 / MEM)
        centre = jnp.where(real, active - mean, 0.0)
        spread = jnp.sum(centre * centre, 0, keepdims=True) * (1.0 / MEM)
        inverse = lax.rsqrt(spread + 1e-05)
        hat = centre * inverse
        queries.append(q)
        probs.append(weights)
        atts.append(att)
        pres.append(pre)
        norms.append((hat, inverse))
        embs.append((hat * gain + shift).astype(BF16))

    src_proj = dot(src_t[...], embs[0]) + bpred
    tails = [src_proj + dot(dst_t[...], embs[1]), src_proj + dot(dst_t[...], embs[2])]
    acts = [gelu(x).astype(BF16) for x in tails]
    logits = [jnp.sum(x.astype(F32) * wout, 0, keepdims=True) + bout for x in acts]
    neg_weight = weight[...].astype(F32)

    def softplus(x):
        return jnp.maximum(x, 0.0) + jnp.log1p(jnp.exp(-jnp.abs(x)))

    d_pos = -sigmoid(-logits[0])
    d_neg = neg_weight * sigmoid(logits[1])
    a_one[0:1, :] += softplus(-logits[0]) + neg_weight * softplus(logits[1])
    a_one[1:2, :] += 1.0 + neg_weight
    a_one[2:3, :] += d_pos + d_neg
    d_logits = [x.astype(BF16).astype(F32) for x in (d_pos, d_neg)]
    a_col[4] += acts[0].astype(F32) * d_logits[0] + acts[1].astype(F32) * d_logits[1]
    d_tails = [wout * d * gelu_slope(x) for d, x in zip(d_logits, tails)]
    d_src = d_tails[0] + d_tails[1]
    a_col[3] += d_src
    d_low = [x.astype(BF16) for x in (d_src, d_tails[0], d_tails[1])]
    a_src[...] += dot(embs[0], d_low[0], 1, 1)
    a_dst[...] += dot(embs[1], d_low[1], 1, 1) + dot(embs[2], d_low[2], 1, 1)
    d_embs = [dot(src_n[...], d_low[0]), dot(dst_n[...], d_low[1]), dot(dst_n[...], d_low[2])]

    d_outs, d_queries = [], []
    for t in range(3):
        at = slice(t * EB, t * EB + EB)
        hat, inverse = norms[t]
        d_emb = d_embs[t]
        a_col[1] += d_emb * hat
        a_col[2] += d_emb
        d_hat = d_emb * gain
        mean = jnp.sum(d_hat, 0, keepdims=True) * (1.0 / MEM)
        mixed = jnp.sum(d_hat * hat, 0, keepdims=True) * (1.0 / MEM)
        d_active = jnp.where(real, inverse * (d_hat - mean - hat * mixed), 0.0)
        d_out = d_active * gelu_slope(pres[t])
        a_col[0] += d_out
        d_out_low = d_out.astype(BF16)
        d_outs.append(d_out_low)
        a_oa[...] += dot(d_out_low, atts[t], 1, 1)
        d_att = dot(o_att_n[...], d_out_low)
        q = queries[t]
        d_q = jnp.zeros((PAD, EB), F32)
        slopes = [[], []]
        for h in range(2):
            rows = slice(PAD + h * HALF, PAD + h * HALF + HALF)
            d_head = d_att[h * HALF : h * HALF + HALF]
            dp = [jnp.sum(d_head * kv[k, rows, at], 0, keepdims=True) for k in range(NBR)]
            mid = functools.reduce(jnp.add, [a * b for a, b in zip(dp, probs[t][h])])
            slopes[h] = [probs[t][h][k] * (dp[k] - mid) * scale for k in range(NBR)]
        for k in range(NBR):
            keys = kv[k, 0:PAD, at]
            factor = jnp.concatenate(
                [jnp.broadcast_to(slopes[h][k], (HALF, EB)) for h in range(2)], 0
            )
            share = jnp.concatenate(
                [jnp.broadcast_to(probs[t][h][k], (HALF, EB)) for h in range(2)], 0
            )
            d_q = d_q + factor * keys
            kv[k, 0:PAD, at] = factor * q
            kv[k, PAD:KV, at] = share * d_att
        d_queries.append(d_q)
        a_q1[...] += d_q.astype(BF16).astype(F32)

    d_out_all = jnp.concatenate(d_outs, 1)
    d_q_all = jnp.concatenate(d_queries, 1).astype(BF16)
    a_oh[...] += dot(d_out_all, roots)
    a_qh[...] += dot(d_q_all, roots)
    d_rows[near:total, :] = dot(d_out_all, o_h[...], 0, 0) + dot(d_q_all, q_h[...], 0, 0)
    for k in range(NBR):
        at = slice(k * SECT, k * SECT + SECT)
        d_kv = kv[k].astype(BF16)
        a_kvh[...] += dot(d_kv, picked[at, :])
        a_kve[:, :EDGE] += dot(d_kv, edge_of(k), 1, 1)
        a_kvt[:, :TENC] += dot(d_kv, code_of(k), 1, 1)
        d_rows[at, :] = dot(d_kv, kv_h[...], 0, 0)

    per = total // STREAMS
    base = step * total

    def add_rows(i, carry):
        for u in range(4):
            for s in range(STREAMS):
                at = s * per + i * 4 + u
                to = pl.ds(index[base + at], 1)
                lanes[s][to, :] += d_rows[pl.ds(at, 1), :]
        return carry

    lax.fori_loop(0, per // 4, add_rows, 0)

    @pl.when(step == pl.num_programs(0) - 1)
    def _():
        owners = counts.shape[0]
        slots = sent.shape[0] // owners
        piece = min(slots, LANES)

        def finish(i, carry):
            start = pl.multiple_of(i * piece, piece)
            at = pl.ds(start, piece)
            whole = functools.reduce(jnp.add, [ref[at, :] for ref in lanes])
            owner = start // slots
            slot = start - owner * slots + row_of((piece, LANES))
            lane = lane_of((piece, LANES))
            live = jnp.where((lane == MEM) & (slot < counts[owner]), 1.0, 0.0)
            sent[at, :] = jnp.where(lane < MEM, whole, live).astype(BF16)
            return carry

        lax.fori_loop(0, sent.shape[0] // piece, finish, 0)
        base_row = ATT_BASE

        def turned(block):
            short = -block.shape[0] % LANES
            if short:
                block = jnp.concatenate([block, jnp.zeros((short, block.shape[1]), F32)], 0)
            return block.T

        grads[...] = jnp.zeros_like(grads)
        q = ROW_Q - base_row
        grads[q : q + 100, :] = join_heads(turned(a_qh[...]))[:100]
        ones = jnp.sum(turned(a_q1[...]), 0, keepdims=True)
        grads[q + 100 : q + 200, :] = jnp.broadcast_to(join_heads(ones), (100, LANES))
        for part in range(2):
            rows = slice(PAD * part, PAD * part + PAD)
            start = ROW_KV - base_row + part
            grads[pl.ds(start, MEM, stride=2), :] = join_heads(turned(a_kvh[rows, :]))[:MEM]
            grads[pl.ds(start + 2 * MEM, EDGE, stride=2), :] = join_heads(turned(a_kve[rows, :]))[:EDGE]
            grads[pl.ds(start + 2 * (MEM + EDGE), TENC, stride=2), :] = join_heads(
                turned(a_kvt[rows, :])
            )[:TENC]
        o = ROW_O - base_row
        wide = jnp.concatenate([a_oa[...], jnp.zeros((PAD, LANES - PAD), F32)], 1)
        grads[o : o + 100, :] = turned(join_heads(wide))[:100]
        grads[o + 100 : o + 200, :] = turned(a_oh[...])[:100]
        for start, ref in ((ROW_SRC, a_src), (ROW_DST, a_dst)):
            wide = jnp.concatenate([ref[...], jnp.zeros((PAD, LANES - PAD), F32)], 1)
            grads[start - base_row : start - base_row + 100, :] = wide[:100]
        for i, r in enumerate((ROW_BO, ROW_GAIN, ROW_SHIFT, ROW_BPRED, ROW_OUT)):
            line = jnp.sum(turned(a_col[i]), 0, keepdims=True)
            grads[r - base_row : r - base_row + 1, :] = line
        line = jnp.where(
            lane_of((1, LANES)) == 0, jnp.sum(a_one[2:3, :], 1, keepdims=True), 0.0
        )
        grads[ROW_BOUT - base_row : ROW_BOUT - base_row + 1, :] = line
        losses[...] = jnp.broadcast_to(jnp.sum(a_one[...], 1, keepdims=True), (8, LANES))


def attention(index, counts, got, edges, codes, weight, wts):
    roots = edges.shape[2]
    blocks = roots // SECT

    def section(rows, t):
        return pl.BlockSpec((NBR, rows, EB), lambda b: (0, 0, t * blocks + b))

    slots = got.shape[0]
    total = (NBR + 1) * SECT
    return pl.pallas_call(
        attention_kernel,
        grid=(blocks,),
        out_shape=(
            jax.ShapeDtypeStruct((slots, LANES), BF16),
            jax.ShapeDtypeStruct((ATT_ROWS, LANES), F32),
            jax.ShapeDtypeStruct((8, LANES), F32),
        ),
        in_specs=[SMEM, SMEM, VMEM]
        + [section(EDGE, t) for t in range(3)]
        + [section(TENC, t) for t in range(3)]
        + [pl.BlockSpec((1, EB), lambda b: (0, b))]
        + [VMEM] * 13,
        out_specs=(VMEM, VMEM, VMEM),
        scratch_shapes=[
            pltpu.VMEM((slots, LANES), F32),
            pltpu.VMEM((total, LANES), BF16),
            pltpu.VMEM((NBR, KV, SECT), F32),
            pltpu.VMEM((total, LANES), F32),
            pltpu.VMEM((KV, LANES), F32),
            pltpu.VMEM((KV, 256), F32),
            pltpu.VMEM((KV, LANES), F32),
            pltpu.VMEM((PAD, LANES), F32),
            pltpu.VMEM((PAD, LANES), F32),
            pltpu.VMEM((PAD, PAD), F32),
            pltpu.VMEM((PAD, LANES), F32),
            pltpu.VMEM((PAD, PAD), F32),
            pltpu.VMEM((PAD, PAD), F32),
            pltpu.VMEM((5, PAD, LANES), F32),
            pltpu.VMEM((8, LANES), F32),
        ]
        + [pltpu.VMEM((slots, LANES), F32) for _ in range(STREAMS)],
        compiler_params=params_of(),
        cost_estimate=pl.CostEstimate(flops=9_000_000_000, bytes_accessed=20_000_000, transcendentals=1_000_000),
    )(index, counts, got, edges, edges, edges, codes, codes, codes, weight, *wts[5:])


def pack_kernel(gru, bias, att, losses, out, rows):
    rows[0:GRU_ROWS, :] = gru[...]
    rows[GRU_ROWS : ATT_BASE + ATT_ROWS, :] = att[8:, :]
    rows[ATT_BASE:GRU_ROWS, :] += att[0:8, :]
    rows[ROW_BIH : ROW_BIH + 8, :] += bias[...]
    rows[ATT_BASE + ATT_ROWS :, :] = jnp.zeros((rows.shape[0] - ATT_BASE - ATT_ROWS, LANES), F32)
    lane = lane_of((PERIODS, LANES))
    for m in range(25):
        first, shift = divmod(LANES * m, 100)
        value = None
        filled = 0
        source = first
        while filled < LANES:
            amount = shift if filled == 0 else -filled
            block = roll_left(rows[pl.ds(source, PERIODS, stride=32), :], amount)
            value = block if value is None else jnp.where(lane < filled, value, block)
            filled += 100 - (shift if filled == 0 else 0)
            source += 1
        out[pl.ds(m, PERIODS, stride=25), :] = value
    first, at = divmod(USED, LANES)
    tail = out.shape[0] - first
    where = row_of((tail, LANES)) * LANES + lane_of((tail, LANES))
    value = jnp.where(where < at, out[first:, :], 0.0)
    value = jnp.where(where == at, losses[0:1, :], value)
    value = jnp.where(where == at + 1, losses[1:2, :], value)
    out[first:, :] = value


def pack(gru, bias, att, losses):
    return pl.pallas_call(
        pack_kernel,
        out_shape=jax.ShapeDtypeStruct((25 * PERIODS + 7, LANES), F32),
        in_specs=[VMEM] * 4,
        out_specs=VMEM,
        scratch_shapes=[pltpu.VMEM((WROWS + 8, LANES), F32)],
        compiler_params=params_of(16 * 2**20),
        cost_estimate=pl.CostEstimate(flops=2_000_000, bytes_accessed=4_000_000, transcendentals=0),
    )(gru, bias, att, losses)


def mail_kernel(
    starts,
    rows,
    events,
    partner,
    edges,
    stamps,
    own,
    mailbox,
    mail_time,
    mail_new,
    time_new,
    near,
    far,
    kept,
    stage,
    lines,
):
    step = pl.program_id(0)
    senders = rows.shape[0] // (2 * EV)

    @pl.when(step == 0)
    def _():
        kept[...] = jnp.zeros_like(kept)
        stage[...] = jnp.zeros_like(stage)
        stage[EDGE + 1 : EDGE + 2, :] = jnp.ones((1, EV), F32)

    @pl.when(step < senders)
    def _():
        near[...] = partner[0].astype(F32)
        stage[0:EDGE, :] = edges[0].astype(F32)
        stage[EDGE : EDGE + 1, :] = stamps[0].astype(F32)
        for part in range(2):
            far[part] = stage[LANES * part : LANES * part + LANES, :].T

        def move(i, carry):
            place = step * 2 * EV + i
            to = pl.ds(rows[place], 1)
            event = pl.ds(events[place], 1)
            kept[0, to, :] = near[pl.ds(i, 1), :]
            kept[1, to, :] = far[0, event, :]
            kept[2, to, :] = far[1, event, :]
            return carry

        lax.fori_loop(starts[2 * step], starts[2 * step + 1], move, 0)

    @pl.when(step >= senders)
    def _():
        block = mailbox.shape[1]
        at = pl.ds(pl.multiple_of((step - senders) * block, LANES), block)
        last = kept[2, at, :].T
        stamp = EDGE - LANES
        has = last[stamp + 1 : stamp + 2, :] > 0.5
        lines[0:MEM, :] = own[...].astype(F32)
        lines[MEM : 2 * MEM, :] = kept[0, at, :].T[0:MEM]
        lines[2 * MEM : 2 * MEM + LANES, :] = kept[1, at, :].T
        lines[2 * MEM + LANES : MAIL, :] = last[0:stamp]
        mail_new[...] = jnp.where(has, lines[0:MAIL, :], mailbox[...].astype(F32)).astype(BF16)
        time_new[...] = jnp.where(has, last[stamp : stamp + 1, :].astype(jnp.int32), mail_time[...])


def deliver(starts, rows, events, partner, edges, stamps, own, mailbox, mail_time):
    senders = partner.shape[0]
    nodes = mailbox.shape[1]
    block = 1024

    def sender(i):
        return (jnp.minimum(i, senders - 1), 0, 0)

    def cols(count):
        return pl.BlockSpec((count, block), lambda i: (0, jnp.maximum(i - senders, 0)))

    return pl.pallas_call(
        mail_kernel,
        grid=(senders + nodes // block,),
        out_shape=(
            jax.ShapeDtypeStruct((MAIL, nodes), BF16),
            jax.ShapeDtypeStruct((1, nodes), jnp.int32),
        ),
        in_specs=[
            SMEM,
            SMEM,
            SMEM,
            pl.BlockSpec((1, 2 * EV, LANES), sender),
            pl.BlockSpec((1, EDGE, EV), sender),
            pl.BlockSpec((1, 1, EV), sender),
            cols(MEM),
            cols(MAIL),
            cols(1),
        ],
        out_specs=(cols(MAIL), cols(1)),
        scratch_shapes=[
            pltpu.VMEM((2 * EV, LANES), F32),
            pltpu.VMEM((2, EV, LANES), F32),
            pltpu.VMEM((3, nodes, LANES), F32),
            pltpu.VMEM((2 * LANES, EV), F32),
            pltpu.VMEM((MAIL + 6, block), F32),
        ],
        compiler_params=params_of(48 * 2**20),
        cost_estimate=pl.CostEstimate(flops=20_000_000, bytes_accessed=16_000_000, transcendentals=0),
    )(starts, rows, events, partner, edges, stamps, own, mailbox, mail_time)


def flip(x, axis, mask):
    return lax.ppermute(x, axis, [(i, i ^ mask) for i in range(lax.axis_size(axis))])


def axis_bits():
    table = []
    for axis in ("batch", "node"):
        count = lax.axis_size(axis).bit_length() - 1
        for b in reversed(range(count)):
            table.append((axis, 1 << b))
    return table


def bit_of(axis, mask):
    return (lax.axis_index(axis) & mask) != 0


def gather_params(x):
    table = axis_bits()
    order = [i for i, (a, m) in enumerate(table) if a == "node" and m > 1]
    order += [i for i, (a, m) in enumerate(table) if a == "batch"][::-1]
    order += [len(table) - 1]
    shape = x.shape
    x = x.reshape((1,) * len(table) + shape)
    for i in order:
        axis, mask = table[i]
        y = flip(x, axis, mask)
        bit = bit_of(axis, mask)
        x = jnp.concatenate([jnp.where(bit, y, x), jnp.where(bit, x, y)], i)
    return x.reshape((-1,) + shape[1:])


def scatter_sum(x):
    table = axis_bits()
    order = [len(table) - 1]
    order += [i for i, (a, m) in enumerate(table) if a == "batch"]
    order += [i for i, (a, m) in enumerate(table) if a == "node" and m > 1][::-1]
    x = x.reshape((2,) * len(table) + (-1, LANES))
    for i in order:
        axis, mask = table[i]
        bit = bit_of(axis, mask).astype(jnp.int32)
        away = lax.dynamic_slice_in_dim(x, 1 - bit, 1, i)
        x = lax.dynamic_slice_in_dim(x, bit, 1, i) + flip(away, axis, mask)
    return x.reshape(-1, LANES)


def sum_all(x):
    for axis, mask in axis_bits()[::-1]:
        x = x + flip(x, axis, mask)
    return x


def swap(x):
    return lax.all_to_all(x, "node", split_axis=0, concat_axis=0, tiled=True)


def to_slot(live, counts, slots):
    upper = jnp.cumsum(counts)
    shape = (-1,) + (1,) * live.ndim
    passed = live[None] >= upper.reshape(shape)
    return live + jnp.sum(jnp.where(passed, (slots - counts).reshape(shape), 0), 0)


def body(
    params,
    moment1,
    moment2,
    memory,
    mailbox,
    mail_time,
    update_time,
    node_feat,
    req_rows,
    req_count,
    root_live,
    nbr_live,
    nbr_dt,
    nbr_edge,
    ev_edge,
    ev_time,
    neg_count,
):
    shards = lax.axis_size("node")
    me = lax.axis_index("node")
    slots = req_rows.shape[3]
    wanted = req_rows[0, 0]
    counts = req_count[0, 0]
    mem_cols = memory[0].T
    mail_cols = mailbox[0].T
    feat_cols = node_feat.T
    edge_cols = jnp.transpose(nbr_edge[0, 0], (1, 2, 0))

    flat = gather_params(params.astype(BF16).reshape(1, -1, LANES)).reshape(-1, LANES)
    wts = weights_of(flat)
    asked = swap(wanted).reshape(-1)

    dt = nbr_dt[0, 0].T
    codes_n, codes_m = time_codes(dt, mail_time - update_time)

    near_slot = to_slot(nbr_live[0, 0].T, counts, slots)
    root_slot = to_slot(root_live[0, 0], counts, slots)
    blocks = EV // EB
    near_index = jnp.transpose(near_slot.reshape(NBR, 3, blocks, EB), (2, 0, 1, 3))
    root_index = jnp.transpose(root_slot.reshape(3, blocks, EB), (1, 0, 2))
    index = jnp.concatenate(
        [near_index.reshape(blocks, -1), root_index.reshape(blocks, -1)], 1
    ).reshape(-1)

    ends = root_slot[:2].reshape(-1)
    ordered = lax.sort(ends * (2 * EV) + jnp.arange(2 * EV, dtype=jnp.int32))
    end_id = ordered % (2 * EV)
    end_slot = ordered // (2 * EV)
    partner_slot = ends[(end_id + EV) % (2 * EV)]
    end_row = wanted.reshape(-1)[end_slot]
    first = jnp.sum(
        (end_slot[None, :] < (jnp.arange(LANES, dtype=jnp.int32) * slots)[:, None]).astype(jnp.int32), 1
    )
    notes = jnp.concatenate([end_row, end_id % EV, ev_time[0, 0], first]).reshape(-1, LANES)
    notes = lax.all_gather(notes, "node", axis=0, tiled=False)
    edges_all = lax.all_gather(ev_edge[0, 0].T, "node", axis=0, tiled=False)
    notes = notes.reshape(shards, -1)

    h_sent, s_rows, s_cols = gru_forward(asked, mail_cols, codes_m, mem_cols, feat_cols, wts, shards * slots)
    h_got = swap(h_sent.reshape(shards, slots, LANES))
    s_sent = gather_rows(s_rows, asked)
    h_got, s_sent = lax.optimization_barrier((h_got, s_sent))
    s_got = swap(s_sent.reshape(shards, slots, LANES)).reshape(-1, LANES)

    d_sent, att_grads, losses = attention(
        index, counts, h_got.reshape(-1, LANES), edge_cols, codes_n, neg_count[0], wts
    )
    d_got = swap(d_sent.reshape(shards, slots, LANES)).reshape(-1, LANES)

    partner = gather_rows(s_got, partner_slot)
    partner = lax.all_gather(partner, "node", axis=0, tiled=False)

    mem_new, mem_grad, upd_new, gru_grads, bias_grads = gru_backward(
        asked, d_got, mail_cols, codes_m, mem_cols, feat_cols, mail_time, update_time, wts
    )
    packed = pack(gru_grads, bias_grads, att_grads, losses)[:FLAT_ROWS]
    shard = scatter_sum(packed)

    events_of = notes[:, 2 * EV : 4 * EV].reshape(-1)
    rows_of = notes[:, : 2 * EV].reshape(-1)
    stamps = notes[:, 4 * EV : 5 * EV].reshape(shards, 1, EV)
    starts = lax.dynamic_slice_in_dim(notes[:, 5 * EV :], me, 2, 1).reshape(-1)
    mail_new, stamp_new = deliver(
        starts, rows_of, events_of, partner, edges_all, stamps, s_cols, mail_cols, mail_time
    )

    number = lax.axis_index("batch") * shards + me
    size = shard.shape[0] * LANES
    place = number * size + jnp.arange(size, dtype=jnp.int32).reshape(-1, LANES)
    grad = jnp.where(place < USED, shard, 0.0)
    values = jnp.stack(
        [
            jnp.sum(grad * grad),
            jnp.sum(jnp.where(place == USED, shard, 0.0)),
            jnp.sum(jnp.where(place == USED + 1, shard, 0.0)),
        ]
    )
    values = sum_all(jnp.zeros((8, LANES), F32).at[0, :3].set(values))
    grad_norm = jnp.sqrt(values[0, 0])
    clipped = grad.reshape(-1) * jnp.minimum(1.0, clip_limit / (grad_norm + 1e-06))
    moment1_new = beta_first * moment1 + (1.0 - beta_first) * clipped
    moment2_new = beta_second * moment2 + (1.0 - beta_second) * clipped * clipped
    ratio = (
        moment1_new
        / (1.0 - beta_first**STEP)
        / (jnp.sqrt(moment2_new / (1.0 - beta_second**STEP)) + adam_floor)
    )
    params_new = params - learn_rate * (ratio + decay_rate * params)
    return (
        values[0, 1],
        values[0, 2],
        grad_norm,
        params_new,
        moment1_new,
        moment2_new,
        params_new.astype(BF16),
        mem_new.T[None],
        mail_new.T[None],
        stamp_new,
        upd_new,
        mem_grad.T[None],
    )


def solution(mesh):
    both, split = P(("batch", "node")), P("batch", "node")
    in_specs = (both, both, both, split, split, split, split, P("node")) + (split,) * 9
    out_specs = (P(), P(), P()) + (both,) * 4 + (split,) * 5
    return jax.shard_map(body, mesh=mesh, in_specs=in_specs, out_specs=out_specs, check_vma=False)
```

time: 1980 us -> 456 us (0.23)
  local copies, waits for them, and re-layouts: 897 us -> 51.1 us
  other arithmetic: 409 us -> 17 us
  blocking collectives: 436 us -> 67.6 us
  Pallas kernels: 0 us -> 187 us
  matrix products: 78.9 us -> 0 us
    all_gather x1, blocking collectives: 397 us -> 14.2 us  [body(): notes = lax.all_gather(notes, 'node', axis=0, tiled=False)]
    gather x15 -> x2, local copies, waits for them, and re-layouts: 298 us -> 11.2 us  [the longest x1 6.15 us: body(): end_row = wanted.reshape(-1)[end_slot]]
    scatter x12 -> x1, local copies, waits for them, and re-layouts: 217 us -> 0.01 us  [body(): values = sum_all(jnp.zeros((8, LANES), F32).at[0, :3].set(values))]
    pallas_call x0 -> x9, Pallas kernels: none -> 187 us  [the longest x1 70.3 us: attention(): pl.pallas_call(attention_kernel, grid=(blocks,), out_shape=(jax.ShapeDtyp...]
    scatter-add x3 -> x0, other arithmetic: 141 us -> none  [the longest x2 92.5 us: body(): jnp.zeros((LIVE, MEM), single).at[roots].add(d_root)]
    unnamed x3 -> x1, other arithmetic: 137 us -> 0.01 us
    convert_element_type x14 -> x0, local copies, waits for them, and re-layouts: 112 us -> none  [the longest x1 38 us: body(): got_back, got_mail, got_tags = (lax.all_to_all(slots_back.reshape(1, shar...]
    concatenate x7 -> x0, local copies, waits for them, and re-layouts: 84.6 us -> none  [the longest x3 38.4 us: widen_cols(): jnp.concatenate([array, jnp.zeros(array.shape[:-1] + (extra,), array.dtyp...]
  transfers between devices with their start and end apart: 7 -> 20, of which waited for: 3 -> 12; matrix products, arithmetic and copies ran while one was open for 32% -> 11% of each run, Pallas kernels for 0% -> 15%
where the time goes in v1:
time: 456 us; the launch traced here: 452 us
  Pallas kernels  187 us (41%)
  waiting for transfers between devices  77.8 us (17%)
  blocking collectives  67.6 us (15%)
  local copies, waits for them, and re-layouts  51.1 us (11%)
  starting transfers between devices  35.1 us (8%)
  other arithmetic  17 us (4%)
  between operations  16.6 us (4%)
    pallas_call x1, Pallas kernels, attention(): pl.pallas_call(attention_kernel, grid=(blocks,), out_shape=(jax.ShapeDtyp...  70.3 us
    all_to_all x1, blocking collectives, swap(): return lax.all_to_all(x, 'node', split_axis=0, concat_axis=0, tiled=True)  53.4 us
    pallas_call x1, Pallas kernels, gru_backward(): pl.pallas_call(gru_back_kernel, grid=(rows // block,), out_shape=(jax.Sha...  40.2 us
    all_to_all x3, waiting for transfers between devices, swap(): return lax.all_to_all(x, 'node', split_axis=0, concat_axis=0, tiled=True)  39.4 us
    ppermute x15, waiting for transfers between devices, flip(): lax.ppermute(x, axis, [(i, i ^ mask) for i in range(lax.axis_size(axis))])  37.7 us
    unnamed x104, local copies, waits for them, and re-layouts  33.9 us
    pallas_call x1, Pallas kernels, gru_forward(): pl.pallas_call(gru_kernel, grid=(rows // block,), out_shape=(jax.ShapeDty...  30.5 us
    ppermute x15, starting transfers between devices, flip(): lax.ppermute(x, axis, [(i, i ^ mask) for i in range(lax.axis_size(axis))])  20.6 us
  transfers between devices with their start and end apart: 20, of which 12 were waited for; matrix products, arithmetic and copies ran while one was open for 11% of the time, Pallas kernels for 15%

profile of v1, /device:TPU:0, one launch (start us, length us, event | category | flops | bytes accessed | tf_op | source)
XLA Modules:
  0.0 452.1 jit_solution(11367818617220601143)
XLA Ops:
  7.2 0.8 convert_bitcast_fusion
  8.0 4.0 collective-permute-start
  12.1 1.8 collective-permute-done
  13.8 0.8 broadcast_select_fusion.9
  14.7 2.0 collective-permute-start.1
  16.6 2.1 collective-permute-done.1
  18.8 2.0 collective-permute-start.2
  20.8 2.6 collective-permute-done.2
  23.5 2.0 collective-permute-start.3
  25.5 3.5 collective-permute-done.3
  29.8 5.4 %all-to-all-start = ((s32[8,1,1024]{2,1,0:T(1,128)}), s32[8,1,1024]{2,1,0:T(1,128)S(1)}, u32[]{:S(2)}, u32[]{:S(2)}) async-start(s32[8,1,1024]{2,1,0:T(1,128)} %all_to_all.15), calls=%async_computation | async-start | bytes 65536 | tf_op jit(solution)/shard_map/all_to_all | solution.py:1071
  35.3 6.0 %copy.59 = f32[1,8192,100]{1,2,0:T(8,128)} copy(f32[1,8192,100]{1,0,2:T(1,128)} %param.23) | data formatting | bytes 6553600
  41.4 9.8 %shard_map.265 = (bf16[10,100,1536]{2,1,0:T(8,128)(2,1)S(1)}, bf16[100,8192]{1,0:T(8,128)(2,1)S(1)}) custom-call(s32[10,1536]{1,0:T(8,128)S(1)} %bitcast.146, s32[1,8192]{1,0:T(1,128)S(1)} %sub.36.delta, f32[100,128]{1,0:T(8,128)S(1)} %copy-done.30), custom_call_target="tpu_custom_call" | custom-call | flops 60000000 | bytes 5000000 | tf_op jit(solution)/shard_map/pallas_call | solution.py:164
  51.2 1.7 copy-done.31
  53.0 3.3 shard_map.266
  62.5 30.5 %shard_map.267 = (bf16[8192,128]{1,0:T(8,128)(2,1)}, f32[8192,128]{1,0:T(8,128)}, bf16[100,8192]{1,0:T(8,128)(2,1)S(1)}) custom-call(s32[8192]{0:T(1024)S(1)} %bitcast.143, bf16[386,8192]{1,0:T(8,128)(2,1)} %bitcast.150, bf16[100,8192]{1,0:T(8,128)(2,1)S(1)} %get-tuple-element.61.phi, f32[100,8192]{1,0:T(8,128)} %bitcast.153, bf16[413,8192]{1,0:T(8,128)(2,1)} %bitcast.155, ...), custom_call_target="tpu_custom_call" | custom-call | flops 4000000000 | bytes 24000000 | tf_op jit(solution)/shard_map/pallas_call | solution.py:373
  93.0 1.3 copy-done.3
  94.3 5.2 %all-to-all-start.1 = ((bf16[8,1024,128]{2,1,0:T(8,128)(2,1)}), bf16[8,1024,128]{2,1,0:T(8,128)(2,1)S(1)}, u32[]{:S(2)}, u32[]{:S(2)}) async-start(bf16[8,1024,128]{2,1,0:T(8,128)(2,1)} %bitcast.163), calls=%async_computation.1 | async-start | bytes 4194304 | tf_op jit(solution)/shard_map/all_to_all | solution.py:1071
  100.2 0.6 reshape.192.index
  100.8 2.2 copy-done
  103.0 10.7 %shard_map.268 = bf16[8192,128]{1,0:T(8,128)(2,1)} custom-call(s32[8192]{0:T(1024)S(1)} %bitcast.144, f32[8192,128]{1,0:T(8,128)S(1)} %copy-done), custom_call_target="tpu_custom_call" | custom-call | flops 8192000 | bytes 6000000 | tf_op jit(solution)/shard_map/pallas_call | solution.py:407
  113.7 34.9 %all-to-all-done.1 = bf16[8,1024,128]{2,1,0:T(8,128)(2,1)S(1)} async-done(((bf16[8,1024,128]{2,1,0:T(8,128)(2,1)}), bf16[8,1024,128]{2,1,0:T(8,128)(2,1)S(1)}, u32[]{:S(2)}, u32[]{:S(2)}) %all-to-all-start.1) | async-done | bytes 2097184 | tf_op jit(solution)/shard_map/all_to_all | solution.py:1071
  148.6 1.3 copy-done.34
  149.9 70.3 %shard_map.269 = (bf16[8192,128]{1,0:T(8,128)(2,1)}, f32[1448,128]{1,0:T(8,128)}, f32[8,128]{1,0:T(8,128)}) custom-call(s32[16896]{0:T(1024)} %reshape.192.index, s32[8]{0:T(128)} %bitcast.184, bf16[8192,128]{1,0:T(8,128)(2,1)} %bitcast.161, bf16[10,186,1536]{2,1,0:T(8,128)(2,1)} %bitcast.180, bf16[10,186,1536]{2,1,0:T(8,128)(2,1)} %bitcast.181, ...), custom_call_target="tpu_custom_call" | custom-call | flops 8999999488 | bytes 20000000 | tf_op jit(solution)/shard_map/pallas_call | solution.py:838
  220.3 53.4 %all_to_all.24 = bf16[8,1024,128]{2,1,0:T(8,128)(2,1)} all-to-all(bf16[8,1024,128]{2,1,0:T(8,128)(2,1)} %bitcast.164), channel_id=1, replica_groups=mesh['batch'=4,'node'=8] {'node'}, dimensions={0} | all-to-all | bytes 4194304 | tf_op jit(solution)/shard_map/all_to_all | solution.py:1071
  273.7 3.6 all-to-all-start.3
  277.3 0.7 all-gather.8.cloned.1.call-update
  278.3 40.2 %shard_map.270 = (f32[100,8192]{1,0:T(8,128)}, f32[100,8192]{1,0:T(8,128)}, s32[1,8192]{1,0:T(1,128)}, f32[2176,128]{1,0:T(8,128)}, f32[8,128]{1,0:T(8,128)}) custom-call(s32[8192]{0:T(1024)} %bitcast.145, bf16[8192,128]{1,0:T(8,128)(2,1)} %bitcast.162, bf16[386,8192]{1,0:T(8,128)(2,1)} %bitcast.151, bf16[100,8192]{1,0:T(8,128)(2,1)} %copy-done.2, ...), custom_call_target="tpu_custom_call" | custom-call | flops 7000000000 | bytes 28000000 | tf_op jit(solution)/shard_map/pallas_call | solution.py:537
  318.5 1.2 copy-done.6
  319.8 0.7 copy-done.16
  320.5 1.8 shard_map.271
  322.4 0.9 constant_dynamic-slice_fusion.5
  323.7 4.4 sort.14
  328.1 1.3 fusion.14
  329.4 5.0 %gather_fusion.1 = s32[1024]{0:T(1024)S(1)} fusion(s32[1024]{0:T(1024)S(1)} %bitcast.148, s32[1024]{0:T(1024)} %get-tuple-element.179), kind=kCustom, calls=%fused_computation.1 | custom fusion | bytes 12288 | tf_op jit(solution)/shard_map/gather | solution.py:1130
  334.4 4.5 all-to-all-done.3
  338.9 2.6 shard_map.272
  341.5 1.2 dynamic-slice_add_fusion
  342.8 1.6 collective-permute-start.6
  344.4 8.5 %collective-permute-done.6 = f32[1,2,2,2,1,88,128]{6,5,4,3,2,1,0:T(8,128)S(1)} collective-permute-done((f32[1,2,2,2,1,88,128]{6,5,4,3,2,1,0:T(8,128)S(1)}, f32[1,2,2,2,1,88,128]{6,5,4,3,2,1,0:T(8,128)S(1)}, u32[]{:S(2)}, u32[]{:S(2)}) %collective-permute-start.6) | collective-permute-done | bytes 360480 | tf_op jit(solution)/shard_map/ppermute | solution.py:1019
  352.9 1.6 collective-permute-start.7
  354.5 4.0 collective-permute-done.7
  358.6 9.0 %collective-permute-done.8 = f32[1,1,2,1,1,88,128]{6,5,4,3,2,1,0:T(8,128)S(1)} collective-permute-done((f32[1,1,2,1,1,88,128]{6,5,4,3,2,1,0:T(8,128)S(1)}, f32[1,1,2,1,1,88,128]{6,5,4,3,2,1,0:T(8,128)S(1)}, u32[]{:S(2)}, u32[]{:S(2)}) %collective-permute-start.8) | collective-permute-done | bytes 90144 | tf_op jit(solution)/shard_map/ppermute | solution.py:1019
  368.3 0.7 convert_reduce_fusion
  369.0 6.2 %gather_fusion = s32[1024]{0:T(1024)S(1)} fusion(s32[8192]{0:T(1024)S(1)} %bitcast.149, s32[1024]{0:T(1024)S(1)} %copy-done.45), kind=kCustom, calls=%fused_computation | custom fusion | bytes 12288 | tf_op jit(solution)/shard_map/gather | solution.py:1131
  375.2 1.4 fusion.3
  376.6 2.0 maximum_bitcast_fusion
  378.7 0.7 add_bitcast_fusion
  379.8 2.0 slice_add_fusion.1
  382.0 2.6 collective-permute-start.11
  384.6 14.2 %all_gather.15 = s32[8,21,128]{2,1,0:T(8,128)S(1)} all-gather(s32[1,21,128]{2,1,0:T(8,128)S(1)} %add_bitcast_fusion), channel_id=1, replica_groups=mesh['batch'=4,'node'=8] {'node'}, dimensions={0}, use_global_device_ids=true | all-gather | bytes 96768 | tf_op jit(solution)/shard_map/all_gather | solution.py:1136
  398.8 0.6 collective-permute-start.12
  399.4 3.9 collective-permute-done.12
  403.4 1.8 collective-permute-start.13
  405.2 1.8 collective-permute-done.13
  407.0 1.8 collective-permute-start.14
  408.9 1.3 slice.63
  410.3 0.7 reshape.208.stamps
  411.0 5.1 %copy.38 = f32[1,8192,100]{1,0,2:T(1,128)} copy(f32[1,8192,100]{1,2,0:T(8,128)S(1)} %bitcast.160) | data formatting | bytes 6553600
  416.2 5.1 %copy.39 = f32[1,8192,100]{1,0,2:T(1,128)} copy(f32[1,8192,100]{1,2,0:T(8,128)S(1)} %bitcast.159) | data formatting | bytes 6553600
  422.7 0.7 fusion.18
  423.4 1.6 copy-done.1
  425.0 1.4 copy-done.5
  426.4 17.8 %shard_map.273 = (bf16[386,8192]{1,0:T(8,128)(2,1)}, s32[1,8192]{1,0:T(1,128)}) custom-call(s32[16]{0:T(128)S(1)} %reshape.203.starts, s32[8192]{0:T(1024)S(1)} %get-tuple-element.187.rows, s32[8192]{0:T(1024)S(1)} %get-tuple-element.186.events, bf16[8,1024,128]{2,1,0:T(8,128)(2,1)S(1)} %bitcast.142, bf16[8,186,512]{2,1,0:T(8,128)(2,1)S(1)} %copy-done.5, ...), custom_call_target="tpu_custom_call" | custom-call | flops 20000000 | bytes 16000000 | tf_op jit(solution)/shard_map/pallas_call | solution.py:987
  (153 shorter events, 11.0 us)
Async XLA Ops:
  7.2 22.0 %copy-start.38 = (s32[1,1,8,1024]{3,2,1,0:T(8,128)S(1)}, s32[1,1,8,1024]{3,2,1,0:T(8,128)}, u32[]{:S(2)}) copy-start(s32[1,1,8,1024]{3,2,1,0:T(8,128)} %param.28) | copy-start | bytes 98308
  7.2 28.1 %copy-start.40 = (s32[1,1,1536,10]{2,1,3,0:T(1,128)S(1)}, s32[1,1,1536,10]{2,1,3,0:T(1,128)}, u32[]{:S(2)}) copy-start(s32[1,1,1536,10]{2,1,3,0:T(1,128)} %param.32) | copy-start | bytes 184324
  8.0 5.8 %collective-permute-start = (bf16[1,1,1,1,1,1,88,128]{7,6,4,3,2,1,0,5:T(8,128)(2,1)S(1)}, bf16[1,1,1,1,1,1,88,128]{7,6,4,3,2,1,0,5:T(8,128)(2,1)S(1)}, u32[]{:S(2)}, u32[]{:S(2)}) collective-permute-start(bf16[1,1,1,1,1,1,88,128]{7,6,4,3,2,1,0,5:T(8,128)(2,1)S(1)} %convert_bitcast_fusion), channel_id=1, source_target_pairs={{0,4},{1,5},{2,6},{3,7},{4,0},{5,1},{6,2},{7,3},{8,12},{9,13},{10,... | collective-permute-start | bytes 67592 | tf_op jit(solution)/shard_map/ppermute | solution.py:1019
  14.7 4.1 collective-permute-start.1
  18.8 4.6 %collective-permute-start.2 = (bf16[1,1,2,2,1,1,88,128]{7,6,4,3,2,1,0,5:T(8,128)(2,1)S(1)}, bf16[1,1,2,2,1,1,88,128]{7,6,4,3,2,1,0,5:T(8,128)(2,1)S(1)}, u32[]{:S(2)}, u32[]{:S(2)}) collective-permute-start(bf16[1,1,2,2,1,1,88,128]{7,6,4,3,2,1,0,5:T(8,128)(2,1)S(1)} %pad_maximum_fusion.3), channel_id=1, source_target_pairs={{0,8},{8,0},{16,24},{24,16},{1,9},{9,1},{17,25},{25,17},{2,10},{10... | collective-permute-start | bytes 270344 | tf_op jit(solution)/shard_map/ppermute | solution.py:1019
  23.5 5.6 %collective-permute-start.3 = (bf16[1,2,2,2,1,1,88,128]{7,6,4,3,2,1,0,5:T(8,128)(2,1)S(1)}, bf16[1,2,2,2,1,1,88,128]{7,6,4,3,2,1,0,5:T(8,128)(2,1)S(1)}, u32[]{:S(2)}, u32[]{:S(2)}) collective-permute-start(bf16[1,2,2,2,1,1,88,128]{7,6,4,3,2,1,0,5:T(8,128)(2,1)S(1)} %pad_maximum_fusion.2), channel_id=1, source_target_pairs={{0,16},{8,24},{16,0},{24,8},{1,17},{9,25},{17,1},{25,9},{2,18},{10... | collective-permute-start | bytes 540680 | tf_op jit(solution)/shard_map/ppermute | solution.py:1019
  29.1 23.8 %collective-permute-start.4 = (bf16[2,2,2,2,1,1,88,128]{7,6,4,3,2,1,0,5:T(8,128)(2,1)S(1)}, bf16[2,2,2,2,1,1,88,128]{7,6,4,3,2,1,0,5:T(8,128)(2,1)S(1)}, u32[]{:S(2)}, u32[]{:S(2)}) collective-permute-start(bf16[2,2,2,2,1,1,88,128]{7,6,4,3,2,1,0,5:T(8,128)(2,1)S(1)} %pad_maximum_fusion.1), channel_id=1, source_target_pairs={{0,1},{1,0},{2,3},{3,2},{4,5},{5,4},{6,7},{7,6},{8,9},{9,8},{10,11... | collective-permute-start | bytes 1081352 | tf_op jit(solution)/shard_map/ppermute | solution.py:1019
  29.8 32.6 %all-to-all-start = ((s32[8,1,1024]{2,1,0:T(1,128)}), s32[8,1,1024]{2,1,0:T(1,128)S(1)}, u32[]{:S(2)}, u32[]{:S(2)}) async-start(s32[8,1,1024]{2,1,0:T(1,128)} %all_to_all.15), calls=%async_computation | async-start | bytes 65536 | tf_op jit(solution)/shard_map/all_to_all | solution.py:1071
  35.3 6.1 %copy-start.11 = (s32[1,8192]{1,0:T(1,128)S(1)}, s32[1,8192]{1,0:T(1,128)}, u32[]{:S(2)}) copy-start(s32[1,8192]{1,0:T(1,128)} %mail_time.3) | copy-start | bytes 98308
  35.3 6.0 %copy-start.43 = (s32[1,8192]{1,0:T(1,128)S(1)}, s32[1,8192]{1,0:T(1,128)}, u32[]{:S(2)}) copy-start(s32[1,8192]{1,0:T(1,128)} %update_time.1) | copy-start | bytes 98308
  35.3 6.1 %copy-start.30 = (f32[100,128]{1,0:T(8,128)S(1)}, f32[100,128]{1,0:T(8,128)}, u32[]{:S(2)}) copy-start(f32[100,128]{1,0:T(8,128)} %constant.139.clone.freq) | copy-start | bytes 153604
  51.2 1.7 copy-start.31
  52.9 40.1 %copy-start.2 = (bf16[100,8192]{1,0:T(8,128)(2,1)}, bf16[100,8192]{1,0:T(8,128)(2,1)S(1)}, u32[]{:S(2)}) copy-start(bf16[100,8192]{1,0:T(8,128)(2,1)S(1)} %get-tuple-element.61.phi) | copy-start | bytes 4915204
  56.3 0.6 copy-start.18
  56.9 0.6 copy-start.20
  57.6 0.6 copy-start.21
  58.2 0.6 copy-start.22
  58.8 0.6 copy-start.23
  59.4 0.6 copy-start.24
  60.0 0.6 copy-start.25
  62.4 30.5 %copy-start.8 = (bf16[336,386]{1,0:T(8,128)(2,1)}, bf16[336,386]{1,0:T(8,128)(2,1)S(1)}, u32[]{:S(2)}) copy-start(bf16[336,386]{1,0:T(8,128)(2,1)S(1)} %get-tuple-element.62.w_mail) | copy-start | bytes 778180
  62.4 30.6 %copy-start.9 = (f32[2,336,128]{2,1,0:T(8,128)}, f32[2,336,128]{2,1,0:T(8,128)S(1)}, u32[]{:S(2)}) copy-start(f32[2,336,128]{2,1,0:T(8,128)S(1)} %get-tuple-element.66.bias) | copy-start | bytes 1032196
  62.4 30.6 %copy-start.13 = (bf16[336,100]{1,0:T(8,128)(2,1)}, bf16[336,100]{1,0:T(8,128)(2,1)S(1)}, u32[]{:S(2)}) copy-start(bf16[336,100]{1,0:T(8,128)(2,1)S(1)} %get-tuple-element.63.w_time) | copy-start | bytes 201604
  62.4 30.6 %copy-start.14 = (bf16[336,100]{1,0:T(8,128)(2,1)}, bf16[336,100]{1,0:T(8,128)(2,1)S(1)}, u32[]{:S(2)}) copy-start(bf16[336,100]{1,0:T(8,128)(2,1)S(1)} %get-tuple-element.64.w_hid) | copy-start | bytes 201604
  62.4 30.6 %copy-start.17 = (f32[6,112,128]{2,1,0:T(8,128)}, f32[6,112,128]{2,1,0:T(8,128)S(1)}, u32[]{:S(2)}) copy-start(f32[6,112,128]{2,1,0:T(8,128)S(1)} %get-tuple-element.83.cols) | copy-start | bytes 1032196
  62.4 30.6 %copy-start.19 = (bf16[224,128]{1,0:T(8,128)(2,1)}, bf16[224,128]{1,0:T(8,128)(2,1)S(1)}, u32[]{:S(2)}) copy-start(bf16[224,128]{1,0:T(8,128)(2,1)S(1)} %get-tuple-element.71.kv_h) | copy-start | bytes 172036
  62.4 30.6 %copy-start.29 = (bf16[112,112]{1,0:T(8,128)(2,1)}, bf16[112,112]{1,0:T(8,128)(2,1)S(1)}, u32[]{:S(2)}) copy-start(bf16[112,112]{1,0:T(8,128)(2,1)S(1)} %get-tuple-element.82.dst_n) | copy-start | bytes 75268
  62.5 38.4 %copy-start.10 = (s32[8,1,1024]{2,1,0:T(1,128)}, s32[8,1,1024]{2,1,0:T(1,128)S(1)}, u32[]{:S(2)}) copy-start(s32[8,1,1024]{2,1,0:T(1,128)S(1)} %all-to-all-done) | copy-start | bytes 98308
  93.0 1.3 copy-start.3
  94.3 5.2 %copy-start.44 = (s32[1,1,3,512]{3,1,2,0:T(1,128)S(1)}, s32[1,1,3,512]{3,1,2,0:T(1,128)}, u32[]{:S(2)}) copy-start(s32[1,1,3,512]{3,1,2,0:T(1,128)} %param.30) | copy-start | bytes 18436
  94.3 5.2 %copy-start.46 = (s32[1,1,8]{2,1,0:T(1,128)S(1)}, s32[1,1,8]{2,1,0:T(1,128)}, u32[]{:S(2)}) copy-start(s32[1,1,8]{2,1,0:T(1,128)} %param.29) | copy-start | bytes 100
  94.3 5.6 %copy-start.37 = (s32[1,1,1536,10]{2,1,3,0:T(1,128)S(1)}, s32[1,1,1536,10]{2,1,3,0:T(1,128)}, u32[]{:S(2)}) copy-start(s32[1,1,1536,10]{2,1,3,0:T(1,128)} %param.31) | copy-start | bytes 184324
  94.3 54.3 %all-to-all-start.1 = ((bf16[8,1024,128]{2,1,0:T(8,128)(2,1)}), bf16[8,1024,128]{2,1,0:T(8,128)(2,1)S(1)}, u32[]{:S(2)}, u32[]{:S(2)}) async-start(bf16[8,1024,128]{2,1,0:T(8,128)(2,1)} %bitcast.163), calls=%async_computation.1 | async-start | bytes 4194304 | tf_op jit(solution)/shard_map/all_to_all | solution.py:1071
  100.8 2.2 copy-start
  148.6 1.3 copy-start.34
  273.7 65.2 %all-to-all-start.3 = ((bf16[8,1024,128]{2,1,0:T(8,128)(2,1)}), bf16[8,1024,128]{2,1,0:T(8,128)(2,1)S(1)}, u32[]{:S(2)}, u32[]{:S(2)}) async-start(bf16[8,1024,128]{2,1,0:T(8,128)(2,1)} %bitcast.39), calls=%async_computation.3 | async-start | bytes 4194304 | tf_op jit(solution)/shard_map/all_to_all | solution.py:1071
  277.3 146.1 %all-gather.8.cloned.1.call-start = ((), (), s32[]{:S(2)}) async-start(), calls=%async_computation.5 | async-start | bytes 1769472 | tf_op jit(solution)/shard_map/all_gather | solution.py:1137
  278.0 145.4 %all-gather.6.cloned.1.call-start = ((), (), s32[]{:S(2)}) async-start(), calls=%async_computation.4 | async-start | bytes 2359296 | tf_op jit(solution)/shard_map/all_gather | solution.py:1152
  278.3 40.2 %copy-start.7 = (f32[1448,128]{1,0:T(8,128)S(1)}, f32[1448,128]{1,0:T(8,128)}, u32[]{:S(2)}) copy-start(f32[1448,128]{1,0:T(8,128)} %get-tuple-element.87.att) | copy-start | bytes 2224132
  278.3 40.2 %copy-start.15 = (f32[8,128]{1,0:T(8,128)S(1)}, f32[8,128]{1,0:T(8,128)}, u32[]{:S(2)}) copy-start(f32[8,128]{1,0:T(8,128)} %get-tuple-element.88.losses) | copy-start | bytes 12292
  318.5 1.3 copy-start.6
  319.8 0.7 copy-start.16
  323.3 18.3 %collective-permute-start.5 = (f32[2,2,2,2,1,88,128]{6,5,4,3,2,1,0:T(8,128)}, f32[2,2,2,2,1,88,128]{6,5,4,3,2,1,0:T(8,128)}, u32[]{:S(2)}, u32[]{:S(2)}) collective-permute-start(f32[2,2,2,2,1,88,128]{6,5,4,3,2,1,0:T(8,128)} %constant_dynamic-slice_fusion.5), channel_id=1, source_target_pairs={{0,1},{1,0},{2,3},{3,2},{4,5},{5,4},{6,7},{7,6},{8,9},{9,8},{10,11... | collective-permute-start | bytes 2162696 | tf_op jit(solution)/shard_map/ppermute | solution.py:1019
  342.7 26.2 %copy-start.39 = (s32[1,1,8,1024]{3,2,1,0:T(8,128)S(1)}, s32[1,1,8,1024]{3,2,1,0:T(8,128)}, u32[]{:S(2)}) copy-start(s32[1,1,8,1024]{3,2,1,0:T(8,128)} %param.28) | copy-start | bytes 98308
  342.8 26.2 %copy-start.45 = (s32[1024]{0:T(1024)S(1)}, s32[1024]{0:T(1024)}, u32[]{:S(2)}) copy-start(s32[1024]{0:T(1024)} %get-tuple-element.181) | copy-start | bytes 12292
  342.8 10.0 %collective-permute-start.6 = (f32[1,2,2,2,1,88,128]{6,5,4,3,2,1,0:T(8,128)S(1)}, f32[1,2,2,2,1,88,128]{6,5,4,3,2,1,0:T(8,128)S(1)}, u32[]{:S(2)}, u32[]{:S(2)}) collective-permute-start(f32[1,2,2,2,1,88,128]{6,5,4,3,2,1,0:T(8,128)S(1)} %constant_dynamic-slice_fusion.4), channel_id=1, source_target_pairs={{0,16},{8,24},{16,0},{24,8},{1,17},{9,25},{17,1},{25,9},{2,18},{10... | collective-permute-start | bytes 1081352 | tf_op jit(solution)/shard_map/ppermute | solution.py:1019
  352.9 5.6 %collective-permute-start.7 = (f32[1,1,2,2,1,88,128]{6,5,4,3,2,1,0:T(8,128)S(1)}, f32[1,1,2,2,1,88,128]{6,5,4,3,2,1,0:T(8,128)S(1)}, u32[]{:S(2)}, u32[]{:S(2)}) collective-permute-start(f32[1,1,2,2,1,88,128]{6,5,4,3,2,1,0:T(8,128)S(1)} %constant_dynamic-slice_fusion.3), channel_id=1, source_target_pairs={{0,8},{8,0},{16,24},{24,16},{1,9},{9,1},{17,25},{25,17},{2,10},{10... | collective-permute-start | bytes 540680 | tf_op jit(solution)/shard_map/ppermute | solution.py:1019
  358.5 9.1 %collective-permute-start.8 = (f32[1,1,2,1,1,88,128]{6,5,4,3,2,1,0:T(8,128)S(1)}, f32[1,1,2,1,1,88,128]{6,5,4,3,2,1,0:T(8,128)S(1)}, u32[]{:S(2)}, u32[]{:S(2)}) collective-permute-start(f32[1,1,2,1,1,88,128]{6,5,4,3,2,1,0:T(8,128)S(1)} %constant_dynamic-slice_fusion.2), channel_id=1, source_target_pairs={{0,2},{1,3},{2,0},{3,1},{4,6},{5,7},{6,4},{7,5},{8,10},{9,11},{10,... | collective-permute-start | bytes 270344 | tf_op jit(solution)/shard_map/ppermute | solution.py:1019
  368.3 6.9 %collective-permute-start.9 = (f32[1,1,1,1,1,88,128]{6,5,4,3,2,1,0:T(8,128)}, f32[1,1,1,1,1,88,128]{6,5,4,3,2,1,0:T(8,128)}, u32[]{:S(2)}, u32[]{:S(2)}) collective-permute-start(f32[1,1,1,1,1,88,128]{6,5,4,3,2,1,0:T(8,128)} %constant_dynamic-slice_fusion.1), channel_id=1, source_target_pairs={{0,4},{1,5},{2,6},{3,7},{4,0},{5,1},{6,2},{7,3},{8,12},{9,13},{10,... | collective-permute-start | bytes 135176 | tf_op jit(solution)/shard_map/ppermute | solution.py:1019
  369.0 42.0 %copy-start.33 = (f32[100,8192]{1,0:T(8,128)S(1)}, f32[100,8192]{1,0:T(8,128)}, u32[]{:S(2)}) copy-start(f32[100,8192]{1,0:T(8,128)} %get-tuple-element.89) | copy-start | bytes 9830404
  378.6 1.2 collective-permute-start.10
  382.0 16.8 %collective-permute-start.11 = (f32[8,128]{1,0:T(8,128)S(1)}, f32[8,128]{1,0:T(8,128)S(1)}, u32[]{:S(2)}, u32[]{:S(2)}) collective-permute-start(f32[8,128]{1,0:T(8,128)S(1)} %add.166), channel_id=1, source_target_pairs={{0,2},{1,3},{2,0},{3,1},{4,6},{5,7},{6,4},{7,5},{8,10},{9,11},{10,... | collective-permute-start | bytes 12296 | tf_op jit(solution)/shard_map/ppermute | solution.py:1019
  398.7 6.4 %copy-start.36 = (s32[1,8,21,128]{3,1,2,0:T(8,128)}, s32[1,8,21,128]{3,1,2,0:T(8,128)S(1)}, u32[]{:S(2)}) copy-start(s32[1,8,21,128]{3,1,2,0:T(8,128)S(1)} %copy.62) | copy-start | bytes 258052
  398.8 4.6 %collective-permute-start.12 = (f32[8,128]{1,0:T(8,128)S(1)}, f32[8,128]{1,0:T(8,128)S(1)}, u32[]{:S(2)}, u32[]{:S(2)}) collective-permute-start(f32[8,128]{1,0:T(8,128)S(1)} %add.167), channel_id=1, source_target_pairs={{0,4},{1,5},{2,6},{3,7},{4,0},{5,1},{6,2},{7,3},{8,12},{9,13},{10,... | collective-permute-start | bytes 12296 | tf_op jit(solution)/shard_map/ppermute | solution.py:1019
  403.4 3.6 collective-permute-start.13
  407.0 14.3 %collective-permute-start.14 = (f32[8,128]{1,0:T(8,128)S(1)}, f32[8,128]{1,0:T(8,128)S(1)}, u32[]{:S(2)}, u32[]{:S(2)}) collective-permute-start(f32[8,128]{1,0:T(8,128)S(1)} %add.169), channel_id=1, source_target_pairs={{0,16},{8,24},{16,0},{24,8},{1,17},{9,25},{17,1},{25,9},{2,18},{10... | collective-permute-start | bytes 12296 | tf_op jit(solution)/shard_map/ppermute | solution.py:1019
  411.0 5.1 %copy-start.32 = (f32[100,8192]{1,0:T(8,128)S(1)}, f32[100,8192]{1,0:T(8,128)}, u32[]{:S(2)}) copy-start(f32[100,8192]{1,0:T(8,128)} %get-tuple-element.96) | copy-start | bytes 9830404
  416.2 6.5 %copy-start.35 = (f32[11264]{0:T(1024)S(1)}, f32[11264]{0:T(1024)}, u32[]{:S(2)}) copy-start(f32[11264]{0:T(1024)} %param.20) | copy-start | bytes 135172
  416.2 6.5 %copy-start.41 = (f32[11264]{0:T(1024)S(1)}, f32[11264]{0:T(1024)}, u32[]{:S(2)}) copy-start(f32[11264]{0:T(1024)} %param.21) | copy-start | bytes 135172
  416.2 6.5 %copy-start.42 = (f32[11264]{0:T(1024)S(1)}, f32[11264]{0:T(1024)}, u32[]{:S(2)}) copy-start(f32[11264]{0:T(1024)} %param.22) | copy-start | bytes 135172
  416.2 7.2 %copy-start.4 = (bf16[100,8192]{1,0:T(8,128)(2,1)S(1)}, bf16[100,8192]{1,0:T(8,128)(2,1)}, u32[]{:S(2)}) copy-start(bf16[100,8192]{1,0:T(8,128)(2,1)} %copy-done.3) | copy-start | bytes 4915204
  416.2 7.2 %copy-start.12 = (s32[1,8192]{1,0:T(1,128)S(1)}, s32[1,8192]{1,0:T(1,128)}, u32[]{:S(2)}) copy-start(s32[1,8192]{1,0:T(1,128)} %mail_time.3) | copy-start | bytes 98308
  423.4 1.6 copy-start.1
  425.0 1.4 copy-start.5
  (3 other events, 1.8 us)
Sparse Core Ops, SparseCore 0:
  279.8 50.8 all-gather.7
  341.7 29.4 all-gather.5

commit v2 on v1

--- a/solution.py
+++ b/solution.py
@@ -31,12 +31,13 @@
 LANES = 128
 PAD = 112
 HALF = 56
+WIRE = 104
 GATES = 3 * PAD
 KV = 4 * HALF
 EB = 128
 SECT = 3 * EB
 STREAMS = 8
-VMEM_LIMIT = 60 * 2**20
+VMEM_LIMIT = 63_000_000
 
 ROW_HH = 1458
 ROW_NF = 1758
@@ -140,38 +141,31 @@
     return jnp.where(lane < 50, x, jnp.where(lane < 100, roll_left(x, 6), 0.0))
 
 
-def codes_kernel(dt, delta, freq, phi_n, phi_m):
+def codes_kernel(delta, freq, out):
     freqs = freq[...]
-    for k in range(NBR):
+    for k in range(out.shape[0]):
 
         def one(i, carry, k=k):
             at = pl.ds(pl.multiple_of(i * LANES, LANES), LANES)
-            phi_n[k, :, at] = cosine(dt[k : k + 1, at].astype(F32) * freqs).astype(BF16)
+            out[k, :, at] = cosine(delta[k : k + 1, at].astype(F32) * freqs).astype(BF16)
             return carry
 
-        lax.fori_loop(0, dt.shape[1] // LANES, one, 0)
-
-    def other(i, carry):
-        at = pl.ds(pl.multiple_of(i * LANES, LANES), LANES)
-        phi_m[:, at] = cosine(delta[:, at].astype(F32) * freqs).astype(BF16)
-        return carry
-
-    lax.fori_loop(0, delta.shape[1] // LANES, other, 0)
-
-
-def time_codes(dt, delta):
+        lax.fori_loop(0, delta.shape[1] // LANES, one, 0)
+
+
+def time_codes(delta):
     freq = jnp.asarray(np.tile(FREQS[:, None], (1, LANES)))
+    rows, count = delta.shape
     return pl.pallas_call(
         codes_kernel,
-        out_shape=(
-            jax.ShapeDtypeStruct((NBR, TENC, dt.shape[1]), BF16),
-            jax.ShapeDtypeStruct((TENC, delta.shape[1]), BF16),
+        out_shape=jax.ShapeDtypeStruct((rows, TENC, count), BF16),
+        in_specs=[VMEM] * 2,
+        out_specs=VMEM,
+        compiler_params=params_of(16 * 2**20),
+        cost_estimate=pl.CostEstimate(
+            flops=rows * count * 3000, bytes_accessed=rows * count * 200, transcendentals=0
         ),
-        in_specs=[VMEM] * 3,
-        out_specs=(VMEM, VMEM),
-        compiler_params=params_of(24 * 2**20),
-        cost_estimate=pl.CostEstimate(flops=60_000_000, bytes_accessed=5_000_000, transcendentals=0),
-    )(dt, delta, freq)
+    )(delta, freq)
 
 
 def weights_kernel(
@@ -288,7 +282,7 @@
         in_specs=[VMEM],
         out_specs=[VMEM] * len(shapes),
         scratch_shapes=[pltpu.VMEM((FLAT_ROWS + 16, LANES), F32), pltpu.VMEM((WROWS + 512, LANES), F32)],
-        compiler_params=params_of(24 * 2**20),
+        compiler_params=params_of(),
         cost_estimate=pl.CostEstimate(flops=4_000_000, bytes_accessed=2_000_000, transcendentals=0),
     )(flat)
 
@@ -306,140 +300,283 @@
     lax.fori_loop(0, count // group, step, 0)
 
 
-def gru_products(mail, phi, feat, w_mail, w_time, w_hid, w_feat, low, gi, gh, nf):
+def gather_turned(index, table, out):
+    slots = out.shape[2]
+    pieces = slots // LANES
+
+    def step(j, carry):
+        owner = j // pieces
+        at = pl.ds(pl.multiple_of((j - owner * pieces) * LANES, LANES), LANES)
+        groups = []
+        for g in range(LANES // 8):
+            picked = [table[pl.ds(index[j * LANES + g * 8 + u], 1), :] for u in range(8)]
+            groups.append(jnp.concatenate(picked, 0))
+        out[owner, 0:WIRE, at] = jnp.concatenate(groups, 0).T[:WIRE].astype(BF16)
+        return carry
+
+    lax.fori_loop(0, out.shape[0] * pieces, step, 0, unroll=2)
+
+
+def turn_into(got, table):
+    slots = got.shape[2]
+    pieces = slots // LANES
+    short = jnp.zeros((LANES - WIRE, LANES), F32)
+
+    def step(j, carry):
+        owner = j // pieces
+        at = pl.ds(pl.multiple_of((j - owner * pieces) * LANES, LANES), LANES)
+        block = jnp.concatenate([got[owner, 0:WIRE, at].astype(F32), short], 0)
+        table[pl.ds(pl.multiple_of(j * LANES, LANES), LANES), :] = block.T
+        return carry
+
+    lax.fori_loop(0, got.shape[0] * pieces, step, 0, unroll=8)
+
+
+def to_rows(block):
+    full = jnp.concatenate([block, jnp.zeros((LANES - PAD, LANES), F32)], 0)
+    return full.T
+
+
+def mem_piece(mem, i):
+    return mem.reshape(MEM * 8, LANES)[pl.ds(i, MEM, stride=8), :]
+
+
+def gru_products(mail, phi, low, w_mail, w_time, w_hid, gi, gh):
     gi[...] = dot(w_mail[...], mail[...]) + dot(w_time[...], phi[...])
-    gh[...] = dot(w_hid[...], low)
-    if nf is not None:
-        nf[...] = dot(w_feat[...], feat[...])
-
-
-def gates_at(at, gi, gh, bias, kept):
+    gh[...] = dot(w_hid[...], low[...])
+
+
+def gates_at(at, gi, gh, bias, low):
     gr, gz, gn = (gi[PAD * g : PAD * g + PAD, at] + bias[0, PAD * g : PAD * g + PAD, :] for g in range(3))
     hr, hz, hn = (gh[PAD * g : PAD * g + PAD, at] + bias[1, PAD * g : PAD * g + PAD, :] for g in range(3))
     r = sigmoid(gr + hr)
     z = sigmoid(gz + hz)
     n = jnp.tanh(gn + r * hn)
-    s = kept[:, at]
+    s = jnp.concatenate([low[:, at].astype(F32), jnp.zeros((PAD - MEM, LANES), F32)], 0)
     return r, z, n, hn, s, (1.0 - z) * n + z * s
 
 
-def to_rows(block):
-    full = jnp.concatenate([block, jnp.zeros((LANES - PAD, LANES), F32)], 0)
-    return full.T
-
-
-def load_memory(mem, kept):
-    low = mem[...].astype(BF16)
-    kept[0:MEM, :] = low.astype(F32)
-    kept[MEM:, :] = jnp.zeros((PAD - MEM, kept.shape[1]), F32)
-    return low
-
-
 def gru_kernel(
-    index, mail, phi, mem, feat, w_mail, w_time, w_hid, w_feat, bias, sent, s_rows, s_cols, table, kept, gi, gh, nf
+    index, mail, phi, mem, feat, w_mail, w_time, w_hid, w_feat, bias, sent, s_rows, low, table, gi, gh, nf
 ):
     block = mail.shape[1]
     step = pl.program_id(0)
-    low = load_memory(mem, kept)
-    gru_products(mail, phi, feat, w_mail, w_time, w_hid, w_feat, low, gi, gh, nf)
+    for i in range(block // LANES):
+        low[:, i * LANES : i * LANES + LANES] = mem_piece(mem, i).astype(BF16)
+    gru_products(mail, phi, low, w_mail, w_time, w_hid, gi, gh)
+    nf[...] = dot(w_feat[...], feat[...])
 
     def piece(i, carry):
         start = pl.multiple_of(i * LANES, LANES)
         at = pl.ds(start, LANES)
-        _, _, _, _, _, renewed = gates_at(at, gi, gh, bias, kept)
+        _, _, _, _, _, renewed = gates_at(at, gi, gh, bias, low)
         hidden = (renewed + nf[:, at]).astype(BF16).astype(F32)
         table[pl.ds(pl.multiple_of(step * block + start, LANES), LANES), :] = to_rows(hidden)
         s_rows[at, :] = to_rows(renewed)
-        s_cols[:, at] = renewed[:MEM].astype(BF16)
         return carry
 
     lax.fori_loop(0, block // LANES, piece, 0)
 
     @pl.when(step == pl.num_programs(0) - 1)
     def _():
-        gather_loop(index, table, sent, sent.shape[0])
-
-
-def gru_specs(block):
-    def cols(rows):
-        return pl.BlockSpec((rows, block), lambda i: (0, i))
-
-    return [cols(MAIL), cols(TENC), cols(MEM), cols(NFEAT)]
-
-
-def gru_forward(index, mail, phi, mem, feat, wts, count):
+        gather_turned(index, table, sent)
+
+
+BLOCK = 1024
+
+
+def cols_spec(rows):
+    return pl.BlockSpec((rows, BLOCK), lambda i: (0, i))
+
+
+def mem_spec():
+    return pl.BlockSpec((MEM, BLOCK // LANES, LANES), lambda i: (0, i, 0))
+
+
+def gru_forward(index, mail, phi, mem, feat, wts, shards, slots):
     rows = mail.shape[1]
-    block = 1024
     return pl.pallas_call(
         gru_kernel,
-        grid=(rows // block,),
+        grid=(rows // BLOCK,),
         out_shape=(
-            jax.ShapeDtypeStruct((count, LANES), BF16),
+            jax.ShapeDtypeStruct((shards, WIRE, slots), BF16),
             jax.ShapeDtypeStruct((rows, LANES), F32),
             jax.ShapeDtypeStruct((MEM, rows), BF16),
         ),
-        in_specs=[SMEM] + gru_specs(block) + [VMEM] * 5,
-        out_specs=(
-            VMEM,
-            pl.BlockSpec((block, LANES), lambda i: (i, 0)),
-            pl.BlockSpec((MEM, block), lambda i: (0, i)),
-        ),
+        in_specs=[SMEM, cols_spec(MAIL), cols_spec(TENC), mem_spec(), cols_spec(NFEAT)] + [VMEM] * 5,
+        out_specs=(VMEM, pl.BlockSpec((BLOCK, LANES), lambda i: (i, 0)), cols_spec(MEM)),
         scratch_shapes=[
             pltpu.VMEM((rows, LANES), F32),
-            pltpu.VMEM((PAD, block), F32),
-            pltpu.VMEM((GATES, block), F32),
-            pltpu.VMEM((GATES, block), F32),
-            pltpu.VMEM((PAD, block), F32),
+            pltpu.VMEM((GATES, BLOCK), F32),
+            pltpu.VMEM((GATES, BLOCK), F32),
+            pltpu.VMEM((PAD, BLOCK), F32),
         ],
-        compiler_params=params_of(48 * 2**20),
+        compiler_params=params_of(),
         cost_estimate=pl.CostEstimate(flops=4_000_000_000, bytes_accessed=24_000_000, transcendentals=3_000_000),
     )(index, mail, phi, mem, feat, *wts[:5])
 
 
-def gather_kernel(index, table, out, wide):
-    if table.dtype != F32:
-        wide[...] = table[...].astype(F32)
-        table = wide
-    gather_loop(index, table, out, out.shape[0])
-
-
-def gather_rows(table, index):
+def send_kernel(index, table, notes, out):
+    for owner in range(out.shape[0]):
+        out[owner, WIRE:, :] = notes[...]
+    gather_turned(index, table, out)
+
+
+def send_rows(table, index, notes, shards, slots):
     return pl.pallas_call(
-        gather_kernel,
+        send_kernel,
+        out_shape=jax.ShapeDtypeStruct((shards, WIRE + notes.shape[0], slots), BF16),
+        in_specs=[SMEM, VMEM, VMEM],
+        out_specs=VMEM,
+        compiler_params=params_of(24 * 2**20),
+        cost_estimate=pl.CostEstimate(flops=8_000_000, bytes_accessed=6_000_000, transcendentals=0),
+    )(index, table, notes)
+
+
+def partner_kernel(index, got, out, table):
+    turn_into(got, table)
+    gather_loop(index, table, out, index.shape[0])
+
+
+def partner_rows(got, index):
+    return pl.pallas_call(
+        partner_kernel,
         out_shape=jax.ShapeDtypeStruct((index.shape[0], LANES), BF16),
         in_specs=[SMEM, VMEM],
         out_specs=VMEM,
-        scratch_shapes=[pltpu.VMEM(table.shape if table.dtype != F32 else (8, LANES), F32)],
+        scratch_shapes=[pltpu.VMEM((got.shape[0] * got.shape[2], LANES), F32)],
         compiler_params=params_of(24 * 2**20),
-        cost_estimate=pl.CostEstimate(
-            flops=index.shape[0] * 1000, bytes_accessed=6_000_000, transcendentals=0
-        ),
-    )(index, table)
-
-
-def gru_back_kernel(
+        cost_estimate=pl.CostEstimate(flops=2_000_000, bytes_accessed=2_000_000, transcendentals=0),
+    )(index, got)
+
+
+def book_kernel(ordered, ends, wanted, row, partner, event):
+    count = ordered.shape[0]
+
+    def step(i, carry):
+        for u in range(8):
+            at = i * 8 + u
+            key = ordered[at]
+            end = jnp.bitwise_and(key, count - 1)
+            row[at] = wanted[lax.shift_right_logical(key, count.bit_length() - 1)]
+            partner[at] = ends[jnp.bitwise_xor(end, count // 2)]
+            event[at] = jnp.bitwise_and(end, count // 2 - 1)
+        return carry
+
+    lax.fori_loop(0, count // 8, step, 0)
+
+
+def bookkeeping(ordered, ends, wanted):
+    shape = jax.ShapeDtypeStruct(ordered.shape, jnp.int32)
+    return pl.pallas_call(
+        book_kernel,
+        out_shape=(shape, shape, shape),
+        in_specs=[SMEM] * 3,
+        out_specs=(SMEM,) * 3,
+        compiler_params=params_of(),
+        cost_estimate=pl.CostEstimate(flops=4_000_000, bytes_accessed=60_000, transcendentals=0),
+    )(ordered, ends, wanted)
+
+
+def factor_kernel(
     index,
-    got,
+    flags,
     mail,
     phi,
+    low,
     mem,
-    feat,
     mail_time,
     update_time,
     w_mail,
     w_time,
     w_hid,
     bias,
+    factors,
+    s_cols,
     mem_new,
+    time_new,
+    placed,
+    gi,
+    gh,
+):
+    step = pl.program_id(0)
+
+    @pl.when(step == 0)
+    def _():
+        count = index.shape[0]
+        if count != placed.shape[0]:
+            placed[...] = jnp.zeros_like(placed)
+        group = 32
+
+        def move(i, carry):
+            for u in range(group):
+                at = i * group + u
+                placed[pl.ds(index[at], 1), :] = jnp.full((1, LANES), flags[at], jnp.int32)
+            return carry
+
+        lax.fori_loop(0, count // group, move, 0)
+
+    gru_products(mail, phi, low, w_mail, w_time, w_hid, gi, gh)
+    for i in range(BLOCK // LANES):
+        at = slice(i * LANES, i * LANES + LANES)
+        r, z, n, hn, s, renewed = gates_at(at, gi, gh, bias, low)
+        live = placed[pl.ds(pl.multiple_of(step * BLOCK + i * LANES, LANES), LANES), :].T[0:1, :] > 0
+        an = (1.0 - z) * (1.0 - n * n)
+        factors[0, :, at] = (an * hn * (r * (1.0 - r)))[:MEM]
+        factors[1, :, at] = ((s - n) * (z * (1.0 - z)))[:MEM]
+        factors[2, :, at] = an[:MEM]
+        factors[3, :, at] = r[:MEM]
+        factors[4, :, at] = z[:MEM]
+        s_cols[:, at] = renewed[:MEM].astype(BF16)
+        value = jnp.where(live, renewed[:MEM], mem_piece(mem, i))
+        mem_new.reshape(MEM * 8, LANES)[pl.ds(i, MEM, stride=8), :] = value
+        time_new[:, at] = jnp.where(live, mail_time[:, at], update_time[:, at])
+
+
+def gru_factors(index, flags, mail, phi, low, mem, mail_time, update_time, wts):
+    rows = mail.shape[1]
+    return pl.pallas_call(
+        factor_kernel,
+        grid=(rows // BLOCK,),
+        out_shape=(
+            jax.ShapeDtypeStruct((5, MEM, rows), F32),
+            jax.ShapeDtypeStruct((MEM, rows), BF16),
+            jax.ShapeDtypeStruct((MEM, rows // LANES, LANES), F32),
+            jax.ShapeDtypeStruct((1, rows), jnp.int32),
+        ),
+        in_specs=[SMEM, SMEM, cols_spec(MAIL), cols_spec(TENC), cols_spec(MEM), mem_spec()]
+        + [cols_spec(1)] * 2
+        + [VMEM] * 4,
+        out_specs=(
+            pl.BlockSpec((5, MEM, BLOCK), lambda i: (0, 0, i)),
+            cols_spec(MEM),
+            mem_spec(),
+            cols_spec(1),
+        ),
+        scratch_shapes=[
+            pltpu.VMEM((rows, LANES), jnp.int32),
+            pltpu.VMEM((GATES, BLOCK), F32),
+            pltpu.VMEM((GATES, BLOCK), F32),
+        ],
+        compiler_params=params_of(),
+        cost_estimate=pl.CostEstimate(flops=3_000_000_000, bytes_accessed=34_000_000, transcendentals=3_000_000),
+    )(index, flags, mail, phi, low, mem, mail_time, update_time, wts[0], wts[1], wts[2], wts[4])
+
+
+def gru_back_kernel(
+    index,
+    got,
+    factors,
+    mail,
+    phi,
+    low,
+    feat,
+    w_hid,
     mem_grad,
-    time_new,
     grads,
     biases,
     wide,
     placed,
-    kept,
-    gi,
-    gh,
     d_in,
     d_hid,
     d_low,
@@ -451,13 +588,13 @@
     a_bin,
     a_bhid,
 ):
-    block = mail.shape[1]
     step = pl.program_id(0)
 
     @pl.when(step == 0)
     def _():
-        wide[...] = got[...].astype(F32)
-        if got.shape[0] != placed.shape[0]:
+        turn_into(got, wide)
+        count = wide.shape[0]
+        if count != placed.shape[0]:
             placed[...] = jnp.zeros_like(placed)
         group = 32
 
@@ -467,49 +604,39 @@
                 placed[pl.ds(index[at], 1), :] = wide[pl.ds(at, 1), :]
             return carry
 
-        lax.fori_loop(0, got.shape[0] // group, move, 0)
-        for ref in (a_mail, a_time, a_hid, a_feat, a_bin, a_bhid):
+        lax.fori_loop(0, count // group, move, 0)
+        for ref in (d_in, d_hid, d_low, a_mail, a_time, a_hid, a_feat, a_bin, a_bhid):
             ref[...] = jnp.zeros_like(ref)
 
-    low = load_memory(mem, kept)
-    gru_products(mail, phi, None, w_mail, w_time, w_hid, None, low, gi, gh, None)
-    real = row_of((PAD, LANES)) < MEM
-
-    def piece(i, carry):
-        start = pl.multiple_of(i * LANES, LANES)
-        at = pl.ds(start, LANES)
-        r, z, n, hn, s, renewed = gates_at(at, gi, gh, bias, kept)
-        turned = placed[pl.ds(pl.multiple_of(step * block + start, LANES), LANES), :].T
-        live = turned[MEM : MEM + 1, :] > 0.5
-        d = jnp.where(real, turned[:PAD], 0.0)
-        d_low[:, at] = d.astype(BF16)
-        dn = d * (1.0 - z) * (1.0 - n * n)
-        dr = dn * hn * r * (1.0 - r)
-        dz = d * (s - n) * z * (1.0 - z)
-        dhn = dn * r
-        direct[:, at] = d * z
+    for i in range(BLOCK // LANES):
+        at = slice(i * LANES, i * LANES + LANES)
+        d = placed[pl.ds(pl.multiple_of(step * BLOCK + i * LANES, LANES), LANES), :].T[:MEM]
+        dr = d * factors[0, :, at]
+        dz = d * factors[1, :, at]
+        dn = d * factors[2, :, at]
+        dhn = dn * factors[3, :, at]
+        direct[:, at] = d * factors[4, :, at]
         low_r, low_z = dr.astype(BF16), dz.astype(BF16)
-        d_in[0:PAD, at] = low_r
-        d_in[PAD : 2 * PAD, at] = low_z
-        d_in[2 * PAD : 3 * PAD, at] = dn.astype(BF16)
-        d_hid[0:PAD, at] = low_r
-        d_hid[PAD : 2 * PAD, at] = low_z
-        d_hid[2 * PAD : 3 * PAD, at] = dhn.astype(BF16)
-        a_bin[0:PAD, :] += dr
-        a_bin[PAD : 2 * PAD, :] += dz
-        a_bin[2 * PAD : 3 * PAD, :] += dn
-        a_bhid[...] += dhn
-        mem_new[:, at] = jnp.where(live, renewed[:MEM], mem[:, at])
-        time_new[:, at] = jnp.where(live, mail_time[:, at], update_time[:, at])
-        return carry
-
-    lax.fori_loop(0, block // LANES, piece, 0)
+        d_low[0:MEM, at] = d.astype(BF16)
+        d_in[0:MEM, at] = low_r
+        d_in[PAD : PAD + MEM, at] = low_z
+        d_in[2 * PAD : 2 * PAD + MEM, at] = dn.astype(BF16)
+        d_hid[0:MEM, at] = low_r
+        d_hid[PAD : PAD + MEM, at] = low_z
+        d_hid[2 * PAD : 2 * PAD + MEM, at] = dhn.astype(BF16)
+        a_bin[0:MEM, :] += dr
+        a_bin[PAD : PAD + MEM, :] += dz
+        a_bin[2 * PAD : 2 * PAD + MEM, :] += dn
+        a_bhid[0:MEM, :] += dhn
     din, dhid = d_in[...], d_hid[...]
     a_mail[:, :MAIL] += dot(din, mail[...], 1, 1)
     a_time[:, :TENC] += dot(din, phi[...], 1, 1)
-    a_hid[:, :MEM] += dot(dhid, low, 1, 1)
+    a_hid[:, :MEM] += dot(dhid, low[...], 1, 1)
     a_feat[:, :NFEAT] += dot(d_low[...], feat[...], 1, 1)
-    mem_grad[...] = direct[0:MEM, :] + dot(w_hid[...], dhid, 0, 0)
+    direct[...] += dot(w_hid[...], dhid, 0, 0)
+    for i in range(BLOCK // LANES):
+        at = slice(i * LANES, i * LANES + LANES)
+        mem_grad.reshape(MEM * 8, LANES)[pl.ds(i, MEM, stride=8), :] = direct[:, at]
 
     @pl.when(step == pl.num_programs(0) - 1)
     def _():
@@ -529,33 +656,27 @@
         biases[...] = jnp.concatenate(sums + [jnp.zeros((2, LANES), F32)], 0)
 
 
-def gru_backward(index, got, mail, phi, mem, feat, mail_time, update_time, wts):
+def gru_backward(index, got, factors, mail, phi, low, feat, wts):
     rows = mail.shape[1]
-    block = 1024
-    one = pl.BlockSpec((1, block), lambda i: (0, i))
-    hundred = pl.BlockSpec((MEM, block), lambda i: (0, i))
     return pl.pallas_call(
         gru_back_kernel,
-        grid=(rows // block,),
+        grid=(rows // BLOCK,),
         out_shape=(
-            jax.ShapeDtypeStruct((MEM, rows), F32),
-            jax.ShapeDtypeStruct((MEM, rows), F32),
-            jax.ShapeDtypeStruct((1, rows), jnp.int32),
+            jax.ShapeDtypeStruct((MEM, rows // LANES, LANES), F32),
             jax.ShapeDtypeStruct((GRU_ROWS, LANES), F32),
             jax.ShapeDtypeStruct((8, LANES), F32),
         ),
-        in_specs=[SMEM, VMEM] + gru_specs(block) + [one, one] + [VMEM] * 4,
-        out_specs=(hundred, hundred, one, VMEM, VMEM),
+        in_specs=[SMEM, VMEM, pl.BlockSpec((5, MEM, BLOCK), lambda i: (0, 0, i))]
+        + [cols_spec(r) for r in (MAIL, TENC, MEM, NFEAT)]
+        + [VMEM],
+        out_specs=(mem_spec(), VMEM, VMEM),
         scratch_shapes=[
-            pltpu.VMEM(got.shape, F32),
+            pltpu.VMEM((got.shape[0] * got.shape[2], LANES), F32),
             pltpu.VMEM((rows, LANES), F32),
-            pltpu.VMEM((PAD, block), F32),
-            pltpu.VMEM((GATES, block), F32),
-            pltpu.VMEM((GATES, block), F32),
-            pltpu.VMEM((GATES, block), BF16),
-            pltpu.VMEM((GATES, block), BF16),
-            pltpu.VMEM((PAD, block), BF16),
-            pltpu.VMEM((PAD, block), F32),
+            pltpu.VMEM((GATES, BLOCK), BF16),
+            pltpu.VMEM((GATES, BLOCK), BF16),
+            pltpu.VMEM((PAD, BLOCK), BF16),
+            pltpu.VMEM((MEM, BLOCK), F32),
             pltpu.VMEM((GATES, 512), F32),
             pltpu.VMEM((GATES, LANES), F32),
             pltpu.VMEM((GATES, LANES), F32),
@@ -564,13 +685,12 @@
             pltpu.VMEM((PAD, LANES), F32),
         ],
         compiler_params=params_of(),
-        cost_estimate=pl.CostEstimate(flops=7_000_000_000, bytes_accessed=28_000_000, transcendentals=3_000_000),
-    )(index, got, mail, phi, mem, feat, mail_time, update_time, wts[0], wts[1], wts[2], wts[4])
+        cost_estimate=pl.CostEstimate(flops=5_000_000_000, bytes_accessed=36_000_000, transcendentals=0),
+    )(index, got, factors, mail, phi, low, feat, wts[2])
 
 
 def attention_kernel(
     index,
-    counts,
     got,
     e0,
     e1,
@@ -596,9 +716,9 @@
     grads,
     losses,
     table,
-    picked,
     kv,
     d_rows,
+    d_two,
     a_kvh,
     a_kve,
     a_kvt,
@@ -610,8 +730,9 @@
     a_dst,
     a_col,
     a_one,
-    *lanes,
+    *rest,
 ):
+    lanes, picks = rest[:STREAMS], rest[STREAMS:]
     step = pl.program_id(0)
     near = NBR * SECT
     total = near + SECT
@@ -620,12 +741,14 @@
 
     @pl.when(step == 0)
     def _():
-        table[...] = got[...].astype(F32)
+        turn_into(got, table)
         for ref in sums + lanes:
             ref[...] = jnp.zeros_like(ref)
 
-    gather_loop(index, table, picked, total, step * total)
-    roots = picked[near:total, :]
+    at_block = step * total
+    gather_loop(index, table, picks[NBR], SECT, at_block + near)
+    gather_loop(index, table, picks[0], SECT, at_block)
+    roots = picks[NBR][...]
 
     def edge_of(k):
         return jnp.concatenate([e0[k], e1[k], e2[k]], 1)
@@ -635,10 +758,15 @@
 
     for k in range(NBR):
         kv[k] = (
-            dot(kv_h[...], picked[k * SECT : k * SECT + SECT, :], 1, 1)
+            dot(kv_h[...], picks[k][...], 1, 1)
             + dot(kv_e[...], edge_of(k))
             + dot(kv_t[...], code_of(k))
         )
+        if k + 1 < NBR:
+            for g in range(SECT // 16):
+                first = (k + 1) * SECT + g * 16
+                rows = [table[pl.ds(index[at_block + first + u], 1), :] for u in range(16)]
+                picks[k + 1][g * 16 : g * 16 + 16, :] = jnp.concatenate(rows, 0).astype(BF16)
     query = dot(q_h[...], roots, 1, 1)
     o_root = dot(o_h[...], roots, 1, 1)
     bo, gain, shift, bpred, wout = (cols[i] for i in range(5))
@@ -748,46 +876,41 @@
     d_q_all = jnp.concatenate(d_queries, 1).astype(BF16)
     a_oh[...] += dot(d_out_all, roots)
     a_qh[...] += dot(d_q_all, roots)
-    d_rows[near:total, :] = dot(d_out_all, o_h[...], 0, 0) + dot(d_q_all, q_h[...], 0, 0)
+    d_rows[...] = dot(d_out_all, o_h[...], 0, 0) + dot(d_q_all, q_h[...], 0, 0)
+    base = step * total
+    each = SECT // STREAMS
+
+    def add_rows(first, ref):
+        for u in range(each):
+            for s in range(STREAMS):
+                at = s * each + u
+                to = pl.ds(index[first + at], 1)
+                lanes[s][to, :] += ref[at : at + 1, :]
+
     for k in range(NBR):
-        at = slice(k * SECT, k * SECT + SECT)
+        mine, other = (d_two, d_rows) if k % 2 == 0 else (d_rows, d_two)
         d_kv = kv[k].astype(BF16)
-        a_kvh[...] += dot(d_kv, picked[at, :])
+        a_kvh[...] += dot(d_kv, picks[k][...])
         a_kve[:, :EDGE] += dot(d_kv, edge_of(k), 1, 1)
         a_kvt[:, :TENC] += dot(d_kv, code_of(k), 1, 1)
-        d_rows[at, :] = dot(d_kv, kv_h[...], 0, 0)
-
-    per = total // STREAMS
-    base = step * total
-
-    def add_rows(i, carry):
-        for u in range(4):
-            for s in range(STREAMS):
-                at = s * per + i * 4 + u
-                to = pl.ds(index[base + at], 1)
-                lanes[s][to, :] += d_rows[pl.ds(at, 1), :]
-        return carry
-
-    lax.fori_loop(0, per // 4, add_rows, 0)
+        mine[...] = dot(d_kv, kv_h[...], 0, 0)
+        add_rows(base + (NBR if k == 0 else k - 1) * SECT, other)
+    add_rows(base + (NBR - 1) * SECT, d_rows)
 
     @pl.when(step == pl.num_programs(0) - 1)
     def _():
-        owners = counts.shape[0]
-        slots = sent.shape[0] // owners
-        piece = min(slots, LANES)
-
-        def finish(i, carry):
-            start = pl.multiple_of(i * piece, piece)
-            at = pl.ds(start, piece)
+        slots = sent.shape[2]
+        pieces = slots // LANES
+
+        def finish(j, carry):
+            owner = j // pieces
+            to = pl.ds(pl.multiple_of((j - owner * pieces) * LANES, LANES), LANES)
+            at = pl.ds(pl.multiple_of(j * LANES, LANES), LANES)
             whole = functools.reduce(jnp.add, [ref[at, :] for ref in lanes])
-            owner = start // slots
-            slot = start - owner * slots + row_of((piece, LANES))
-            lane = lane_of((piece, LANES))
-            live = jnp.where((lane == MEM) & (slot < counts[owner]), 1.0, 0.0)
-            sent[at, :] = jnp.where(lane < MEM, whole, live).astype(BF16)
+            sent[owner, :, to] = jnp.where(lane_of((LANES, LANES)) < MEM, whole, 0.0).T[:WIRE].astype(BF16)
             return carry
 
-        lax.fori_loop(0, sent.shape[0] // piece, finish, 0)
+        lax.fori_loop(0, sent.shape[0] * pieces, finish, 0, unroll=4)
         base_row = ATT_BASE
 
         def turned(block):
@@ -826,24 +949,24 @@
         losses[...] = jnp.broadcast_to(jnp.sum(a_one[...], 1, keepdims=True), (8, LANES))
 
 
-def attention(index, counts, got, edges, codes, weight, wts):
+def attention(index, got, edges, codes, weight, wts):
     roots = edges.shape[2]
     blocks = roots // SECT
 
     def section(rows, t):
         return pl.BlockSpec((NBR, rows, EB), lambda b: (0, 0, t * blocks + b))
 
-    slots = got.shape[0]
+    slots = got.shape[0] * got.shape[2]
     total = (NBR + 1) * SECT
     return pl.pallas_call(
         attention_kernel,
         grid=(blocks,),
         out_shape=(
-            jax.ShapeDtypeStruct((slots, LANES), BF16),
+            jax.ShapeDtypeStruct(got.shape, BF16),
             jax.ShapeDtypeStruct((ATT_ROWS, LANES), F32),
             jax.ShapeDtypeStruct((8, LANES), F32),
         ),
-        in_specs=[SMEM, SMEM, VMEM]
+        in_specs=[SMEM, VMEM]
         + [section(EDGE, t) for t in range(3)]
         + [section(TENC, t) for t in range(3)]
         + [pl.BlockSpec((1, EB), lambda b: (0, b))]
@@ -851,9 +974,9 @@
         out_specs=(VMEM, VMEM, VMEM),
         scratch_shapes=[
             pltpu.VMEM((slots, LANES), F32),
-            pltpu.VMEM((total, LANES), BF16),
             pltpu.VMEM((NBR, KV, SECT), F32),
-            pltpu.VMEM((total, LANES), F32),
+            pltpu.VMEM((SECT, LANES), F32),
+            pltpu.VMEM((SECT, LANES), F32),
             pltpu.VMEM((KV, LANES), F32),
             pltpu.VMEM((KV, 256), F32),
             pltpu.VMEM((KV, LANES), F32),
@@ -866,10 +989,11 @@
             pltpu.VMEM((5, PAD, LANES), F32),
             pltpu.VMEM((8, LANES), F32),
         ]
-        + [pltpu.VMEM((slots, LANES), F32) for _ in range(STREAMS)],
+        + [pltpu.VMEM((slots, LANES), F32) for _ in range(STREAMS)]
+        + [pltpu.VMEM((SECT, LANES), BF16) for _ in range(NBR + 1)],
         compiler_params=params_of(),
         cost_estimate=pl.CostEstimate(flops=9_000_000_000, bytes_accessed=20_000_000, transcendentals=1_000_000),
-    )(index, counts, got, edges, edges, edges, codes, codes, codes, weight, *wts[5:])
+    )(index, got, edges, edges, edges, codes, codes, codes, weight, *wts[5:])
 
 
 def pack_kernel(gru, bias, att, losses, out, rows):
@@ -912,48 +1036,53 @@
     )(gru, bias, att, losses)
 
 
+def edge_kernel(edges, stamps, out, stage):
+    stage[...] = jnp.zeros_like(stage)
+    stage[EDGE + 1 : EDGE + 2, :] = jnp.ones((1, EV), F32)
+    stage[0:EDGE, :] = edges[0].astype(F32)
+    stage[EDGE : EDGE + 1, :] = stamps[0].astype(F32)
+    for part in range(2):
+        out[0, part] = stage[LANES * part : LANES * part + LANES, :].T
+
+
+def edge_tables(edges, stamps):
+    senders = edges.shape[0]
+    return pl.pallas_call(
+        edge_kernel,
+        grid=(senders,),
+        out_shape=jax.ShapeDtypeStruct((senders, 2, EV, LANES), F32),
+        in_specs=[
+            pl.BlockSpec((1, EDGE, EV), lambda i: (i, 0, 0)),
+            pl.BlockSpec((1, 1, EV), lambda i: (i, 0, 0)),
+        ],
+        out_specs=pl.BlockSpec((1, 2, EV, LANES), lambda i: (i, 0, 0, 0)),
+        scratch_shapes=[pltpu.VMEM((2 * LANES, EV), F32)],
+        compiler_params=params_of(16 * 2**20),
+        cost_estimate=pl.CostEstimate(flops=3_000_000, bytes_accessed=6_000_000, transcendentals=0),
+    )(edges, stamps)
+
+
 def mail_kernel(
-    starts,
-    rows,
-    events,
-    partner,
-    edges,
-    stamps,
-    own,
-    mailbox,
-    mail_time,
-    mail_new,
-    time_new,
-    near,
-    far,
-    kept,
-    stage,
-    lines,
+    starts, rows, events, partner, far, own, mailbox, mail_time, mail_new, time_new, near, kept, lines
 ):
     step = pl.program_id(0)
     senders = rows.shape[0] // (2 * EV)
 
     @pl.when(step == 0)
     def _():
-        kept[...] = jnp.zeros_like(kept)
-        stage[...] = jnp.zeros_like(stage)
-        stage[EDGE + 1 : EDGE + 2, :] = jnp.ones((1, EV), F32)
+        kept[2] = jnp.zeros(kept.shape[1:], F32)
 
     @pl.when(step < senders)
     def _():
         near[...] = partner[0].astype(F32)
-        stage[0:EDGE, :] = edges[0].astype(F32)
-        stage[EDGE : EDGE + 1, :] = stamps[0].astype(F32)
-        for part in range(2):
-            far[part] = stage[LANES * part : LANES * part + LANES, :].T
 
         def move(i, carry):
             place = step * 2 * EV + i
             to = pl.ds(rows[place], 1)
             event = pl.ds(events[place], 1)
             kept[0, to, :] = near[pl.ds(i, 1), :]
-            kept[1, to, :] = far[0, event, :]
-            kept[2, to, :] = far[1, event, :]
+            kept[1, to, :] = far[0, 0, event, :]
+            kept[2, to, :] = far[0, 1, event, :]
             return carry
 
         lax.fori_loop(starts[2 * step], starts[2 * step + 1], move, 0)
@@ -973,7 +1102,7 @@
         time_new[...] = jnp.where(has, last[stamp : stamp + 1, :].astype(jnp.int32), mail_time[...])
 
 
-def deliver(starts, rows, events, partner, edges, stamps, own, mailbox, mail_time):
+def deliver(starts, rows, events, partner, far, own, mailbox, mail_time):
     senders = partner.shape[0]
     nodes = mailbox.shape[1]
     block = 1024
@@ -996,8 +1125,7 @@
             SMEM,
             SMEM,
             pl.BlockSpec((1, 2 * EV, LANES), sender),
-            pl.BlockSpec((1, EDGE, EV), sender),
-            pl.BlockSpec((1, 1, EV), sender),
+            pl.BlockSpec((1, 2, EV, LANES), lambda i: (jnp.minimum(i, senders - 1), 0, 0, 0)),
             cols(MEM),
             cols(MAIL),
             cols(1),
@@ -1005,66 +1133,85 @@
         out_specs=(cols(MAIL), cols(1)),
         scratch_shapes=[
             pltpu.VMEM((2 * EV, LANES), F32),
-            pltpu.VMEM((2, EV, LANES), F32),
             pltpu.VMEM((3, nodes, LANES), F32),
-            pltpu.VMEM((2 * LANES, EV), F32),
             pltpu.VMEM((MAIL + 6, block), F32),
         ],
-        compiler_params=params_of(48 * 2**20),
+        compiler_params=params_of(44 * 2**20),
         cost_estimate=pl.CostEstimate(flops=20_000_000, bytes_accessed=16_000_000, transcendentals=0),
-    )(starts, rows, events, partner, edges, stamps, own, mailbox, mail_time)
+    )(starts, rows, events, partner, far, own, mailbox, mail_time)
 
 
 def flip(x, axis, mask):
     return lax.ppermute(x, axis, [(i, i ^ mask) for i in range(lax.axis_size(axis))])
 
 
-def axis_bits():
+def rounds():
     table = []
-    for axis in ("batch", "node"):
-        count = lax.axis_size(axis).bit_length() - 1
-        for b in reversed(range(count)):
-            table.append((axis, 1 << b))
+    low, count = 2, lax.axis_size("node")
+    while low < count:
+        size = min(4, count // low)
+        table.append(("node", low, size))
+        low *= size
+    table.append(("batch", 1, lax.axis_size("batch")))
+    table.append(("node", 1, 2))
     return table
 
 
-def bit_of(axis, mask):
-    return (lax.axis_index(axis) & mask) != 0
-
-
-def gather_params(x):
-    table = axis_bits()
-    order = [i for i, (a, m) in enumerate(table) if a == "node" and m > 1]
-    order += [i for i, (a, m) in enumerate(table) if a == "batch"][::-1]
-    order += [len(table) - 1]
+def place_in(axis, low, size):
+    return (lax.axis_index(axis) // low) % size
+
+
+def tree_sum(parts):
+    while len(parts) > 1:
+        parts = [a + b for a, b in zip(parts[::2], parts[1::2])]
+    return parts[0]
+
+
+def gather_params(x, between):
     shape = x.shape
-    x = x.reshape((1,) * len(table) + shape)
-    for i in order:
-        axis, mask = table[i]
-        y = flip(x, axis, mask)
-        bit = bit_of(axis, mask)
-        x = jnp.concatenate([jnp.where(bit, y, x), jnp.where(bit, x, y)], i)
+    axes = []
+    for number, (axis, low, size) in enumerate(rounds()):
+        parts = [x] + [flip(x, axis, low * m) for m in range(1, size)]
+        parts = between(number, x, parts)
+        here = place_in(axis, low, size)
+        key = (axis == "node", -low)
+        at = sum(1 for k in axes if k < key)
+        axes.append(key)
+        axes.sort()
+        out = jnp.zeros(x.shape[:at] + (size,) + x.shape[at:], x.dtype)
+        for m, part in enumerate(parts):
+            to = jnp.bitwise_xor(here, m)
+            out = lax.dynamic_update_slice_in_dim(out, jnp.expand_dims(part, at), to, at)
+        x = out
     return x.reshape((-1,) + shape[1:])
 
 
-def scatter_sum(x):
-    table = axis_bits()
-    order = [len(table) - 1]
-    order += [i for i, (a, m) in enumerate(table) if a == "batch"]
-    order += [i for i, (a, m) in enumerate(table) if a == "node" and m > 1][::-1]
-    x = x.reshape((2,) * len(table) + (-1, LANES))
-    for i in order:
-        axis, mask = table[i]
-        bit = bit_of(axis, mask).astype(jnp.int32)
-        away = lax.dynamic_slice_in_dim(x, 1 - bit, 1, i)
-        x = lax.dynamic_slice_in_dim(x, bit, 1, i) + flip(away, axis, mask)
+def scatter_sum(x, between):
+    table = rounds()
+    dims = sorted(((axis == "node", -low), size) for axis, low, size in table)
+    keys = [k for k, _ in dims]
+    x = x.reshape(tuple(n for _, n in dims) + (-1, LANES))
+    for number, (axis, low, size) in enumerate(table[::-1]):
+        at = keys.index((axis == "node", -low))
+        here = place_in(axis, low, size)
+
+        def part(m, x=x, at=at, here=here):
+            return lax.dynamic_slice_in_dim(x, jnp.bitwise_xor(here, m), 1, at)
+
+        away = [flip(part(m), axis, low * m) for m in range(1, size)]
+        away = between(number, x, away)
+        x = tree_sum([part(0)] + list(away))
     return x.reshape(-1, LANES)
 
 
 def sum_all(x):
-    for axis, mask in axis_bits()[::-1]:
-        x = x + flip(x, axis, mask)
+    for axis, low, size in rounds()[::-1]:
+        x = tree_sum([x] + [flip(x, axis, low * m) for m in range(1, size)])
     return x
+
+
+def after(x, *others):
+    return lax.optimization_barrier((x,) + others)[0]
 
 
 def swap(x):
@@ -1102,17 +1249,14 @@
     slots = req_rows.shape[3]
     wanted = req_rows[0, 0]
     counts = req_count[0, 0]
-    mem_cols = memory[0].T
+    rows = memory.shape[1]
+    mem_cols = jnp.transpose(memory.reshape(rows // LANES, LANES, MEM), (2, 0, 1))
     mail_cols = mailbox[0].T
     feat_cols = node_feat.T
     edge_cols = jnp.transpose(nbr_edge[0, 0], (1, 2, 0))
 
-    flat = gather_params(params.astype(BF16).reshape(1, -1, LANES)).reshape(-1, LANES)
-    wts = weights_of(flat)
-    asked = swap(wanted).reshape(-1)
-
-    dt = nbr_dt[0, 0].T
-    codes_n, codes_m = time_codes(dt, mail_time - update_time)
+    dead = jnp.arange(slots, dtype=jnp.int32)[None, :] >= counts[:, None]
+    wanted_or_dead = wanted + rows * dead.astype(jnp.int32)
 
     near_slot = to_slot(nbr_live[0, 0].T, counts, slots)
     root_slot = to_slot(root_live[0, 0], counts, slots)
@@ -1123,61 +1267,96 @@
         [near_index.reshape(blocks, -1), root_index.reshape(blocks, -1)], 1
     ).reshape(-1)
 
+    edge_sent = ev_edge[0, 0].T
+    early = {}
+
+    last = len(rounds()) - 1
+
+    def between(number, x, parts):
+        if number == last - 1:
+            early["asked"] = swap(after(wanted_or_dead, x))
+            early["codes"] = time_codes(after(mail_time - update_time, x))
+            *parts, early["asked"], early["codes"] = lax.optimization_barrier(
+                (*parts, early["asked"], early["codes"])
+            )
+        if number == last:
+            early["edges"] = swap(jnp.broadcast_to(after(edge_sent, x), (shards,) + edge_sent.shape))
+        return parts
+
+    flat = gather_params(params.astype(BF16).reshape(1, -1, LANES), between).reshape(-1, LANES)
+    asked = early["asked"].reshape(-1)
+    flags = (asked < rows).astype(jnp.int32)
+    asked = asked % rows
+    codes_m = early["codes"][0]
+    wts = weights_of(flat)
+    h_sent, s_rows, low = gru_forward(asked, mail_cols, codes_m, mem_cols, feat_cols, wts, shards, slots)
+    h_got = swap(h_sent)
+
+    codes_n = time_codes(nbr_dt[0, 0].T)
+    edges_all = early["edges"]
     ends = root_slot[:2].reshape(-1)
     ordered = lax.sort(ends * (2 * EV) + jnp.arange(2 * EV, dtype=jnp.int32))
-    end_id = ordered % (2 * EV)
-    end_slot = ordered // (2 * EV)
-    partner_slot = ends[(end_id + EV) % (2 * EV)]
-    end_row = wanted.reshape(-1)[end_slot]
+    end_row, partner_slot, event = bookkeeping(ordered, ends, wanted.reshape(-1))
     first = jnp.sum(
-        (end_slot[None, :] < (jnp.arange(LANES, dtype=jnp.int32) * slots)[:, None]).astype(jnp.int32), 1
+        (ordered[None, :] < (jnp.arange(LANES, dtype=jnp.int32) * (slots * 2 * EV))[:, None]).astype(jnp.int32),
+        1,
     )
-    notes = jnp.concatenate([end_row, end_id % EV, ev_time[0, 0], first]).reshape(-1, LANES)
-    notes = lax.all_gather(notes, "node", axis=0, tiled=False)
-    edges_all = lax.all_gather(ev_edge[0, 0].T, "node", axis=0, tiled=False)
-    notes = notes.reshape(shards, -1)
-
-    h_sent, s_rows, s_cols = gru_forward(asked, mail_cols, codes_m, mem_cols, feat_cols, wts, shards * slots)
-    h_got = swap(h_sent.reshape(shards, slots, LANES))
-    s_sent = gather_rows(s_rows, asked)
-    h_got, s_sent = lax.optimization_barrier((h_got, s_sent))
-    s_got = swap(s_sent.reshape(shards, slots, LANES)).reshape(-1, LANES)
-
-    d_sent, att_grads, losses = attention(
-        index, counts, h_got.reshape(-1, LANES), edge_cols, codes_n, neg_count[0], wts
+    notes = jnp.concatenate([end_row, event, ev_time[0, 0], first])
+    digits = jnp.concatenate([notes // 128, notes % 128]).astype(BF16)
+    lines = -(-digits.shape[0] // (8 * slots)) * 8
+    digits = jnp.pad(digits, (0, lines * slots - digits.shape[0])).reshape(lines, slots)
+    s_sent = send_rows(s_rows, asked, digits, shards, slots)
+    h_got, s_sent, codes_n, edges_all, partner_slot, index = lax.optimization_barrier(
+        (h_got, s_sent, codes_n, edges_all, partner_slot, index)
     )
-    d_got = swap(d_sent.reshape(shards, slots, LANES)).reshape(-1, LANES)
-
-    partner = gather_rows(s_got, partner_slot)
-    partner = lax.all_gather(partner, "node", axis=0, tiled=False)
-
-    mem_new, mem_grad, upd_new, gru_grads, bias_grads = gru_backward(
-        asked, d_got, mail_cols, codes_m, mem_cols, feat_cols, mail_time, update_time, wts
+    s_got = swap(s_sent)
+    d_sent, att_grads, losses = attention(index, h_got, edge_cols, codes_n, neg_count[0], wts)
+    d_sent, s_got, low = lax.optimization_barrier((d_sent, s_got, low))
+    d_got = swap(d_sent)
+
+    factors, s_cols, mem_new, upd_new = gru_factors(
+        asked, flags, mail_cols, codes_m, low, mem_cols, mail_time, update_time, wts
+    )
+    partner = partner_rows(s_got, partner_slot)
+    digits = s_got[:, WIRE:, :].reshape(shards, -1)[:, : 2 * notes.shape[0]].astype(F32).astype(jnp.int32)
+    notes = digits[:, : notes.shape[0]] * 128 + digits[:, notes.shape[0] :]
+    stamps = notes[:, 4 * EV : 5 * EV].reshape(shards, 1, EV)
+    far = edge_tables(edges_all, stamps)
+    partner = jnp.broadcast_to(partner[None], (shards,) + partner.shape)
+    d_got, factors, partner, far = lax.optimization_barrier((d_got, factors, partner, far))
+    partner_got = swap(partner)
+    mem_grad, gru_grads, bias_grads = gru_backward(
+        asked, d_got, factors, mail_cols, codes_m, low, feat_cols, wts
     )
     packed = pack(gru_grads, bias_grads, att_grads, losses)[:FLAT_ROWS]
-    shard = scatter_sum(packed)
-
-    events_of = notes[:, 2 * EV : 4 * EV].reshape(-1)
-    rows_of = notes[:, : 2 * EV].reshape(-1)
-    stamps = notes[:, 4 * EV : 5 * EV].reshape(shards, 1, EV)
-    starts = lax.dynamic_slice_in_dim(notes[:, 5 * EV :], me, 2, 1).reshape(-1)
-    mail_new, stamp_new = deliver(
-        starts, rows_of, events_of, partner, edges_all, stamps, s_cols, mail_cols, mail_time
-    )
+    late = {}
+
+    def during(number, x, parts):
+        if number == 1:
+            events_of = notes[:, 2 * EV : 4 * EV].reshape(-1)
+            rows_of = notes[:, : 2 * EV].reshape(-1)
+            starts = lax.dynamic_slice_in_dim(notes[:, 5 * EV :], me, 2, 1).reshape(-1)
+            mail = deliver(
+                starts, rows_of, events_of, after(partner_got, x), far, s_cols, mail_cols, mail_time
+            )
+            *parts, late["mail"], late["stamp"] = lax.optimization_barrier((*parts, *mail))
+        return parts
+
+    shard = scatter_sum(packed, during)
+    mail_new, stamp_new = late["mail"], late["stamp"]
 
     number = lax.axis_index("batch") * shards + me
     size = shard.shape[0] * LANES
     place = number * size + jnp.arange(size, dtype=jnp.int32).reshape(-1, LANES)
     grad = jnp.where(place < USED, shard, 0.0)
-    values = jnp.stack(
-        [
-            jnp.sum(grad * grad),
-            jnp.sum(jnp.where(place == USED, shard, 0.0)),
-            jnp.sum(jnp.where(place == USED + 1, shard, 0.0)),
-        ]
-    )
-    values = sum_all(jnp.zeros((8, LANES), F32).at[0, :3].set(values))
-    grad_norm = jnp.sqrt(values[0, 0])
+    lines = [
+        jnp.sum(grad * grad, 0, keepdims=True),
+        jnp.sum(jnp.where(place == USED, shard, 0.0), 0, keepdims=True),
+        jnp.sum(jnp.where(place == USED + 1, shard, 0.0), 0, keepdims=True),
+        jnp.zeros((5, LANES), F32),
+    ]
+    values = jnp.sum(sum_all(jnp.concatenate(lines, 0)), 1)
+    grad_norm = jnp.sqrt(values[0])
     clipped = grad.reshape(-1) * jnp.minimum(1.0, clip_limit / (grad_norm + 1e-06))
     moment1_new = beta_first * moment1 + (1.0 - beta_first) * clipped
     moment2_new = beta_second * moment2 + (1.0 - beta_second) * clipped * clipped
@@ -1188,18 +1367,18 @@
     )
     params_new = params - learn_rate * (ratio + decay_rate * params)
     return (
-        values[0, 1],
-        values[0, 2],
+        values[1],
+        values[2],
         grad_norm,
         params_new,
         moment1_new,
         moment2_new,
         params_new.astype(BF16),
-        mem_new.T[None],
+        jnp.transpose(mem_new, (1, 2, 0)).reshape(memory.shape),
         mail_new.T[None],
         stamp_new,
         upd_new,
-        mem_grad.T[None],
+        jnp.transpose(mem_grad, (1, 2, 0)).reshape(memory.shape),
     )
 
 

time: 456 us -> 332 us (0.73)
  blocking collectives: 67.6 us -> 0 us
  waiting for transfers between devices: 77.8 us -> 32.6 us
  local copies, waits for them, and re-layouts: 51.1 us -> 25 us
  starting transfers between devices: 35.1 us -> 53.4 us
  between operations: 16.6 us -> 3.2 us
  Pallas kernels: 187 us -> 200 us
    all_to_all x1 -> x0, blocking collectives: 53.4 us -> none  [swap(): return lax.all_to_all(x, 'node', split_axis=0, concat_axis=0, tiled=True)]
    pallas_call x5 -> x9, Pallas kernels: 93.8 us -> 118 us  [the longest x1 31.2 us: gru_forward(): pl.pallas_call(gru_kernel, grid=(rows // BLOCK,), out_shape=(jax.ShapeDty...]
    all_to_all x3 -> x6, waiting for transfers between devices: 39.4 us -> 16.3 us  [swap(): return lax.all_to_all(x, 'node', split_axis=0, concat_axis=0, tiled=True)]
    ppermute x15 -> x21, waiting for transfers between devices: 37.7 us -> 16.4 us  [flip(): lax.ppermute(x, axis, [(i, i ^ mask) for i in range(lax.axis_size(axis))])]
    unnamed x104 -> x67, local copies, waits for them, and re-layouts: 33.9 us -> 17.1 us
    all_gather x1 -> x0, blocking collectives: 14.2 us -> none  [body(): notes = lax.all_gather(notes, 'node', axis=0, tiled=False)]
    pallas_call x1, Pallas kernels: 70.3 us -> 58.7 us  [attention(): pl.pallas_call(attention_kernel, grid=(blocks,), out_shape=(jax.ShapeDtyp...]
    all_to_all x3 -> x6, starting transfers between devices: 14.2 us -> 25.6 us  [swap(): return lax.all_to_all(x, 'node', split_axis=0, concat_axis=0, tiled=True)]
  transfers between devices with their start and end apart: 20 -> 27, of which waited for: 12 -> 15; matrix products, arithmetic and copies ran while one was open for 11% -> 5% of each run, Pallas kernels for 15% -> 61%
where the time goes in v2:
time: 332 us; the launch traced here: 330 us
  Pallas kernels  200 us (60%)
  starting transfers between devices  53.4 us (16%)
  waiting for transfers between devices  32.6 us (10%)
  local copies, waits for them, and re-layouts  25 us (8%)
  other arithmetic  15.5 us (5%)
    pallas_call x1, Pallas kernels, attention(): pl.pallas_call(attention_kernel, grid=(blocks,), out_shape=(jax.ShapeDtyp...  58.7 us
    pallas_call x1, Pallas kernels, gru_forward(): pl.pallas_call(gru_kernel, grid=(rows // BLOCK,), out_shape=(jax.ShapeDty...  31.2 us
    pallas_call x1, Pallas kernels, gru_backward(): pl.pallas_call(gru_back_kernel, grid=(rows // BLOCK,), out_shape=(jax.Sha...  29 us
    pallas_call x1, Pallas kernels, gru_factors(): pl.pallas_call(factor_kernel, grid=(rows // BLOCK,), out_shape=(jax.Shape...  28 us
    ppermute x21, starting transfers between devices, flip(): lax.ppermute(x, axis, [(i, i ^ mask) for i in range(lax.axis_size(axis))])  27.8 us
    all_to_all x6, starting transfers between devices, swap(): return lax.all_to_all(x, 'node', split_axis=0, concat_axis=0, tiled=True)  25.6 us
    unnamed x67, local copies, waits for them, and re-layouts  17.1 us
    ppermute x21, waiting for transfers between devices, flip(): lax.ppermute(x, axis, [(i, i ^ mask) for i in range(lax.axis_size(axis))])  16.4 us
  transfers between devices with their start and end apart: 27, of which 15 were waited for; matrix products, arithmetic and copies ran while one was open for 5% of the time, Pallas kernels for 61%

profile of v2, /device:TPU:0, one launch (start us, length us, event | category | flops | bytes accessed | tf_op | source)
XLA Modules:
  0.0 329.8 jit_solution(6461441529168548279)
XLA Ops:
  0.6 0.8 convert_bitcast_fusion
  1.4 5.0 %collective-permute-start.2 = (bf16[1,88,128]{2,1,0:T(8,128)(2,1)S(1)}, bf16[1,88,128]{2,1,0:T(8,128)(2,1)S(1)}, u32[]{:S(2)}, u32[]{:S(2)}) collective-permute-start(bf16[1,88,128]{2,1,0:T(8,128)(2,1)S(1)} %convert_bitcast_fusion), channel_id=1, source_target_pairs={{0,6},{1,7},{2,4},{3,5},{4,2},{5,3},{6,0},{7,1},{8,14},{9,15},{10,... | collective-permute-start | bytes 67592 | tf_op jit(solution)/shard_map/ppermute | solution.py:1145
  7.1 0.8 bitcast_dynamic-update-slice_fusion.9
  7.9 2.4 collective-permute-done
  10.3 0.9 collective-permute-done.1
  11.2 2.5 collective-permute-start.5
  14.8 0.8 bitcast_add_fusion
  16.2 3.3 %all-to-all-start = ((s32[8,1,1024]{2,1,0:T(1,128)}), s32[8,1,1024]{2,1,0:T(1,128)S(1)}, u32[]{:S(2)}, u32[]{:S(2)}) async-start(s32[8,1,1024]{2,1,0:T(1,128)} %all_to_all.23), calls=%async_computation | async-start | bytes 65536 | tf_op jit(solution)/shard_map/all_to_all | solution.py:1218
  19.6 0.8 sub.30.delta
  20.5 0.8 copy-done.13
  21.3 3.4 %shard_map.274 = bf16[1,100,8192]{2,1,0:T(8,128)(2,1)S(1)} custom-call(s32[1,8192]{1,0:T(1,128)S(1)} %sub.30.delta, f32[100,128]{1,0:T(8,128)S(1)} %copy-done.13), custom_call_target="tpu_custom_call" | custom-call | flops 24576000 | bytes 1638400 | tf_op jit(solution)/shard_map/pallas_call | solution.py:159
  24.7 1.2 copy-done
  26.1 1.3 broadcast_in_dim.110
  27.4 5.0 %all-to-all-start.2 = ((bf16[8,186,512]{2,1,0:T(8,128)(2,1)}), bf16[8,186,512]{2,1,0:T(8,128)(2,1)S(1)}, u32[]{:S(2)}, u32[]{:S(2)}) async-start(bf16[8,186,512]{2,1,0:T(8,128)(2,1)} %broadcast_in_dim.110), calls=%async_computation.2 | async-start | bytes 3145728 | tf_op jit(solution)/shard_map/all_to_all | solution.py:1218
  34.4 0.8 copy-done.18
  35.3 5.3 %shard_map.275 = (bf16[336,386]{1,0:T(8,128)(2,1)}, bf16[336,100]{1,0:T(8,128)(2,1)}, bf16[336,100]{1,0:T(8,128)(2,1)}, bf16[112,413]{1,0:T(8,128)(2,1)}, f32[2,...) custom-call(bf16[2816,128]{1,0:T(8,128)(2,1)} %bitcast.175), custom_call_target="tpu_custom_call" | custom-call | flops 4000000 | bytes 2000000 | tf_op jit(solution)/shard_map/pallas_call | solution.py:279
  40.6 31.2 %shard_map.276 = (bf16[8,104,1024]{2,1,0:T(8,128)(2,1)}, f32[8192,128]{1,0:T(8,128)}, bf16[100,8192]{1,0:T(8,128)(2,1)}) custom-call(s32[8192]{0:T(1024)} %add_select_fusion.index, bf16[386,8192]{1,0:T(8,128)(2,1)} %bitcast.167, bf16[100,8192]{1,0:T(8,128)(2,1)} %bitcast.163, f32[100,64,128]{2,1,0:T(8,128)} %bitcast.173, bf16[413,8192]{1,0:T(8,128)(2,1)} %bitcast.171, ...), custom_call_target="tpu_custom_call" | custom-call | flops 4000000000 | bytes 24000000 | tf_op jit(solution)/shard_map/pallas_call | solution.py:398
  71.9 5.0 %all-to-all-start.1 = ((bf16[8,104,1024]{2,1,0:T(8,128)(2,1)}), bf16[8,104,1024]{2,1,0:T(8,128)(2,1)}, u32[]{:S(2)}, u32[]{:S(2)}) async-start(bf16[8,104,1024]{2,1,0:T(8,128)(2,1)} %get-tuple-element.91), calls=%async_computation.1 | async-start | bytes 3407872 | tf_op jit(solution)/shard_map/all_to_all | solution.py:1218
  77.8 4.4 %sort.10 = (s32[1024]{0:T(1024)}, s32[1024]{0:T(1024)}) sort(s32[1024]{0:T(1024)S(1)} %iota_add_fusion, s32[1024]{0:T(1024)S(1)} %iota.29), dimensions={0}, to_apply=%region_2.3 | sort | flops 10240 | bytes 16384 | tf_op jit(solution)/shard_map/sort | solution.py:1298
  82.2 6.3 %shard_map.277 = (s32[1024]{0:T(1024)}, s32[1024]{0:T(1024)}, s32[1024]{0:T(1024)}) custom-call(s32[1024]{0:T(1024)} %get-tuple-element.93.ordered, s32[1024]{0:T(1024)} %bitcast.187, s32[8192]{0:T(1024)} %bitcast.182), custom_call_target="tpu_custom_call" | custom-call | flops 4000000 | bytes 60000 | tf_op jit(solution)/shard_map/pallas_call | solution.py:471
  88.5 0.9 convert_reduce_fusion
  91.2 6.4 %shard_map.279.p0.p1.p2 = bf16[10,100,1536]{2,1,0:T(8,128)(2,1)S(1)} custom-call(s32[10,1536]{1,0:T(8,128)S(1)} %bitcast.166, f32[100,128]{1,0:T(8,128)S(1)} %copy-done.14), custom_call_target="tpu_custom_call" | custom-call | flops 46080000 | bytes 3072000 | tf_op jit(solution)/shard_map/pallas_call | solution.py:159
  97.6 1.7 copy-done.5
  99.3 2.2 copy-done.4
  101.5 9.8 %shard_map.278 = bf16[8,112,1024]{2,1,0:T(8,128)(2,1)S(1)} custom-call(s32[8192]{0:T(1024)S(1)} %copy-done.10, f32[8192,128]{1,0:T(8,128)S(1)} %copy-done.4, bf16[8,1024]{1,0:T(8,128)(2,1)S(1)} %reshape.156.notes), custom_call_target="tpu_custom_call" | custom-call | flops 8000000 | bytes 6000000 | tf_op jit(solution)/shard_map/pallas_call | solution.py:426
  111.3 1.2 copy-done.3
  112.5 5.0 %all-to-all-done.1.got = bf16[8,104,1024]{2,1,0:T(8,128)(2,1)} async-done(((bf16[8,104,1024]{2,1,0:T(8,128)(2,1)}), bf16[8,104,1024]{2,1,0:T(8,128)(2,1)}, u32[]{:S(2)}, u32[]{:S(2)}) %all-to-all-start.1) | async-done | bytes 1703968 | tf_op jit(solution)/shard_map/all_to_all | solution.py:1218
  117.6 3.6 %all-to-all-start.3 = ((bf16[8,112,1024]{2,1,0:T(8,128)(2,1)}), bf16[8,112,1024]{2,1,0:T(8,128)(2,1)S(1)}, u32[]{:S(2)}, u32[]{:S(2)}) async-start(bf16[8,112,1024]{2,1,0:T(8,128)(2,1)} %copy-done.3), calls=%async_computation.3 | async-start | bytes 3670016 | tf_op jit(solution)/shard_map/all_to_all | solution.py:1218
  121.2 58.7 %shard_map.280 = (bf16[8,104,1024]{2,1,0:T(8,128)(2,1)}, f32[1448,128]{1,0:T(8,128)}, f32[8,128]{1,0:T(8,128)}) custom-call(s32[16896]{0:T(1024)} %reshape.160.index, bf16[8,104,1024]{2,1,0:T(8,128)(2,1)} %all-to-all-done.1.got, bf16[10,186,1536]{2,1,0:T(8,128)(2,1)} %bitcast.204, bf16[10,186,1536]{2,1,0:T(8,128)(2,1)} %bitcast.205, ...), custom_call_target="tpu_custom_call" | custom-call | flops 8999999488 | bytes 20000000 | tf_op jit(solution)/shard_map/pallas_call | solution.py:961
  179.9 5.0 %all-to-all-start.4 = ((bf16[8,104,1024]{2,1,0:T(8,128)(2,1)}), bf16[8,104,1024]{2,1,0:T(8,128)(2,1)}, u32[]{:S(2)}, u32[]{:S(2)}) async-start(bf16[8,104,1024]{2,1,0:T(8,128)(2,1)} %get-tuple-element.117), calls=%async_computation.4 | async-start | bytes 3407872 | tf_op jit(solution)/shard_map/all_to_all | solution.py:1218
  185.8 2.9 shard_map.282
  189.4 1.4 shard_map.283.far
  190.8 2.0 copy-done.1
  192.8 28.0 %shard_map.281 = (f32[5,100,8192]{2,1,0:T(8,128)}, bf16[100,8192]{1,0:T(8,128)(2,1)}, f32[100,64,128]{2,1,0:T(8,128)}, s32[1,8192]{1,0:T(1,128)}) custom-call(s32[8192]{0:T(1024)} %add_select_fusion.index, s32[8192]{0:T(1024)} %fusion.13.flags, bf16[386,8192]{1,0:T(8,128)(2,1)} %bitcast.168, bf16[100,8192]{1,0:T(8,128)(2,1)} %bitcast.164, ...), custom_call_target="tpu_custom_call" | custom-call | flops 3000000000 | bytes 34000000 | tf_op jit(solution)/shard_map/pallas_call | solution.py:538
  220.9 4.8 %all-to-all-done.4.got = bf16[8,104,1024]{2,1,0:T(8,128)(2,1)} async-done(((bf16[8,104,1024]{2,1,0:T(8,128)(2,1)}), bf16[8,104,1024]{2,1,0:T(8,128)(2,1)}, u32[]{:S(2)}, u32[]{:S(2)}) %all-to-all-start.4) | async-done | bytes 1703968 | tf_op jit(solution)/shard_map/all_to_all | solution.py:1218
  225.7 1.6 broadcast_in_dim.113
  227.3 3.6 %all-to-all-start.5 = ((bf16[8,1024,128]{2,1,0:T(8,128)(2,1)}), bf16[8,1024,128]{2,1,0:T(8,128)(2,1)S(1)}, u32[]{:S(2)}, u32[]{:S(2)}) async-start(bf16[8,1024,128]{2,1,0:T(8,128)(2,1)} %broadcast_in_dim.113), calls=%async_computation.5 | async-start | bytes 4194304 | tf_op jit(solution)/shard_map/all_to_all | solution.py:1218
  231.0 29.0 %shard_map.284 = (f32[100,64,128]{2,1,0:T(8,128)}, f32[2176,128]{1,0:T(8,128)}, f32[8,128]{1,0:T(8,128)}) custom-call(s32[8192]{0:T(1024)} %add_select_fusion.index, bf16[8,104,1024]{2,1,0:T(8,128)(2,1)} %all-to-all-done.4.got, f32[5,100,8192]{2,1,0:T(8,128)} %get-tuple-element.124.factors, bf16[386,8192]{1,0:T(8,128)(2,1)} %bitcast.169, ...), custom_call_target="tpu_custom_call" | custom-call | flops 5000000000 | bytes 36000000 | tf_op jit(solution)/shard_map/pallas_call | solution.py:661
  260.0 1.2 copy-done.7
  261.9 1.8 shard_map.285
  263.7 1.2 slice.58
  264.9 1.2 constant_dynamic-slice_fusion.7
  266.7 1.8 collective-permute-done.7
  268.5 1.4 dynamic-slice_add_fusion
  270.0 2.5 collective-permute-start.10
  273.5 6.4 %all-to-all-done.5.partner = bf16[8,1024,128]{2,1,0:T(8,128)(2,1)S(1)} async-done(((bf16[8,1024,128]{2,1,0:T(8,128)(2,1)}), bf16[8,1024,128]{2,1,0:T(8,128)(2,1)S(1)}, u32[]{:S(2)}, u32[]{:S(2)}) %all-to-all-start.5) | async-done | bytes 2097184 | tf_op jit(solution)/shard_map/all_to_all | solution.py:1218
  279.9 2.2 copy-done.2
  282.1 1.5 copy-done.6
  283.6 15.7 %shard_map.286 = (bf16[386,8192]{1,0:T(8,128)(2,1)}, s32[1,8192]{1,0:T(1,128)}) custom-call(s32[16]{0:T(128)S(1)} %reshape.164.starts, s32[8192]{0:T(1024)S(1)} %get-tuple-element.213.rows, s32[8192]{0:T(1024)S(1)} %get-tuple-element.212.events, bf16[8,1024,128]{2,1,0:T(8,128)(2,1)S(1)} %all-to-all-done.5.partner, f32[8,2,512,128]{3,2,1,0:T(8,128)S(1)} %copy-done.2, ...), custom_call_target="tpu_custom_call" | custom-call | flops 20000000 | bytes 16000000 | tf_op jit(solution)/shard_map/pallas_call | solution.py:1116
  299.3 1.1 add_add_fusion
  300.5 2.3 collective-permute-start.11
  302.8 4.0 %collective-permute-start.13 = (f32[1,1,1,88,128]{4,3,2,1,0:T(8,128)S(1)}, f32[1,1,1,88,128]{4,3,2,1,0:T(8,128)S(1)}, u32[]{:S(2)}, u32[]{:S(2)}) collective-permute-start(f32[1,1,1,88,128]{4,3,2,1,0:T(8,128)S(1)} %get-tuple-element.202), channel_id=1, source_target_pairs={{0,6},{1,7},{2,4},{3,5},{4,2},{5,3},{6,0},{7,1},{8,14},{9,15},{10,... | collective-permute-start | bytes 135176 | tf_op jit(solution)/shard_map/ppermute | solution.py:1145
  306.9 2.9 collective-permute-done.13
  309.8 2.0 collective-permute-done.12
  311.9 1.2 collective-permute-done.14
  313.1 1.3 collective-permute-start.16
  314.4 1.4 collective-permute-start.17
  315.8 0.8 collective-permute-start.15
  316.7 2.2 collective-permute-done.17
  319.5 1.7 collective-permute-start.20
  321.2 2.7 collective-permute-start.18
  323.9 1.0 collective-permute-done.20
  324.9 0.8 collective-permute-done.19
  327.2 1.5 fusion.21
  (133 shorter events, 12.8 us)
Async XLA Ops:
  1.4 9.8 %collective-permute-start.2 = (bf16[1,88,128]{2,1,0:T(8,128)(2,1)S(1)}, bf16[1,88,128]{2,1,0:T(8,128)(2,1)S(1)}, u32[]{:S(2)}, u32[]{:S(2)}) collective-permute-start(bf16[1,88,128]{2,1,0:T(8,128)(2,1)S(1)} %convert_bitcast_fusion), channel_id=1, source_target_pairs={{0,6},{1,7},{2,4},{3,5},{4,2},{5,3},{6,0},{7,1},{8,14},{9,15},{10,... | collective-permute-start | bytes 67592 | tf_op jit(solution)/shard_map/ppermute | solution.py:1145
  6.5 4.7 %collective-permute-start.1 = (bf16[1,88,128]{2,1,0:T(8,128)(2,1)S(1)}, bf16[1,88,128]{2,1,0:T(8,128)(2,1)S(1)}, u32[]{:S(2)}, u32[]{:S(2)}) collective-permute-start(bf16[1,88,128]{2,1,0:T(8,128)(2,1)S(1)} %convert_bitcast_fusion), channel_id=1, source_target_pairs={{0,4},{1,5},{2,6},{3,7},{4,0},{5,1},{6,2},{7,3},{8,12},{9,13},{10,... | collective-permute-start | bytes 67592 | tf_op jit(solution)/shard_map/ppermute | solution.py:1145
  6.5 3.8 %collective-permute-start = (bf16[1,88,128]{2,1,0:T(8,128)(2,1)S(1)}, bf16[1,88,128]{2,1,0:T(8,128)(2,1)S(1)}, u32[]{:S(2)}, u32[]{:S(2)}) collective-permute-start(bf16[1,88,128]{2,1,0:T(8,128)(2,1)S(1)} %convert_bitcast_fusion), channel_id=1, source_target_pairs={{0,2},{1,3},{2,0},{3,1},{4,6},{5,7},{6,4},{7,5},{8,10},{9,11},{10,... | collective-permute-start | bytes 67592 | tf_op jit(solution)/shard_map/ppermute | solution.py:1145
  7.1 19.0 %copy-start.21 = (bf16[1,1,512,186]{2,3,1,0:T(8,128)(2,1)S(1)}, bf16[1,1,512,186]{2,3,1,0:T(8,128)(2,1)}, u32[]{:S(2)}) copy-start(bf16[1,1,512,186]{2,3,1,0:T(8,128)(2,1)} %param.33) | copy-start | bytes 571396
  11.2 14.7 %collective-permute-start.5 = (bf16[4,1,88,128]{3,2,0,1:T(8,128)(2,1)S(1)}, bf16[4,1,88,128]{3,2,0,1:T(8,128)(2,1)S(1)}, u32[]{:S(2)}, u32[]{:S(2)}) collective-permute-start(bf16[4,1,88,128]{3,2,0,1:T(8,128)(2,1)S(1)} %bitcast_dynamic-update-slice_fusion.8), channel_id=1, source_target_pairs={{0,24},{8,16},{16,8},{24,0},{1,25},{9,17},{17,9},{25,1},{2,26},{10... | collective-permute-start | bytes 270344 | tf_op jit(solution)/shard_map/ppermute | solution.py:1145
  13.7 12.2 %collective-permute-start.4 = (bf16[4,1,88,128]{3,2,0,1:T(8,128)(2,1)S(1)}, bf16[4,1,88,128]{3,2,0,1:T(8,128)(2,1)S(1)}, u32[]{:S(2)}, u32[]{:S(2)}) collective-permute-start(bf16[4,1,88,128]{3,2,0,1:T(8,128)(2,1)S(1)} %bitcast_dynamic-update-slice_fusion.8), channel_id=1, source_target_pairs={{0,16},{8,24},{16,0},{24,8},{1,17},{9,25},{17,1},{25,9},{2,18},{10... | collective-permute-start | bytes 270344 | tf_op jit(solution)/shard_map/ppermute | solution.py:1145
  14.2 11.7 %collective-permute-start.3 = (bf16[4,1,88,128]{3,2,0,1:T(8,128)(2,1)S(1)}, bf16[4,1,88,128]{3,2,0,1:T(8,128)(2,1)S(1)}, u32[]{:S(2)}, u32[]{:S(2)}) collective-permute-start(bf16[4,1,88,128]{3,2,0,1:T(8,128)(2,1)S(1)} %bitcast_dynamic-update-slice_fusion.8), channel_id=1, source_target_pairs={{0,8},{8,0},{16,24},{24,16},{1,9},{9,1},{17,25},{25,17},{2,10},{10... | collective-permute-start | bytes 270344 | tf_op jit(solution)/shard_map/ppermute | solution.py:1145
  16.2 9.6 %all-to-all-start = ((s32[8,1,1024]{2,1,0:T(1,128)}), s32[8,1,1024]{2,1,0:T(1,128)S(1)}, u32[]{:S(2)}, u32[]{:S(2)}) async-start(s32[8,1,1024]{2,1,0:T(1,128)} %all_to_all.23), calls=%async_computation | async-start | bytes 65536 | tf_op jit(solution)/shard_map/all_to_all | solution.py:1218
  20.4 0.8 copy-start.13
  24.7 1.2 copy-start
  27.4 44.4 %all-to-all-start.2 = ((bf16[8,186,512]{2,1,0:T(8,128)(2,1)}), bf16[8,186,512]{2,1,0:T(8,128)(2,1)S(1)}, u32[]{:S(2)}, u32[]{:S(2)}) async-start(bf16[8,186,512]{2,1,0:T(8,128)(2,1)} %broadcast_in_dim.110), calls=%async_computation.2 | async-start | bytes 3145728 | tf_op jit(solution)/shard_map/all_to_all | solution.py:1218
  32.4 1.9 collective-permute-start.6
  34.4 0.9 copy-start.18
  71.8 5.1 %copy-start.28 = (s32[1,1,8]{2,1,0:T(1,128)S(1)}, s32[1,1,8]{2,1,0:T(1,128)}, u32[]{:S(2)}) copy-start(s32[1,1,8]{2,1,0:T(1,128)} %param.28) | copy-start | bytes 100
  71.8 5.2 %copy-start.26 = (s32[1,1,3,512]{3,1,2,0:T(1,128)S(1)}, s32[1,1,3,512]{3,1,2,0:T(1,128)}, u32[]{:S(2)}) copy-start(s32[1,1,3,512]{3,1,2,0:T(1,128)} %param.29) | copy-start | bytes 18436
  71.8 5.4 %copy-start.22 = (s32[1,1,8,1024]{3,2,1,0:T(8,128)S(1)}, s32[1,1,8,1024]{3,2,1,0:T(8,128)}, u32[]{:S(2)}) copy-start(s32[1,1,8,1024]{3,2,1,0:T(8,128)} %param.27) | copy-start | bytes 98308
  71.8 17.6 %copy-start.27 = (s32[1,1,512]{2,1,0:T(1,128)S(1)}, s32[1,1,512]{2,1,0:T(1,128)}, u32[]{:S(2)}) copy-start(s32[1,1,512]{2,1,0:T(1,128)} %param.34) | copy-start | bytes 6148
  71.8 18.3 %copy-start.23 = (s32[1,1,1536,10]{2,1,3,0:T(1,128)S(1)}, s32[1,1,1536,10]{2,1,3,0:T(1,128)}, u32[]{:S(2)}) copy-start(s32[1,1,1536,10]{2,1,3,0:T(1,128)} %param.31) | copy-start | bytes 184324
  71.8 18.4 %copy-start.20 = (s32[1,1,1536,10]{2,1,3,0:T(1,128)S(1)}, s32[1,1,1536,10]{2,1,3,0:T(1,128)}, u32[]{:S(2)}) copy-start(s32[1,1,1536,10]{2,1,3,0:T(1,128)} %param.30) | copy-start | bytes 184324
  71.8 19.4 %copy-start.14 = (f32[100,128]{1,0:T(8,128)S(1)}, f32[100,128]{1,0:T(8,128)}, u32[]{:S(2)}) copy-start(f32[100,128]{1,0:T(8,128)} %constant.170.clone.freq) | copy-start | bytes 153604
  71.9 45.7 %all-to-all-start.1 = ((bf16[8,104,1024]{2,1,0:T(8,128)(2,1)}), bf16[8,104,1024]{2,1,0:T(8,128)(2,1)}, u32[]{:S(2)}, u32[]{:S(2)}) async-start(bf16[8,104,1024]{2,1,0:T(8,128)(2,1)} %get-tuple-element.91), calls=%async_computation.1 | async-start | bytes 3407872 | tf_op jit(solution)/shard_map/all_to_all | solution.py:1218
  77.2 5.0 %copy-start.25 = (s32[1,4,2,128]{3,1,2,0:T(4,128)}, s32[1,4,2,128]{3,1,2,0:T(4,128)S(1)}, u32[]{:S(2)}) copy-start(s32[1,4,2,128]{3,1,2,0:T(4,128)S(1)} %copy.68) | copy-start | bytes 12292
  90.5 8.8 %copy-start.10 = (s32[8192]{0:T(1024)S(1)}, s32[8192]{0:T(1024)}, u32[]{:S(2)}) copy-start(s32[8192]{0:T(1024)} %add_select_fusion.index) | copy-start | bytes 98308
  97.6 1.7 copy-start.5
  99.3 2.2 copy-start.4
  111.3 1.2 copy-start.3
  117.6 62.3 %all-to-all-start.3 = ((bf16[8,112,1024]{2,1,0:T(8,128)(2,1)}), bf16[8,112,1024]{2,1,0:T(8,128)(2,1)S(1)}, u32[]{:S(2)}, u32[]{:S(2)}) async-start(bf16[8,112,1024]{2,1,0:T(8,128)(2,1)} %copy-done.3), calls=%async_computation.3 | async-start | bytes 3670016 | tf_op jit(solution)/shard_map/all_to_all | solution.py:1218
  179.9 5.8 %copy-start.15 = (s32[1024]{0:T(1024)S(1)}, s32[1024]{0:T(1024)}, u32[]{:S(2)}) copy-start(s32[1024]{0:T(1024)} %get-tuple-element.120.index) | copy-start | bytes 12292
  179.9 45.8 %all-to-all-start.4 = ((bf16[8,104,1024]{2,1,0:T(8,128)(2,1)}), bf16[8,104,1024]{2,1,0:T(8,128)(2,1)}, u32[]{:S(2)}, u32[]{:S(2)}) async-start(bf16[8,104,1024]{2,1,0:T(8,128)(2,1)} %get-tuple-element.117), calls=%async_computation.4 | async-start | bytes 3407872 | tf_op jit(solution)/shard_map/all_to_all | solution.py:1218
  188.7 0.7 copy-start.8
  190.8 2.0 copy-start.1
  192.8 32.9 %copy-start.9 = (bf16[1024,128]{1,0:T(8,128)(2,1)S(1)}, bf16[1024,128]{1,0:T(8,128)(2,1)}, u32[]{:S(2)}) copy-start(bf16[1024,128]{1,0:T(8,128)(2,1)} %copy-done.8) | copy-start | bytes 786436
  227.3 52.6 %all-to-all-start.5 = ((bf16[8,1024,128]{2,1,0:T(8,128)(2,1)}), bf16[8,1024,128]{2,1,0:T(8,128)(2,1)S(1)}, u32[]{:S(2)}, u32[]{:S(2)}) async-start(bf16[8,1024,128]{2,1,0:T(8,128)(2,1)} %broadcast_in_dim.113), calls=%async_computation.5 | async-start | bytes 4194304 | tf_op jit(solution)/shard_map/all_to_all | solution.py:1218
  230.9 29.0 %copy-start.11 = (f32[1448,128]{1,0:T(8,128)S(1)}, f32[1448,128]{1,0:T(8,128)}, u32[]{:S(2)}) copy-start(f32[1448,128]{1,0:T(8,128)} %get-tuple-element.127.att) | copy-start | bytes 2224132
  230.9 29.0 %copy-start.16 = (f32[8,128]{1,0:T(8,128)S(1)}, f32[8,128]{1,0:T(8,128)}, u32[]{:S(2)}) copy-start(f32[8,128]{1,0:T(8,128)} %get-tuple-element.128.losses) | copy-start | bytes 12292
  260.0 1.2 copy-start.7
  261.2 0.7 copy-start.17
  266.1 13.8 %copy-start.12 = (s32[1,8192]{1,0:T(1,128)S(1)}, s32[1,8192]{1,0:T(1,128)}, u32[]{:S(2)}) copy-start(s32[1,8192]{1,0:T(1,128)} %mail_time.3) | copy-start | bytes 98308
  266.1 2.4 collective-permute-start.7
  270.0 29.4 %collective-permute-start.10 = (f32[1,4,1,88,128]{4,3,2,1,0:T(8,128)S(1)}, f32[1,4,1,88,128]{4,3,2,1,0:T(8,128)}, u32[]{:S(2)}, u32[]{:S(2)}) collective-permute-start(f32[1,4,1,88,128]{4,3,2,1,0:T(8,128)S(1)} %get-tuple-element.198), channel_id=1, source_target_pairs={{0,24},{8,16},{16,8},{24,0},{1,25},{9,17},{17,9},{25,1},{2,26},{10... | collective-permute-start | bytes 540680 | tf_op jit(solution)/shard_map/ppermute | solution.py:1145
  272.5 26.9 %collective-permute-start.9 = (f32[1,4,1,88,128]{4,3,2,1,0:T(8,128)S(1)}, f32[1,4,1,88,128]{4,3,2,1,0:T(8,128)}, u32[]{:S(2)}, u32[]{:S(2)}) collective-permute-start(f32[1,4,1,88,128]{4,3,2,1,0:T(8,128)S(1)} %get-tuple-element.199), channel_id=1, source_target_pairs={{0,16},{8,24},{16,0},{24,8},{1,17},{9,25},{17,1},{25,9},{2,18},{10... | collective-permute-start | bytes 540680 | tf_op jit(solution)/shard_map/ppermute | solution.py:1145
  273.0 26.3 %collective-permute-start.8 = (f32[1,4,1,88,128]{4,3,2,1,0:T(8,128)S(1)}, f32[1,4,1,88,128]{4,3,2,1,0:T(8,128)}, u32[]{:S(2)}, u32[]{:S(2)}) collective-permute-start(f32[1,4,1,88,128]{4,3,2,1,0:T(8,128)S(1)} %get-tuple-element.200), channel_id=1, source_target_pairs={{0,8},{8,0},{16,24},{24,16},{1,9},{9,1},{17,25},{25,17},{2,10},{10... | collective-permute-start | bytes 540680 | tf_op jit(solution)/shard_map/ppermute | solution.py:1145
  279.9 2.2 copy-start.2
  282.1 1.5 copy-start.6
  283.6 43.6 %copy-start.19 = (f32[11264]{0:T(1024)S(1)}, f32[11264]{0:T(1024)}, u32[]{:S(2)}) copy-start(f32[11264]{0:T(1024)} %param.19) | copy-start | bytes 135172
  283.6 43.6 %copy-start.24 = (f32[11264]{0:T(1024)S(1)}, f32[11264]{0:T(1024)}, u32[]{:S(2)}) copy-start(f32[11264]{0:T(1024)} %param.20) | copy-start | bytes 135172
  300.5 6.3 %collective-permute-start.11 = (f32[1,1,1,88,128]{4,3,2,1,0:T(8,128)S(1)}, f32[1,1,1,88,128]{4,3,2,1,0:T(8,128)S(1)}, u32[]{:S(2)}, u32[]{:S(2)}) collective-permute-start(f32[1,1,1,88,128]{4,3,2,1,0:T(8,128)S(1)} %get-tuple-element.201), channel_id=1, source_target_pairs={{0,2},{1,3},{2,0},{3,1},{4,6},{5,7},{6,4},{7,5},{8,10},{9,11},{10,... | collective-permute-start | bytes 135176 | tf_op jit(solution)/shard_map/ppermute | solution.py:1145
  302.8 6.9 %collective-permute-start.13 = (f32[1,1,1,88,128]{4,3,2,1,0:T(8,128)S(1)}, f32[1,1,1,88,128]{4,3,2,1,0:T(8,128)S(1)}, u32[]{:S(2)}, u32[]{:S(2)}) collective-permute-start(f32[1,1,1,88,128]{4,3,2,1,0:T(8,128)S(1)} %get-tuple-element.202), channel_id=1, source_target_pairs={{0,6},{1,7},{2,4},{3,5},{4,2},{5,3},{6,0},{7,1},{8,14},{9,15},{10,... | collective-permute-start | bytes 135176 | tf_op jit(solution)/shard_map/ppermute | solution.py:1145
  306.8 4.9 %collective-permute-start.12 = (f32[1,1,1,88,128]{4,3,2,1,0:T(8,128)S(1)}, f32[1,1,1,88,128]{4,3,2,1,0:T(8,128)S(1)}, u32[]{:S(2)}, u32[]{:S(2)}) collective-permute-start(f32[1,1,1,88,128]{4,3,2,1,0:T(8,128)S(1)} %get-tuple-element.203), channel_id=1, source_target_pairs={{0,4},{1,5},{2,6},{3,7},{4,0},{5,1},{6,2},{7,3},{8,12},{9,13},{10,... | collective-permute-start | bytes 135176 | tf_op jit(solution)/shard_map/ppermute | solution.py:1145
  311.8 1.2 collective-permute-start.14
  313.1 3.6 %collective-permute-start.16 = (f32[8,128]{1,0:T(8,128)S(1)}, f32[8,128]{1,0:T(8,128)S(1)}, u32[]{:S(2)}, u32[]{:S(2)}) collective-permute-start(f32[8,128]{1,0:T(8,128)S(1)} %fusion.20), channel_id=1, source_target_pairs={{0,16},{8,24},{16,0},{24,8},{1,17},{9,25},{17,1},{25,9},{2,18},{10... | collective-permute-start | bytes 12296 | tf_op jit(solution)/shard_map/ppermute | solution.py:1145
  314.4 4.5 %collective-permute-start.17 = (f32[8,128]{1,0:T(8,128)S(1)}, f32[8,128]{1,0:T(8,128)S(1)}, u32[]{:S(2)}, u32[]{:S(2)}) collective-permute-start(f32[8,128]{1,0:T(8,128)S(1)} %fusion.20), channel_id=1, source_target_pairs={{0,24},{8,16},{16,8},{24,0},{1,25},{9,17},{17,9},{25,1},{2,26},{10... | collective-permute-start | bytes 12296 | tf_op jit(solution)/shard_map/ppermute | solution.py:1145
  315.8 3.6 %collective-permute-start.15 = (f32[8,128]{1,0:T(8,128)S(1)}, f32[8,128]{1,0:T(8,128)S(1)}, u32[]{:S(2)}, u32[]{:S(2)}) collective-permute-start(f32[8,128]{1,0:T(8,128)S(1)} %fusion.20), channel_id=1, source_target_pairs={{0,8},{8,0},{16,24},{24,16},{1,9},{9,1},{17,25},{25,17},{2,10},{10... | collective-permute-start | bytes 12296 | tf_op jit(solution)/shard_map/ppermute | solution.py:1145
  319.5 5.4 %collective-permute-start.20 = (f32[8,128]{1,0:T(8,128)S(1)}, f32[8,128]{1,0:T(8,128)S(1)}, u32[]{:S(2)}, u32[]{:S(2)}) collective-permute-start(f32[8,128]{1,0:T(8,128)S(1)} %add_add_fusion.3), channel_id=1, source_target_pairs={{0,6},{1,7},{2,4},{3,5},{4,2},{5,3},{6,0},{7,1},{8,14},{9,15},{10,... | collective-permute-start | bytes 12296 | tf_op jit(solution)/shard_map/ppermute | solution.py:1145
  321.2 4.5 %collective-permute-start.19 = (f32[8,128]{1,0:T(8,128)S(1)}, f32[8,128]{1,0:T(8,128)S(1)}, u32[]{:S(2)}, u32[]{:S(2)}) collective-permute-start(f32[8,128]{1,0:T(8,128)S(1)} %add_add_fusion.3), channel_id=1, source_target_pairs={{0,4},{1,5},{2,6},{3,7},{4,0},{5,1},{6,2},{7,3},{8,12},{9,13},{10,... | collective-permute-start | bytes 12296 | tf_op jit(solution)/shard_map/ppermute | solution.py:1145
  321.2 4.5 %collective-permute-start.18 = (f32[8,128]{1,0:T(8,128)S(1)}, f32[8,128]{1,0:T(8,128)S(1)}, u32[]{:S(2)}, u32[]{:S(2)}) collective-permute-start(f32[8,128]{1,0:T(8,128)S(1)} %add_add_fusion.3), channel_id=1, source_target_pairs={{0,2},{1,3},{2,0},{3,1},{4,6},{5,7},{6,4},{7,5},{8,10},{9,11},{10,... | collective-permute-start | bytes 12296 | tf_op jit(solution)/shard_map/ppermute | solution.py:1145

commit v3 on v2

--- a/solution.py
+++ b/solution.py
@@ -143,22 +143,28 @@
 
 def codes_kernel(delta, freq, out):
     freqs = freq[...]
+    extra = out.shape[1] - TENC
+    if extra:
+        tail = (row_of((extra, LANES)) == 0).astype(F32)
     for k in range(out.shape[0]):
 
         def one(i, carry, k=k):
             at = pl.ds(pl.multiple_of(i * LANES, LANES), LANES)
-            out[k, :, at] = cosine(delta[k : k + 1, at].astype(F32) * freqs).astype(BF16)
+            value = cosine(delta[k : k + 1, at].astype(F32) * freqs)
+            if extra:
+                value = jnp.concatenate([value, tail], 0)
+            out[k, :, at] = value.astype(BF16)
             return carry
 
         lax.fori_loop(0, delta.shape[1] // LANES, one, 0)
 
 
-def time_codes(delta):
+def time_codes(delta, lines=TENC):
     freq = jnp.asarray(np.tile(FREQS[:, None], (1, LANES)))
     rows, count = delta.shape
     return pl.pallas_call(
         codes_kernel,
-        out_shape=jax.ShapeDtypeStruct((rows, TENC, count), BF16),
+        out_shape=jax.ShapeDtypeStruct((rows, lines, count), BF16),
         in_specs=[VMEM] * 2,
         out_specs=VMEM,
         compiler_params=params_of(16 * 2**20),
@@ -168,13 +174,12 @@
     )(delta, freq)
 
 
-def weights_kernel(
+def unpack_weights(
     flat,
     w_mail,
-    w_time,
+    w_two,
     w_hid,
     w_feat,
-    gate_bias,
     kv_h,
     kv_e,
     kv_t,
@@ -210,19 +215,27 @@
             block = rows[pl.ds(start, size, stride=stride), :]
         return jnp.where(row_of((size, LANES)) < count, block, 0.0).T
 
+    def column(r):
+        return jnp.broadcast_to(rows[r : r + 1, :], (LANES, LANES)).T[:PAD, :]
+
+    at_bias = lane_of((PAD, LANES)) == MEM
     for g in range(3):
         to = slice(PAD * g, PAD * g + PAD)
         w_mail[to, :] = turned(g, MAIL, 3)[:PAD, :MAIL].astype(BF16)
-        w_time[to, :] = turned(3 * MAIL + g, TENC, 3)[:PAD, :TENC].astype(BF16)
-        w_hid[to, :] = turned(ROW_HH + g, MEM, 3)[:PAD, :MEM].astype(BF16)
+        time = jnp.where(at_bias, column(ROW_BIH + g), turned(3 * MAIL + g, TENC, 3)[:PAD])
+        hid = jnp.where(at_bias, column(ROW_BHH + g), turned(ROW_HH + g, MEM, 3)[:PAD])
+        time, hid = time[:, :PAD].astype(BF16), hid[:, :PAD].astype(BF16)
+        none = jnp.zeros((PAD, PAD), BF16)
+        if g < 2:
+            w_two[to, :] = jnp.concatenate([time, hid], 1)
+            w_hid[to, :] = hid
+        else:
+            w_two[to, :] = jnp.concatenate([time, none], 1)
+            w_hid[to, :] = none
+            last = slice(PAD * 3, PAD * 4)
+            w_two[last, :] = jnp.concatenate([none, hid], 1)
+            w_hid[last, :] = hid
     w_feat[...] = turned(ROW_NF, NFEAT)[:PAD, :NFEAT].astype(BF16)
-
-    def column(r):
-        return jnp.broadcast_to(rows[r : r + 1, :], (LANES, LANES)).T[:PAD, :]
-
-    for g in range(3):
-        gate_bias[0, PAD * g : PAD * g + PAD, :] = column(ROW_BIH + g)
-        gate_bias[1, PAD * g : PAD * g + PAD, :] = column(ROW_BHH + g)
     for part in range(2):
         to = slice(PAD * part, PAD * part + PAD)
 
@@ -255,36 +268,25 @@
     cols[5, :, :] = jnp.broadcast_to(value, (PAD, LANES))
 
 
-def weights_of(flat):
-    shapes = [
-        ((GATES, MAIL), BF16),
-        ((GATES, TENC), BF16),
-        ((GATES, MEM), BF16),
-        ((PAD, NFEAT), BF16),
-        ((2, GATES, LANES), F32),
-        ((KV, LANES), BF16),
-        ((KV, EDGE), BF16),
-        ((KV, TENC), BF16),
-        ((PAD, LANES), BF16),
-        ((PAD, LANES), F32),
-        ((PAD, PAD), BF16),
-        ((PAD, PAD), BF16),
-        ((PAD, LANES), BF16),
-        ((PAD, PAD), BF16),
-        ((PAD, PAD), BF16),
-        ((PAD, PAD), BF16),
-        ((PAD, PAD), BF16),
-        ((6, PAD, LANES), F32),
-    ]
-    return pl.pallas_call(
-        weights_kernel,
-        out_shape=[jax.ShapeDtypeStruct(s, d) for s, d in shapes],
-        in_specs=[VMEM],
-        out_specs=[VMEM] * len(shapes),
-        scratch_shapes=[pltpu.VMEM((FLAT_ROWS + 16, LANES), F32), pltpu.VMEM((WROWS + 512, LANES), F32)],
-        compiler_params=params_of(),
-        cost_estimate=pl.CostEstimate(flops=4_000_000, bytes_accessed=2_000_000, transcendentals=0),
-    )(flat)
+WEIGHTS = [
+    ((GATES, MAIL), BF16),
+    ((4 * PAD, 2 * PAD), BF16),
+    ((4 * PAD, PAD), BF16),
+    ((PAD, NFEAT), BF16),
+    ((KV, LANES), BF16),
+    ((KV, EDGE), BF16),
+    ((KV, TENC), BF16),
+    ((PAD, LANES), BF16),
+    ((PAD, LANES), F32),
+    ((PAD, PAD), BF16),
+    ((PAD, PAD), BF16),
+    ((PAD, LANES), BF16),
+    ((PAD, PAD), BF16),
+    ((PAD, PAD), BF16),
+    ((PAD, PAD), BF16),
+    ((PAD, PAD), BF16),
+    ((6, PAD, LANES), F32),
+]
 
 
 def gather_loop(index, table, out, count, base=0, to=0):
@@ -300,21 +302,27 @@
     lax.fori_loop(0, count // group, step, 0)
 
 
-def gather_turned(index, table, out):
+def gather_turned(index, table, out, finished=None):
     slots = out.shape[2]
     pieces = slots // LANES
 
-    def step(j, carry):
-        owner = j // pieces
-        at = pl.ds(pl.multiple_of((j - owner * pieces) * LANES, LANES), LANES)
-        groups = []
-        for g in range(LANES // 8):
-            picked = [table[pl.ds(index[j * LANES + g * 8 + u], 1), :] for u in range(8)]
-            groups.append(jnp.concatenate(picked, 0))
-        out[owner, 0:WIRE, at] = jnp.concatenate(groups, 0).T[:WIRE].astype(BF16)
+    def one(owner, carry):
+        def step(j, inner):
+            at = pl.ds(pl.multiple_of(j * LANES, LANES), LANES)
+            base = owner * slots + j * LANES
+            groups = []
+            for g in range(LANES // 8):
+                picked = [table[pl.ds(index[base + g * 8 + u], 1), :] for u in range(8)]
+                groups.append(jnp.concatenate(picked, 0))
+            out[owner, 0:WIRE, at] = jnp.concatenate(groups, 0).T[:WIRE].astype(BF16)
+            return inner
+
+        lax.fori_loop(0, pieces, step, 0, unroll=min(2, pieces))
+        if finished is not None:
+            finished(owner)
         return carry
 
-    lax.fori_loop(0, out.shape[0] * pieces, step, 0, unroll=2)
+    lax.fori_loop(0, out.shape[0], one, 0)
 
 
 def turn_into(got, table):
@@ -341,45 +349,89 @@
     return mem.reshape(MEM * 8, LANES)[pl.ds(i, MEM, stride=8), :]
 
 
-def gru_products(mail, phi, low, w_mail, w_time, w_hid, gi, gh):
-    gi[...] = dot(w_mail[...], mail[...]) + dot(w_time[...], phi[...])
-    gh[...] = dot(w_hid[...], low[...])
-
-
-def gates_at(at, gi, gh, bias, low):
-    gr, gz, gn = (gi[PAD * g : PAD * g + PAD, at] + bias[0, PAD * g : PAD * g + PAD, :] for g in range(3))
-    hr, hz, hn = (gh[PAD * g : PAD * g + PAD, at] + bias[1, PAD * g : PAD * g + PAD, :] for g in range(3))
-    r = sigmoid(gr + hr)
-    z = sigmoid(gz + hz)
+def gate_products(mail, two, w_mail, w_two):
+    both = dot(w_two[...], two)
+    first = both[:GATES] + dot(w_mail[...], mail)
+    return first[:PAD], first[PAD : 2 * PAD], first[2 * PAD :], both[GATES:]
+
+
+def gates_at(at, sums, low, s=None):
+    gr, gz, gn, hn = (x[:, at] for x in sums)
+    r = sigmoid(gr)
+    z = sigmoid(gz)
     n = jnp.tanh(gn + r * hn)
-    s = jnp.concatenate([low[:, at].astype(F32), jnp.zeros((PAD - MEM, LANES), F32)], 0)
+    if s is None:
+        s = low[:, at].astype(F32)
     return r, z, n, hn, s, (1.0 - z) * n + z * s
 
 
-def gru_kernel(
-    index, mail, phi, mem, feat, w_mail, w_time, w_hid, w_feat, bias, sent, s_rows, low, table, gi, gh, nf
-):
-    block = mail.shape[1]
-    step = pl.program_id(0)
-    for i in range(block // LANES):
-        low[:, i * LANES : i * LANES + LANES] = mem_piece(mem, i).astype(BF16)
-    gru_products(mail, phi, low, w_mail, w_time, w_hid, gi, gh)
-    nf[...] = dot(w_feat[...], feat[...])
-
-    def piece(i, carry):
-        start = pl.multiple_of(i * LANES, LANES)
-        at = pl.ds(start, LANES)
-        _, _, _, _, _, renewed = gates_at(at, gi, gh, bias, low)
-        hidden = (renewed + nf[:, at]).astype(BF16).astype(F32)
-        table[pl.ds(pl.multiple_of(step * block + start, LANES), LANES), :] = to_rows(hidden)
-        s_rows[at, :] = to_rows(renewed)
+def gru_kernel(index, flat, mail_in, phi_in, mem_in, feat_in, *refs):
+    wts, rest = refs[: len(WEIGHTS)], refs[len(WEIGHTS) :]
+    sent_out, low_out, s_out = rest[:3]
+    wide, rows, mail, two, mem, feat, s_cols, table, sent, in_sems, out_sems, sent_sems = rest[3:]
+    w_mail, w_two, w_hid, w_feat = wts[:4]
+    nodes = mail.shape[1]
+    half = nodes // 2
+    copies = []
+    for part in range(2):
+        cols = slice(part * half, part * half + half)
+        lines = slice(part * half // LANES, (part + 1) * half // LANES)
+        pairs = [(r.at[:, cols], v.at[:, cols]) for r, v in ((mail_in, mail), (feat_in, feat))]
+        pairs.append((phi_in.at[:, cols], two.at[0:PAD, cols]))
+        pairs.append((mem_in.at[:, lines, :], mem.at[:, lines, :]))
+        copies.append([pltpu.make_async_copy(r, v, in_sems.at[part, i]) for i, (r, v) in enumerate(pairs)])
+        for copy in copies[-1]:
+            copy.start()
+    unpack_weights(flat, *wts, wide, rows)
+    sub = 256
+    real = row_of((PAD, sub)) < MEM
+    ones = (row_of((PAD, sub)) == MEM).astype(F32)
+    short = jnp.zeros((PAD - MEM, sub), F32)
+    for part in range(2):
+        for copy in copies[part]:
+            copy.wait()
+
+        def piece(j, carry):
+            start = pl.multiple_of(j * sub, sub)
+            at = pl.ds(start, sub)
+            lows = []
+            for i in range(sub // LANES):
+                line = j * (sub // LANES) + i
+                lows.append(mem.reshape(MEM * (nodes // LANES), LANES)[pl.ds(line, MEM, stride=nodes // LANES), :])
+            full = jnp.concatenate([jnp.concatenate(lows, 1), short], 0)
+            low_now = full.astype(BF16)
+            two[PAD : 2 * PAD, at] = jnp.where(real, full, ones).astype(BF16)
+            sums = gate_products(mail[:, at], two[:, at], w_mail, w_two)
+            nf = dot(w_feat[...], feat[:, at])
+            for i in range(sub // LANES):
+                here = slice(i * LANES, i * LANES + LANES)
+                _, _, _, _, _, renewed = gates_at(here, sums, low_now)
+                hidden = (renewed + nf[:, here]).astype(BF16).astype(F32)
+                to = pl.ds(pl.multiple_of(start + i * LANES, LANES), LANES)
+                table[to, :] = to_rows(hidden)
+                s_cols[:, to] = renewed[:MEM].astype(BF16)
+            return carry
+
+        lax.fori_loop(part * half // sub, (part + 1) * half // sub, piece, 0, unroll=4)
+    outs = [
+        pltpu.make_async_copy(two.at[PAD : 2 * PAD, :], low_out, out_sems.at[0]),
+        pltpu.make_async_copy(s_cols, s_out, out_sems.at[1]),
+    ]
+    for copy in outs:
+        copy.start()
+
+    def done(owner):
+        return pltpu.make_async_copy(sent.at[owner], sent_out.at[owner], sent_sems.at[owner])
+
+    gather_turned(index, table, sent, lambda owner: done(owner).start())
+
+    def settle(owner, carry):
+        done(owner).wait()
         return carry
 
-    lax.fori_loop(0, block // LANES, piece, 0)
-
-    @pl.when(step == pl.num_programs(0) - 1)
-    def _():
-        gather_turned(index, table, sent)
+    lax.fori_loop(0, sent.shape[0], settle, 0)
+    for copy in outs:
+        copy.wait()
 
 
 BLOCK = 1024
@@ -393,59 +445,94 @@
     return pl.BlockSpec((MEM, BLOCK // LANES, LANES), lambda i: (0, i, 0))
 
 
-def gru_forward(index, mail, phi, mem, feat, wts, shards, slots):
+HBM = pl.BlockSpec(memory_space=pl.ANY)
+
+
+def gru_forward(index, flat, mail, phi, mem, feat, shards, slots):
     rows = mail.shape[1]
-    return pl.pallas_call(
+    shapes = [jax.ShapeDtypeStruct(s, d) for s, d in WEIGHTS]
+    shapes += [
+        jax.ShapeDtypeStruct((shards, WIRE, slots), BF16),
+        jax.ShapeDtypeStruct((PAD, rows), BF16),
+        jax.ShapeDtypeStruct((MEM, rows), BF16),
+    ]
+    got = pl.pallas_call(
         gru_kernel,
-        grid=(rows // BLOCK,),
-        out_shape=(
-            jax.ShapeDtypeStruct((shards, WIRE, slots), BF16),
-            jax.ShapeDtypeStruct((rows, LANES), F32),
-            jax.ShapeDtypeStruct((MEM, rows), BF16),
-        ),
-        in_specs=[SMEM, cols_spec(MAIL), cols_spec(TENC), mem_spec(), cols_spec(NFEAT)] + [VMEM] * 5,
-        out_specs=(VMEM, pl.BlockSpec((BLOCK, LANES), lambda i: (i, 0)), cols_spec(MEM)),
+        out_shape=shapes,
+        in_specs=[SMEM, VMEM] + [HBM] * 4,
+        out_specs=[VMEM] * len(WEIGHTS) + [HBM] * 3,
         scratch_shapes=[
+            pltpu.VMEM((FLAT_ROWS + 16, LANES), F32),
+            pltpu.VMEM((WROWS + 512, LANES), F32),
+            pltpu.VMEM((MAIL, rows), BF16),
+            pltpu.VMEM((2 * PAD, rows), BF16),
+            pltpu.VMEM((MEM, rows // LANES, LANES), F32),
+            pltpu.VMEM((NFEAT, rows), BF16),
+            pltpu.VMEM((MEM, rows), BF16),
             pltpu.VMEM((rows, LANES), F32),
-            pltpu.VMEM((GATES, BLOCK), F32),
-            pltpu.VMEM((GATES, BLOCK), F32),
-            pltpu.VMEM((PAD, BLOCK), F32),
+            pltpu.VMEM((shards, WIRE, slots), BF16),
+            pltpu.SemaphoreType.DMA((2, 4)),
+            pltpu.SemaphoreType.DMA((2,)),
+            pltpu.SemaphoreType.DMA((shards,)),
         ],
         compiler_params=params_of(),
         cost_estimate=pl.CostEstimate(flops=4_000_000_000, bytes_accessed=24_000_000, transcendentals=3_000_000),
-    )(index, mail, phi, mem, feat, *wts[:5])
-
-
-def send_kernel(index, table, notes, out):
+    )(index, flat, mail, phi, mem, feat)
+    return got[: len(WEIGHTS)], *got[len(WEIGHTS) :]
+
+
+def send_kernel(index, s_cols, notes, out, table):
     for owner in range(out.shape[0]):
         out[owner, WIRE:, :] = notes[...]
+    short = jnp.zeros((LANES - MEM, LANES), F32)
+
+    def step(j, carry):
+        at = pl.ds(pl.multiple_of(j * LANES, LANES), LANES)
+        table[at, :] = jnp.concatenate([s_cols[:, at].astype(F32), short], 0).T
+        return carry
+
+    lax.fori_loop(0, table.shape[0] // LANES, step, 0, unroll=8)
     gather_turned(index, table, out)
 
 
-def send_rows(table, index, notes, shards, slots):
+def send_rows(s_cols, index, notes, shards, slots):
     return pl.pallas_call(
         send_kernel,
         out_shape=jax.ShapeDtypeStruct((shards, WIRE + notes.shape[0], slots), BF16),
         in_specs=[SMEM, VMEM, VMEM],
         out_specs=VMEM,
+        scratch_shapes=[pltpu.VMEM((s_cols.shape[1], LANES), F32)],
         compiler_params=params_of(24 * 2**20),
         cost_estimate=pl.CostEstimate(flops=8_000_000, bytes_accessed=6_000_000, transcendentals=0),
-    )(index, table, notes)
-
-
-def partner_kernel(index, got, out, table):
+    )(index, s_cols, notes)
+
+
+def partner_kernel(index, got, out, table, rows):
     turn_into(got, table)
-    gather_loop(index, table, out, index.shape[0])
-
-
-def partner_rows(got, index):
+    gather_loop(index, table, rows, index.shape[0])
+    flag = lane_of((LANES, LANES)) == MEM
+    for i in range(index.shape[0] // LANES):
+        at = slice(i * LANES, i * LANES + LANES)
+        block = jnp.where(flag, 1.0, rows[at, :]).T[:WIRE].astype(BF16)
+
+        def copy(owner, carry, at=at, block=block):
+            out[owner, :, at] = block
+            return carry
+
+        lax.fori_loop(0, out.shape[0], copy, 0)
+
+
+def partner_rows(got, index, shards):
     return pl.pallas_call(
         partner_kernel,
-        out_shape=jax.ShapeDtypeStruct((index.shape[0], LANES), BF16),
+        out_shape=jax.ShapeDtypeStruct((shards, WIRE, index.shape[0]), BF16),
         in_specs=[SMEM, VMEM],
         out_specs=VMEM,
-        scratch_shapes=[pltpu.VMEM((got.shape[0] * got.shape[2], LANES), F32)],
-        compiler_params=params_of(24 * 2**20),
+        scratch_shapes=[
+            pltpu.VMEM((got.shape[0] * got.shape[2], LANES), F32),
+            pltpu.VMEM((index.shape[0], LANES), F32),
+        ],
+        compiler_params=params_of(44 * 2**20),
         cost_estimate=pl.CostEstimate(flops=2_000_000, bytes_accessed=2_000_000, transcendentals=0),
     )(index, got)
 
@@ -479,214 +566,194 @@
 
 
 def factor_kernel(
-    index,
-    flags,
-    mail,
-    phi,
-    low,
-    mem,
-    mail_time,
-    update_time,
-    w_mail,
-    w_time,
-    w_hid,
-    bias,
-    factors,
-    s_cols,
-    mem_new,
-    time_new,
-    placed,
-    gi,
-    gh,
+    mail, phi, low, mem, live_in, mail_time, update_time, w_mail, w_two, factors, mem_new, time_new
 ):
-    step = pl.program_id(0)
-
-    @pl.when(step == 0)
-    def _():
-        count = index.shape[0]
-        if count != placed.shape[0]:
-            placed[...] = jnp.zeros_like(placed)
-        group = 32
-
-        def move(i, carry):
-            for u in range(group):
-                at = i * group + u
-                placed[pl.ds(index[at], 1), :] = jnp.full((1, LANES), flags[at], jnp.int32)
-            return carry
-
-        lax.fori_loop(0, count // group, move, 0)
-
-    gru_products(mail, phi, low, w_mail, w_time, w_hid, gi, gh)
-    for i in range(BLOCK // LANES):
-        at = slice(i * LANES, i * LANES + LANES)
-        r, z, n, hn, s, renewed = gates_at(at, gi, gh, bias, low)
-        live = placed[pl.ds(pl.multiple_of(step * BLOCK + i * LANES, LANES), LANES), :].T[0:1, :] > 0
-        an = (1.0 - z) * (1.0 - n * n)
-        factors[0, :, at] = (an * hn * (r * (1.0 - r)))[:MEM]
-        factors[1, :, at] = ((s - n) * (z * (1.0 - z)))[:MEM]
-        factors[2, :, at] = an[:MEM]
-        factors[3, :, at] = r[:MEM]
-        factors[4, :, at] = z[:MEM]
-        s_cols[:, at] = renewed[:MEM].astype(BF16)
-        value = jnp.where(live, renewed[:MEM], mem_piece(mem, i))
-        mem_new.reshape(MEM * 8, LANES)[pl.ds(i, MEM, stride=8), :] = value
-        time_new[:, at] = jnp.where(live, mail_time[:, at], update_time[:, at])
-
-
-def gru_factors(index, flags, mail, phi, low, mem, mail_time, update_time, wts):
+    sub = 256
+    for j in range(BLOCK // sub):
+        part = slice(j * sub, j * sub + sub)
+        sums = gate_products(mail[:, part], jnp.concatenate([phi[:, part], low[:, part]], 0), w_mail, w_two)
+        for i in range(sub // LANES):
+            there = slice(i * LANES, i * LANES + LANES)
+            at = slice(j * sub + i * LANES, j * sub + i * LANES + LANES)
+            s_low = jnp.where(row_of((PAD, LANES)) < MEM, low[:, at].astype(F32), 0.0)
+            r, z, n, hn, s, renewed = gates_at(there, sums, None, s_low)
+            live = live_in[:, at] > 0.5
+            an = (1.0 - z) * (1.0 - n * n)
+            factors[0, :, at] = (an * hn * (r * (1.0 - r))).astype(BF16)
+            factors[1, :, at] = ((s - n) * (z * (1.0 - z))).astype(BF16)
+            factors[2, :, at] = an.astype(BF16)
+            factors[3, :, at] = r.astype(BF16)
+            factors[4, :, at] = z.astype(BF16)
+            line = (j * sub) // LANES + i
+            value = jnp.where(live, renewed[:MEM], mem_piece(mem, line))
+            mem_new.reshape(MEM * 8, LANES)[pl.ds(line, MEM, stride=8), :] = value
+            time_new[:, at] = jnp.where(live, mail_time[:, at], update_time[:, at])
+
+
+def gru_factors(mail, phi, low, mem, live, mail_time, update_time, wts):
     rows = mail.shape[1]
     return pl.pallas_call(
         factor_kernel,
         grid=(rows // BLOCK,),
         out_shape=(
-            jax.ShapeDtypeStruct((5, MEM, rows), F32),
-            jax.ShapeDtypeStruct((MEM, rows), BF16),
+            jax.ShapeDtypeStruct((5, PAD, rows), BF16),
             jax.ShapeDtypeStruct((MEM, rows // LANES, LANES), F32),
             jax.ShapeDtypeStruct((1, rows), jnp.int32),
         ),
-        in_specs=[SMEM, SMEM, cols_spec(MAIL), cols_spec(TENC), cols_spec(MEM), mem_spec()]
-        + [cols_spec(1)] * 2
-        + [VMEM] * 4,
+        in_specs=[cols_spec(MAIL), cols_spec(PAD), cols_spec(PAD), mem_spec()]
+        + [cols_spec(1)] * 3
+        + [VMEM] * 2,
         out_specs=(
-            pl.BlockSpec((5, MEM, BLOCK), lambda i: (0, 0, i)),
-            cols_spec(MEM),
+            pl.BlockSpec((5, PAD, BLOCK), lambda i: (0, 0, i)),
             mem_spec(),
             cols_spec(1),
         ),
-        scratch_shapes=[
-            pltpu.VMEM((rows, LANES), jnp.int32),
-            pltpu.VMEM((GATES, BLOCK), F32),
-            pltpu.VMEM((GATES, BLOCK), F32),
-        ],
         compiler_params=params_of(),
         cost_estimate=pl.CostEstimate(flops=3_000_000_000, bytes_accessed=34_000_000, transcendentals=3_000_000),
-    )(index, flags, mail, phi, low, mem, mail_time, update_time, wts[0], wts[1], wts[2], wts[4])
+    )(mail, phi, low, mem, live, mail_time, update_time, wts[0], wts[1])
 
 
 def gru_back_kernel(
     index,
     got,
+    w_hid,
+    factors_in,
+    mail_in,
+    phi_in,
+    low_in,
+    feat_in,
+    grads,
+    biases,
+    grad_out,
     factors,
     mail,
-    phi,
-    low,
+    two,
     feat,
-    w_hid,
     mem_grad,
-    grads,
-    biases,
     wide,
     placed,
-    d_in,
-    d_hid,
-    d_low,
-    direct,
+    d_one,
+    d_two,
     a_mail,
-    a_time,
-    a_hid,
+    a_two,
     a_feat,
-    a_bin,
-    a_bhid,
+    in_sems,
+    out_sems,
 ):
-    step = pl.program_id(0)
-
-    @pl.when(step == 0)
-    def _():
-        turn_into(got, wide)
-        count = wide.shape[0]
-        if count != placed.shape[0]:
-            placed[...] = jnp.zeros_like(placed)
-        group = 32
-
-        def move(i, carry):
-            for u in range(group):
-                at = i * group + u
-                placed[pl.ds(index[at], 1), :] = wide[pl.ds(at, 1), :]
-            return carry
-
-        lax.fori_loop(0, count // group, move, 0)
-        for ref in (d_in, d_hid, d_low, a_mail, a_time, a_hid, a_feat, a_bin, a_bhid):
-            ref[...] = jnp.zeros_like(ref)
-
-    for i in range(BLOCK // LANES):
-        at = slice(i * LANES, i * LANES + LANES)
-        d = placed[pl.ds(pl.multiple_of(step * BLOCK + i * LANES, LANES), LANES), :].T[:MEM]
-        dr = d * factors[0, :, at]
-        dz = d * factors[1, :, at]
-        dn = d * factors[2, :, at]
-        dhn = dn * factors[3, :, at]
-        direct[:, at] = d * factors[4, :, at]
-        low_r, low_z = dr.astype(BF16), dz.astype(BF16)
-        d_low[0:MEM, at] = d.astype(BF16)
-        d_in[0:MEM, at] = low_r
-        d_in[PAD : PAD + MEM, at] = low_z
-        d_in[2 * PAD : 2 * PAD + MEM, at] = dn.astype(BF16)
-        d_hid[0:MEM, at] = low_r
-        d_hid[PAD : PAD + MEM, at] = low_z
-        d_hid[2 * PAD : 2 * PAD + MEM, at] = dhn.astype(BF16)
-        a_bin[0:MEM, :] += dr
-        a_bin[PAD : PAD + MEM, :] += dz
-        a_bin[2 * PAD : 2 * PAD + MEM, :] += dn
-        a_bhid[0:MEM, :] += dhn
-    din, dhid = d_in[...], d_hid[...]
-    a_mail[:, :MAIL] += dot(din, mail[...], 1, 1)
-    a_time[:, :TENC] += dot(din, phi[...], 1, 1)
-    a_hid[:, :MEM] += dot(dhid, low[...], 1, 1)
-    a_feat[:, :NFEAT] += dot(d_low[...], feat[...], 1, 1)
-    direct[...] += dot(w_hid[...], dhid, 0, 0)
-    for i in range(BLOCK // LANES):
-        at = slice(i * LANES, i * LANES + LANES)
-        mem_grad.reshape(MEM * 8, LANES)[pl.ds(i, MEM, stride=8), :] = direct[:, at]
-
-    @pl.when(step == pl.num_programs(0) - 1)
-    def _():
-        def turned_back(ref, g):
-            part = ref[PAD * g : PAD * g + PAD, :]
-            return jnp.concatenate([part, jnp.zeros((LANES - PAD, part.shape[1]), F32)], 0).T
-
-        grads[ROW_Q:GRU_ROWS, :] = jnp.zeros((GRU_ROWS - ROW_Q, LANES), F32)
-        for g in range(3):
-            grads[pl.ds(g, MAIL, stride=3), :] = turned_back(a_mail, g)[:MAIL]
-            grads[pl.ds(3 * MAIL + g, TENC, stride=3), :] = turned_back(a_time, g)[:TENC]
-            grads[pl.ds(ROW_HH + g, MEM, stride=3), :] = turned_back(a_hid, g)[:MEM]
-        grads[ROW_NF:ROW_Q, :] = turned_back(a_feat, 0)[:NFEAT]
-        sums = []
-        for ref, g in ((a_bin, 0), (a_bin, 1), (a_bin, 2), (a_bin, 0), (a_bin, 1), (a_bhid, 0)):
-            sums.append(jnp.sum(turned_back(ref, g), 0, keepdims=True))
-        biases[...] = jnp.concatenate(sums + [jnp.zeros((2, LANES), F32)], 0)
+    pairs = ((factors_in, factors), (mail_in, mail), (phi_in, two.at[0:PAD, :]), (low_in, two.at[PAD : 2 * PAD, :]), (feat_in, feat))
+    copies = [pltpu.make_async_copy(r, v, in_sems.at[i]) for i, (r, v) in enumerate(pairs)]
+    for copy in copies:
+        copy.start()
+    turn_into(got, wide)
+    count = wide.shape[0]
+    if count != placed.shape[0]:
+        placed[...] = jnp.zeros_like(placed)
+    group = 32
+
+    def move(i, carry):
+        for u in range(group):
+            at = i * group + u
+            placed[pl.ds(index[at], 1), :] = wide[pl.ds(at, 1), :]
+        return carry
+
+    lax.fori_loop(0, count // group, move, 0)
+    for ref in (a_mail, a_two, a_feat):
+        ref[...] = jnp.zeros_like(ref)
+    for copy in copies:
+        copy.wait()
+    nodes = mail.shape[1]
+    lines = nodes // LANES
+
+    def out_copy(step):
+        part = pl.ds(step * (BLOCK // LANES), BLOCK // LANES)
+        return pltpu.make_async_copy(mem_grad.at[:, part, :], grad_out.at[:, part, :], out_sems.at[step])
+
+    def block(step, d_all):
+        start = pl.multiple_of(step * BLOCK, BLOCK)
+        for i in range(BLOCK // LANES):
+            at = slice(i * LANES, i * LANES + LANES)
+            there = pl.ds(pl.multiple_of(start + i * LANES, LANES), LANES)
+            d = placed[there, :].T[:PAD]
+            dn = d * factors[2, :, there]
+            for part, value in enumerate(
+                (d * factors[0, :, there], d * factors[1, :, there], dn, dn * factors[3, :, there], d)
+            ):
+                d_all[PAD * part : PAD * part + PAD, at] = value.astype(BF16)
+        gates, dlow = d_all[0 : 4 * PAD, :], d_all[4 * PAD :, :]
+        there = pl.ds(start, BLOCK)
+        a_mail[:, :MAIL] += dot(gates[:GATES], mail[:, there], 1, 1)
+        a_two[:, : 2 * PAD] += dot(gates, two[:, there], 1, 1)
+        a_feat[:, :NFEAT] += dot(dlow, feat[:, there], 1, 1)
+        direct = dlow.astype(F32) * factors[4, :, there].astype(F32) + dot(w_hid[...], gates, 0, 0)
+        for i in range(BLOCK // LANES):
+            line = pl.ds(step * (BLOCK // LANES) + i, MEM, stride=lines)
+            mem_grad.reshape(MEM * lines, LANES)[line, :] = direct[:MEM, i * LANES : i * LANES + LANES]
+        out_copy(step).start()
+
+    def two_blocks(i, carry):
+        block(2 * i, d_one)
+        block(2 * i + 1, d_two)
+        return carry
+
+    lax.fori_loop(0, nodes // BLOCK // 2, two_blocks, 0)
+
+    def turned_back(block):
+        return jnp.concatenate([block, jnp.zeros((LANES - PAD, block.shape[1]), F32)], 0).T
+
+    grads[ROW_Q:GRU_ROWS, :] = jnp.zeros((GRU_ROWS - ROW_Q, LANES), F32)
+    lines_of = []
+    for g in range(3):
+        rows = slice(PAD * g, PAD * g + PAD)
+        grads[pl.ds(g, MAIL, stride=3), :] = turned_back(a_mail[rows, :])[:MAIL]
+        both = turned_back(a_two[rows, :])
+        grads[pl.ds(3 * MAIL + g, TENC, stride=3), :] = both[:TENC]
+        lines_of.append(both[MEM : MEM + 1])
+        if g == 2:
+            both = turned_back(a_two[GATES:, :])
+        wide[0 : 2 * LANES, :] = both
+        grads[pl.ds(ROW_HH + g, MEM, stride=3), :] = wide[PAD : PAD + MEM, :]
+    hidden_bias = wide[PAD + MEM : PAD + MEM + 1, :]
+    grads[ROW_NF:ROW_Q, :] = turned_back(a_feat[...])[:NFEAT]
+    sums = lines_of + lines_of[:2] + [hidden_bias]
+    biases[...] = jnp.concatenate(sums + [jnp.zeros((2, LANES), F32)], 0)
+
+    def settle(step, carry):
+        out_copy(step).wait()
+        return carry
+
+    lax.fori_loop(0, nodes // BLOCK, settle, 0)
 
 
 def gru_backward(index, got, factors, mail, phi, low, feat, wts):
     rows = mail.shape[1]
     return pl.pallas_call(
         gru_back_kernel,
-        grid=(rows // BLOCK,),
         out_shape=(
-            jax.ShapeDtypeStruct((MEM, rows // LANES, LANES), F32),
             jax.ShapeDtypeStruct((GRU_ROWS, LANES), F32),
             jax.ShapeDtypeStruct((8, LANES), F32),
+            jax.ShapeDtypeStruct((MEM, rows // LANES, LANES), F32),
         ),
-        in_specs=[SMEM, VMEM, pl.BlockSpec((5, MEM, BLOCK), lambda i: (0, 0, i))]
-        + [cols_spec(r) for r in (MAIL, TENC, MEM, NFEAT)]
-        + [VMEM],
-        out_specs=(mem_spec(), VMEM, VMEM),
+        in_specs=[SMEM, VMEM, VMEM] + [HBM] * 5,
+        out_specs=(VMEM, VMEM, HBM),
         scratch_shapes=[
+            pltpu.VMEM((5, PAD, rows), BF16),
+            pltpu.VMEM((MAIL, rows), BF16),
+            pltpu.VMEM((2 * PAD, rows), BF16),
+            pltpu.VMEM((NFEAT, rows), BF16),
+            pltpu.VMEM((MEM, rows // LANES, LANES), F32),
             pltpu.VMEM((got.shape[0] * got.shape[2], LANES), F32),
             pltpu.VMEM((rows, LANES), F32),
-            pltpu.VMEM((GATES, BLOCK), BF16),
-            pltpu.VMEM((GATES, BLOCK), BF16),
-            pltpu.VMEM((PAD, BLOCK), BF16),
-            pltpu.VMEM((MEM, BLOCK), F32),
+            pltpu.VMEM((5 * PAD, BLOCK), BF16),
+            pltpu.VMEM((5 * PAD, BLOCK), BF16),
             pltpu.VMEM((GATES, 512), F32),
-            pltpu.VMEM((GATES, LANES), F32),
-            pltpu.VMEM((GATES, LANES), F32),
+            pltpu.VMEM((4 * PAD, 256), F32),
             pltpu.VMEM((PAD, 512), F32),
-            pltpu.VMEM((GATES, LANES), F32),
-            pltpu.VMEM((PAD, LANES), F32),
+            pltpu.SemaphoreType.DMA((5,)),
+            pltpu.SemaphoreType.DMA((rows // BLOCK,)),
         ],
         compiler_params=params_of(),
         cost_estimate=pl.CostEstimate(flops=5_000_000_000, bytes_accessed=36_000_000, transcendentals=0),
-    )(index, got, factors, mail, phi, low, feat, wts[2])
+    )(index, got, wts[2], factors, mail, phi, low, feat)
 
 
 def attention_kernel(
@@ -993,7 +1060,7 @@
         + [pltpu.VMEM((SECT, LANES), BF16) for _ in range(NBR + 1)],
         compiler_params=params_of(),
         cost_estimate=pl.CostEstimate(flops=9_000_000_000, bytes_accessed=20_000_000, transcendentals=1_000_000),
-    )(index, got, edges, edges, edges, codes, codes, codes, weight, *wts[5:])
+    )(index, got, edges, edges, edges, codes, codes, codes, weight, *wts[4:])
 
 
 def pack_kernel(gru, bias, att, losses, out, rows):
@@ -1036,109 +1103,138 @@
     )(gru, bias, att, losses)
 
 
-def edge_kernel(edges, stamps, out, stage):
-    stage[...] = jnp.zeros_like(stage)
-    stage[EDGE + 1 : EDGE + 2, :] = jnp.ones((1, EV), F32)
-    stage[0:EDGE, :] = edges[0].astype(F32)
-    stage[EDGE : EDGE + 1, :] = stamps[0].astype(F32)
-    for part in range(2):
-        out[0, part] = stage[LANES * part : LANES * part + LANES, :].T
-
-
-def edge_tables(edges, stamps):
-    senders = edges.shape[0]
-    return pl.pallas_call(
-        edge_kernel,
-        grid=(senders,),
-        out_shape=jax.ShapeDtypeStruct((senders, 2, EV, LANES), F32),
-        in_specs=[
-            pl.BlockSpec((1, EDGE, EV), lambda i: (i, 0, 0)),
-            pl.BlockSpec((1, 1, EV), lambda i: (i, 0, 0)),
-        ],
-        out_specs=pl.BlockSpec((1, 2, EV, LANES), lambda i: (i, 0, 0, 0)),
-        scratch_shapes=[pltpu.VMEM((2 * LANES, EV), F32)],
-        compiler_params=params_of(16 * 2**20),
-        cost_estimate=pl.CostEstimate(flops=3_000_000, bytes_accessed=6_000_000, transcendentals=0),
-    )(edges, stamps)
-
-
-def mail_kernel(
-    starts, rows, events, partner, far, own, mailbox, mail_time, mail_new, time_new, near, kept, lines
+NODES = 2048
+
+
+def each_message(starts, sender, body_of):
+    first, end = starts[2 * sender], starts[2 * sender + 1]
+
+    def move(i, carry):
+        for u in range(8):
+            body_of(jnp.minimum(first + i * 8 + u, end - 1))
+        return carry
+
+    lax.fori_loop(0, (end - first + 7) // 8, move, 0)
+
+
+def after_first(count):
+    return pl.BlockSpec((count, NODES), lambda i: (0, jnp.maximum(i - 1, 0)))
+
+
+def edge_kernel(
+    starts, rows, events, edges, stamps, own, mailbox, mail_time, mail_new, time_new, stage, far, kept, lines
 ):
     step = pl.program_id(0)
-    senders = rows.shape[0] // (2 * EV)
 
     @pl.when(step == 0)
     def _():
-        kept[2] = jnp.zeros(kept.shape[1:], F32)
-
-    @pl.when(step < senders)
+        kept[1] = jnp.zeros(kept.shape[1:], F32)
+        stage[...] = jnp.zeros_like(stage)
+        stage[EDGE + 1 : EDGE + 2, :] = jnp.ones((1, EV), F32)
+
+        def sender(s, carry):
+            stage[0:EDGE, :] = edges[s].astype(F32)
+            stage[EDGE : EDGE + 1, :] = stamps[s].astype(F32)
+            for part in range(2):
+                far[part] = stage[LANES * part : LANES * part + LANES, :].T
+
+            def one(i):
+                place = s * 2 * EV + i
+                to = pl.ds(rows[place], 1)
+                event = pl.ds(events[place], 1)
+                kept[0, to, :] = far[0, event, :]
+                kept[1, to, :] = far[1, event, :]
+
+            each_message(starts, s, one)
+            return carry
+
+        lax.fori_loop(0, edges.shape[0], sender, 0)
+
+    @pl.when(step > 0)
     def _():
-        near[...] = partner[0].astype(F32)
-
-        def move(i, carry):
-            place = step * 2 * EV + i
-            to = pl.ds(rows[place], 1)
-            event = pl.ds(events[place], 1)
-            kept[0, to, :] = near[pl.ds(i, 1), :]
-            kept[1, to, :] = far[0, 0, event, :]
-            kept[2, to, :] = far[0, 1, event, :]
-            return carry
-
-        lax.fori_loop(starts[2 * step], starts[2 * step + 1], move, 0)
-
-    @pl.when(step >= senders)
-    def _():
-        block = mailbox.shape[1]
-        at = pl.ds(pl.multiple_of((step - senders) * block, LANES), block)
-        last = kept[2, at, :].T
+        at = pl.ds(pl.multiple_of((step - 1) * NODES, LANES), NODES)
+        last = kept[1, at, :].T
         stamp = EDGE - LANES
         has = last[stamp + 1 : stamp + 2, :] > 0.5
         lines[0:MEM, :] = own[...].astype(F32)
-        lines[MEM : 2 * MEM, :] = kept[0, at, :].T[0:MEM]
-        lines[2 * MEM : 2 * MEM + LANES, :] = kept[1, at, :].T
+        lines[2 * MEM : 2 * MEM + LANES, :] = kept[0, at, :].T
         lines[2 * MEM + LANES : MAIL, :] = last[0:stamp]
         mail_new[...] = jnp.where(has, lines[0:MAIL, :], mailbox[...].astype(F32)).astype(BF16)
         time_new[...] = jnp.where(has, last[stamp : stamp + 1, :].astype(jnp.int32), mail_time[...])
 
 
-def deliver(starts, rows, events, partner, far, own, mailbox, mail_time):
-    senders = partner.shape[0]
+def deliver_edges(starts, rows, events, edges, stamps, own, mailbox, mail_time):
     nodes = mailbox.shape[1]
-    block = 1024
-
-    def sender(i):
-        return (jnp.minimum(i, senders - 1), 0, 0)
-
-    def cols(count):
-        return pl.BlockSpec((count, block), lambda i: (0, jnp.maximum(i - senders, 0)))
-
     return pl.pallas_call(
-        mail_kernel,
-        grid=(senders + nodes // block,),
+        edge_kernel,
+        grid=(1 + nodes // NODES,),
         out_shape=(
             jax.ShapeDtypeStruct((MAIL, nodes), BF16),
             jax.ShapeDtypeStruct((1, nodes), jnp.int32),
         ),
-        in_specs=[
-            SMEM,
-            SMEM,
-            SMEM,
-            pl.BlockSpec((1, 2 * EV, LANES), sender),
-            pl.BlockSpec((1, 2, EV, LANES), lambda i: (jnp.minimum(i, senders - 1), 0, 0, 0)),
-            cols(MEM),
-            cols(MAIL),
-            cols(1),
+        in_specs=[SMEM, SMEM, SMEM, VMEM, VMEM]
+        + [after_first(MEM), after_first(MAIL), after_first(1)],
+        out_specs=(after_first(MAIL), after_first(1)),
+        scratch_shapes=[
+            pltpu.VMEM((2 * LANES, EV), F32),
+            pltpu.VMEM((2, EV, LANES), F32),
+            pltpu.VMEM((2, nodes, LANES), F32),
+            pltpu.VMEM((MAIL + 6, NODES), F32),
         ],
-        out_specs=(cols(MAIL), cols(1)),
+        compiler_params=params_of(),
+        cost_estimate=pl.CostEstimate(flops=20_000_000, bytes_accessed=16_000_000, transcendentals=0),
+    )(starts, rows, events, edges, stamps, own, mailbox, mail_time)
+
+
+def partner_into_kernel(starts, rows, partner, mailbox, mail_new, near, kept, lines):
+    step = pl.program_id(0)
+
+    @pl.when(step == 0)
+    def _():
+        kept[...] = jnp.zeros_like(kept)
+        short = jnp.zeros((LANES - WIRE, LANES), F32)
+
+        def sender(s, carry):
+            for i in range(2 * EV // LANES):
+                at = slice(i * LANES, i * LANES + LANES)
+                near[at, :] = jnp.concatenate([partner[s, :, at].astype(F32), short], 0).T
+
+            def one(i):
+                kept[pl.ds(rows[s * 2 * EV + i], 1), :] = near[pl.ds(i, 1), :]
+
+            each_message(starts, s, one)
+            return carry
+
+        lax.fori_loop(0, partner.shape[0], sender, 0)
+
+    @pl.when(step > 0)
+    def _():
+        at = pl.ds(pl.multiple_of((step - 1) * NODES, LANES), NODES)
+        turned = kept[at, :].T
+        has = turned[MEM : MEM + 1, :] > 0.5
+        lines[...] = mailbox[...].astype(F32)
+        lines[MEM : 2 * MEM, :] = jnp.where(has, turned[0:MEM], lines[MEM : 2 * MEM, :])
+        mail_new[...] = lines[...].astype(BF16)
+
+
+def deliver_partners(starts, rows, partner, mailbox):
+    nodes = mailbox.shape[1]
+    upper = 208
+    return pl.pallas_call(
+        partner_into_kernel,
+        grid=(1 + nodes // NODES,),
+        out_shape=jax.ShapeDtypeStruct((MAIL, nodes), BF16),
+        in_specs=[SMEM, SMEM, VMEM, after_first(upper)],
+        out_specs=after_first(upper),
         scratch_shapes=[
             pltpu.VMEM((2 * EV, LANES), F32),
-            pltpu.VMEM((3, nodes, LANES), F32),
-            pltpu.VMEM((MAIL + 6, block), F32),
+            pltpu.VMEM((nodes, LANES), F32),
+            pltpu.VMEM((upper, NODES), F32),
         ],
-        compiler_params=params_of(44 * 2**20),
-        cost_estimate=pl.CostEstimate(flops=20_000_000, bytes_accessed=16_000_000, transcendentals=0),
-    )(starts, rows, events, partner, far, own, mailbox, mail_time)
+        input_output_aliases={3: 0},
+        compiler_params=params_of(),
+        cost_estimate=pl.CostEstimate(flops=10_000_000, bytes_accessed=8_000_000, transcendentals=0),
+    )(starts, rows, partner, mailbox)
 
 
 def flip(x, axis, mask):
@@ -1167,23 +1263,37 @@
     return parts[0]
 
 
-def gather_params(x, between):
-    shape = x.shape
-    axes = []
-    for number, (axis, low, size) in enumerate(rounds()):
-        parts = [x] + [flip(x, axis, low * m) for m in range(1, size)]
-        parts = between(number, x, parts)
-        here = place_in(axis, low, size)
-        key = (axis == "node", -low)
+def gather_first(x, lines, between):
+    grown = [[x, []], [lines, []]]
+
+    def grow(entry, key, here, parts):
+        x, axes = entry
         at = sum(1 for k in axes if k < key)
         axes.append(key)
         axes.sort()
-        out = jnp.zeros(x.shape[:at] + (size,) + x.shape[at:], x.dtype)
+        out = jnp.zeros(x.shape[:at] + (len(parts),) + x.shape[at:], x.dtype)
         for m, part in enumerate(parts):
             to = jnp.bitwise_xor(here, m)
             out = lax.dynamic_update_slice_in_dim(out, jnp.expand_dims(part, at), to, at)
-        x = out
-    return x.reshape((-1,) + shape[1:])
+        entry[0] = out
+
+    for number, (axis, low, size) in enumerate(rounds()):
+        here = place_in(axis, low, size)
+        key = (axis == "node", -low)
+        x, lines = grown[0][0], grown[1][0]
+        if number == 0:
+            both = jnp.concatenate([x, lines], 0)
+            got = [flip(both, axis, low * m) for m in range(1, size)]
+            parts = [x] + [g[: x.shape[0]] for g in got]
+            others = [lines] + [g[x.shape[0] :] for g in got]
+        else:
+            parts = [x] + [flip(x, axis, low * m) for m in range(1, size)]
+            others = [lines] + [flip(lines, axis, low * m) for m in range(1, size)] if axis == "node" else None
+        parts = between(number, x, parts)
+        grow(grown[0], key, here, parts)
+        if others is not None:
+            grow(grown[1], key, here, others)
+    return [g[0] for g in grown]
 
 
 def scatter_sum(x, between):
@@ -1274,22 +1384,24 @@
 
     def between(number, x, parts):
         if number == last - 1:
-            early["asked"] = swap(after(wanted_or_dead, x))
-            early["codes"] = time_codes(after(mail_time - update_time, x))
-            *parts, early["asked"], early["codes"] = lax.optimization_barrier(
-                (*parts, early["asked"], early["codes"])
-            )
-        if number == last:
-            early["edges"] = swap(jnp.broadcast_to(after(edge_sent, x), (shards,) + edge_sent.shape))
+            edges = after(edge_sent, x)
+            early["edges"] = swap(jnp.broadcast_to(edges, (shards,) + edges.shape))
+            early["codes"] = time_codes(after(mail_time - update_time, x), PAD)
+            *parts, early["codes"] = lax.optimization_barrier((*parts, early["codes"]))
         return parts
 
-    flat = gather_params(params.astype(BF16).reshape(1, -1, LANES), between).reshape(-1, LANES)
-    asked = early["asked"].reshape(-1)
-    flags = (asked < rows).astype(jnp.int32)
+    digits = jnp.stack([wanted_or_dead // 128, wanted_or_dead % 128]).astype(BF16)
+    flat, asked = gather_first(
+        params.astype(BF16).reshape(-1, LANES), digits.reshape(-1, LANES), between
+    )
+    flat = flat.reshape(-1, LANES)
+    asked = asked.reshape(shards, 2, shards, slots)
+    asked = lax.dynamic_slice_in_dim(asked, me, 1, 2).astype(F32).astype(jnp.int32)
+    asked = (asked[:, 0] * 128 + asked[:, 1]).reshape(-1)
+    alive = asked < rows
     asked = asked % rows
     codes_m = early["codes"][0]
-    wts = weights_of(flat)
-    h_sent, s_rows, low = gru_forward(asked, mail_cols, codes_m, mem_cols, feat_cols, wts, shards, slots)
+    wts, h_sent, low, s_cols = gru_forward(asked, flat, mail_cols, codes_m, mem_cols, feat_cols, shards, slots)
     h_got = swap(h_sent)
 
     codes_n = time_codes(nbr_dt[0, 0].T)
@@ -1305,7 +1417,7 @@
     digits = jnp.concatenate([notes // 128, notes % 128]).astype(BF16)
     lines = -(-digits.shape[0] // (8 * slots)) * 8
     digits = jnp.pad(digits, (0, lines * slots - digits.shape[0])).reshape(lines, slots)
-    s_sent = send_rows(s_rows, asked, digits, shards, slots)
+    s_sent = send_rows(s_cols, asked, digits, shards, slots)
     h_got, s_sent, codes_n, edges_all, partner_slot, index = lax.optimization_barrier(
         (h_got, s_sent, codes_n, edges_all, partner_slot, index)
     )
@@ -1314,18 +1426,27 @@
     d_sent, s_got, low = lax.optimization_barrier((d_sent, s_got, low))
     d_got = swap(d_sent)
 
-    factors, s_cols, mem_new, upd_new = gru_factors(
-        asked, flags, mail_cols, codes_m, low, mem_cols, mail_time, update_time, wts
+    upper = (jnp.arange(rows // LANES, dtype=jnp.int32)[:, None] == (asked // LANES)[None, :]) & alive[None, :]
+    lower = (asked % LANES)[:, None] == jnp.arange(LANES, dtype=jnp.int32)[None, :]
+    live = dot(upper.astype(BF16), lower.astype(BF16)).reshape(1, rows)
+    factors, mem_new, upd_new = gru_factors(
+        mail_cols, codes_m, low, mem_cols, live, mail_time, update_time, wts
     )
-    partner = partner_rows(s_got, partner_slot)
+    partner = partner_rows(s_got, partner_slot, shards)
     digits = s_got[:, WIRE:, :].reshape(shards, -1)[:, : 2 * notes.shape[0]].astype(F32).astype(jnp.int32)
     notes = digits[:, : notes.shape[0]] * 128 + digits[:, notes.shape[0] :]
     stamps = notes[:, 4 * EV : 5 * EV].reshape(shards, 1, EV)
-    far = edge_tables(edges_all, stamps)
-    partner = jnp.broadcast_to(partner[None], (shards,) + partner.shape)
-    d_got, factors, partner, far = lax.optimization_barrier((d_got, factors, partner, far))
+    events_of = notes[:, 2 * EV : 4 * EV].reshape(-1)
+    rows_of = notes[:, : 2 * EV].reshape(-1)
+    starts = lax.dynamic_slice_in_dim(notes[:, 5 * EV :], me, 2, 1).reshape(-1)
+    mail_new, stamp_new = deliver_edges(
+        starts, rows_of, events_of, edges_all, stamps, s_cols, mail_cols, mail_time
+    )
+    d_got, factors, partner, mail_new, starts, rows_of = lax.optimization_barrier(
+        (d_got, factors, partner, mail_new, starts, rows_of)
+    )
     partner_got = swap(partner)
-    mem_grad, gru_grads, bias_grads = gru_backward(
+    gru_grads, bias_grads, mem_grad = gru_backward(
         asked, d_got, factors, mail_cols, codes_m, low, feat_cols, wts
     )
     packed = pack(gru_grads, bias_grads, att_grads, losses)[:FLAT_ROWS]
@@ -1333,17 +1454,12 @@
 
     def during(number, x, parts):
         if number == 1:
-            events_of = notes[:, 2 * EV : 4 * EV].reshape(-1)
-            rows_of = notes[:, : 2 * EV].reshape(-1)
-            starts = lax.dynamic_slice_in_dim(notes[:, 5 * EV :], me, 2, 1).reshape(-1)
-            mail = deliver(
-                starts, rows_of, events_of, after(partner_got, x), far, s_cols, mail_cols, mail_time
-            )
-            *parts, late["mail"], late["stamp"] = lax.optimization_barrier((*parts, *mail))
+            mail = deliver_partners(starts, rows_of, after(partner_got, x), mail_new)
+            *parts, late["mail"] = lax.optimization_barrier((*parts, mail))
         return parts
 
     shard = scatter_sum(packed, during)
-    mail_new, stamp_new = late["mail"], late["stamp"]
+    mail_new = late["mail"]
 
     number = lax.axis_index("batch") * shards + me
     size = shard.shape[0] * LANES

time: 332 us -> 300 us (0.904)
  Pallas kernels: 200 us -> 183 us
  local copies, waits for them, and re-layouts: 25 us -> 18.5 us
  starting transfers between devices: 53.4 us -> 49.1 us
  other arithmetic: 15.5 us -> 11.9 us
    pallas_call x1, Pallas kernels: 28 us -> 15.4 us  [gru_factors(): pl.pallas_call(factor_kernel, grid=(rows // BLOCK,), out_shape=(jax.Shape...]
    unnamed x67 -> x60, local copies, waits for them, and re-layouts: 17.1 us -> 10.4 us
    pallas_call x8 -> x7, Pallas kernels: 95.3 us -> 89.6 us  [the longest x1 27.6 us: gru_forward(): pl.pallas_call(gru_kernel, out_shape=shapes, in_specs=[SMEM, VMEM] + [HBM...]
    all_to_all x6 -> x5, waiting for transfers between devices: 16.3 us -> 13.5 us  [swap(): return lax.all_to_all(x, 'node', split_axis=0, concat_axis=0, tiled=True)]
    all_to_all x6 -> x5, starting transfers between devices: 25.6 us -> 23.4 us  [swap(): return lax.all_to_all(x, 'node', split_axis=0, concat_axis=0, tiled=True)]
    ppermute x21 -> x22, starting transfers between devices: 27.8 us -> 25.8 us  [flip(): lax.ppermute(x, axis, [(i, i ^ mask) for i in range(lax.axis_size(axis))])]
    ppermute x21 -> x22, waiting for transfers between devices: 16.4 us -> 17.1 us  [flip(): lax.ppermute(x, axis, [(i, i ^ mask) for i in range(lax.axis_size(axis))])]
  transfers between devices with their start and end apart: 27 -> 27, of which waited for: 15 -> 14; matrix products, arithmetic and copies ran while one was open for 5% -> 7% of each run, Pallas kernels for 61% -> 61%
where the time goes in v3:
time: 300 us; the launch traced here: 299 us
  Pallas kernels  183 us (61%)
  starting transfers between devices  49.1 us (16%)
  waiting for transfers between devices  30.6 us (10%)
  local copies, waits for them, and re-layouts  18.5 us (6%)
  other arithmetic  11.9 us (4%)
  between operations  3.37 us (1%)
    pallas_call x1, Pallas kernels, attention(): pl.pallas_call(attention_kernel, grid=(blocks,), out_shape=(jax.ShapeDtyp...  58.6 us
    pallas_call x1, Pallas kernels, gru_forward(): pl.pallas_call(gru_kernel, out_shape=shapes, in_specs=[SMEM, VMEM] + [HBM...  27.6 us
    ppermute x22, starting transfers between devices, flip(): lax.ppermute(x, axis, [(i, i ^ mask) for i in range(lax.axis_size(axis))])  25.8 us
    pallas_call x1, Pallas kernels, gru_backward(): pl.pallas_call(gru_back_kernel, out_shape=(jax.ShapeDtypeStruct((GRU_ROWS...  23.8 us
    all_to_all x5, starting transfers between devices, swap(): return lax.all_to_all(x, 'node', split_axis=0, concat_axis=0, tiled=True)  23.4 us
    ppermute x22, waiting for transfers between devices, flip(): lax.ppermute(x, axis, [(i, i ^ mask) for i in range(lax.axis_size(axis))])  17.1 us
    pallas_call x1, Pallas kernels, gru_factors(): pl.pallas_call(factor_kernel, grid=(rows // BLOCK,), out_shape=(jax.Shape...  15.4 us
    all_to_all x5, waiting for transfers between devices, swap(): return lax.all_to_all(x, 'node', split_axis=0, concat_axis=0, tiled=True)  13.5 us
  transfers between devices with their start and end apart: 27, of which 14 were waited for; matrix products, arithmetic and copies ran while one was open for 7% of the time, Pallas kernels for 61%

profile of v3, /device:TPU:0, one launch (start us, length us, event | category | flops | bytes accessed | tf_op | source)
XLA Modules:
  0.0 298.9 jit_solution(7734392609516610946)
XLA Ops:
  0.6 0.9 add_select_fusion.4
  1.6 0.8 convert_bitcast_fusion
  2.4 3.1 %collective-permute-start = (bf16[216,128]{1,0:T(8,128)(2,1)S(1)}, bf16[216,128]{1,0:T(8,128)(2,1)S(1)}, u32[]{:S(2)}, u32[]{:S(2)}) collective-permute-start(bf16[216,128]{1,0:T(8,128)(2,1)S(1)} %pad_maximum_fusion), channel_id=1, source_target_pairs={{0,2},{1,3},{2,0},{3,1},{4,6},{5,7},{6,4},{7,5},{8,10},{9,11},{10,... | collective-permute-start | bytes 165896 | tf_op jit(solution)/shard_map/ppermute | solution.py:1241
  5.4 2.6 collective-permute-start.1
  8.1 0.8 bitcast_dynamic-update-slice_fusion.8
  9.0 0.8 sub.43.delta
  9.9 1.7 collective-permute-done.1
  11.6 2.4 collective-permute-done.2
  14.0 1.5 collective-permute-start.4
  15.5 1.5 collective-permute-start.5
  17.6 2.2 broadcast_in_dim.137
  19.8 3.7 %all-to-all-start.1 = ((bf16[8,186,512]{2,1,0:T(8,128)(2,1)}), bf16[8,186,512]{2,1,0:T(8,128)(2,1)S(1)}, u32[]{:S(2)}, u32[]{:S(2)}) async-start(bf16[8,186,512]{2,1,0:T(8,128)(2,1)} %broadcast_in_dim.137), calls=%async_computation.1 | async-start | bytes 3145728 | tf_op jit(solution)/shard_map/all_to_all | solution.py:1328
  23.6 3.5 %shard_map.274 = bf16[1,112,8192]{2,1,0:T(8,128)(2,1)S(1)} custom-call(s32[1,8192]{1,0:T(1,128)S(1)} %sub.43.delta, f32[100,128]{1,0:T(8,128)S(1)} %copy-done.7), custom_call_target="tpu_custom_call" | custom-call | flops 24576000 | bytes 1638400 | tf_op jit(solution)/shard_map/pallas_call | solution.py:165
  27.1 1.2 copy-done
  29.5 0.7 add_select_fusion.1
  30.5 1.0 bitcast_dynamic-update-slice_fusion.1
  31.5 0.8 copy-done.13
  32.4 27.6 %shard_map.275 = (bf16[336,386]{1,0:T(8,128)(2,1)}, bf16[448,224]{1,0:T(8,128)(2,1)}, bf16[448,112]{1,0:T(8,128)(2,1)}, bf16[112,413]{1,0:T(8,128)(2,1)}, bf16[2...) custom-call(s32[8192]{0:T(1024)} %get-tuple-element.191.index, ...), custom_call_target="tpu_custom_call" | custom-call | flops 4000000000 | bytes 24000000 | tf_op jit(solution)/shard_map/pallas_call | solution.py:459
  60.0 1.3 all-to-all-done.1.edges
  61.3 4.4 %all-to-all-start = ((bf16[8,104,1024]{2,1,0:T(8,128)(2,1)}), bf16[8,104,1024]{2,1,0:T(8,128)(2,1)}, u32[]{:S(2)}, u32[]{:S(2)}) async-start(bf16[8,104,1024]{2,1,0:T(8,128)(2,1)} %get-tuple-element.80), calls=%async_computation | async-start | bytes 3407872 | tf_op jit(solution)/shard_map/all_to_all | solution.py:1328
  66.7 4.4 %sort.10 = (s32[1024]{0:T(1024)}, s32[1024]{0:T(1024)}) sort(s32[1024]{0:T(1024)S(1)} %iota_add_fusion, s32[1024]{0:T(1024)S(1)} %iota.44), dimensions={0}, to_apply=%region_2.3 | sort | flops 10240 | bytes 16384 | tf_op jit(solution)/shard_map/sort | solution.py:1410
  71.1 6.3 %shard_map.276 = (s32[1024]{0:T(1024)}, s32[1024]{0:T(1024)}, s32[1024]{0:T(1024)}) custom-call(s32[1024]{0:T(1024)} %get-tuple-element.82.ordered, s32[1024]{0:T(1024)} %bitcast.210, s32[8192]{0:T(1024)} %bitcast.206), custom_call_target="tpu_custom_call" | custom-call | flops 4000000 | bytes 60000 | tf_op jit(solution)/shard_map/pallas_call | solution.py:558
  77.4 0.9 convert_reduce_fusion
  78.3 0.7 fusion.30
  79.5 0.7 reshape.416.index
  80.1 6.4 %shard_map.278.p0.p1.p2 = bf16[10,100,1536]{2,1,0:T(8,128)(2,1)S(1)} custom-call(s32[10,1536]{1,0:T(8,128)S(1)} %bitcast.183, f32[100,128]{1,0:T(8,128)S(1)} %copy-done.7), custom_call_target="tpu_custom_call" | custom-call | flops 46080000 | bytes 3072000 | tf_op jit(solution)/shard_map/pallas_call | solution.py:165
  86.5 1.7 copy-done.3
  88.2 10.9 %shard_map.277 = bf16[8,112,1024]{2,1,0:T(8,128)(2,1)S(1)} custom-call(s32[8192]{0:T(1024)S(1)} %copy-done.6, bf16[100,8192]{1,0:T(8,128)(2,1)S(1)} %copy-done.2, bf16[8,1024]{1,0:T(8,128)(2,1)S(1)} %reshape.412.notes), custom_call_target="tpu_custom_call" | custom-call | flops 8000000 | bytes 6000000 | tf_op jit(solution)/shard_map/pallas_call | solution.py:499
  99.2 1.2 copy-done.1
  100.4 6.0 %all-to-all-done.got = bf16[8,104,1024]{2,1,0:T(8,128)(2,1)} async-done(((bf16[8,104,1024]{2,1,0:T(8,128)(2,1)}), bf16[8,104,1024]{2,1,0:T(8,128)(2,1)}, u32[]{:S(2)}, u32[]{:S(2)}) %all-to-all-start) | async-done | bytes 1703968 | tf_op jit(solution)/shard_map/all_to_all | solution.py:1328
  106.4 3.6 %all-to-all-start.2 = ((bf16[8,112,1024]{2,1,0:T(8,128)(2,1)}), bf16[8,112,1024]{2,1,0:T(8,128)(2,1)S(1)}, u32[]{:S(2)}, u32[]{:S(2)}) async-start(bf16[8,112,1024]{2,1,0:T(8,128)(2,1)} %copy-done.1), calls=%async_computation.2 | async-start | bytes 3670016 | tf_op jit(solution)/shard_map/all_to_all | solution.py:1328
  110.0 58.6 %shard_map.279 = (bf16[8,104,1024]{2,1,0:T(8,128)(2,1)}, f32[1448,128]{1,0:T(8,128)}, f32[8,128]{1,0:T(8,128)}) custom-call(s32[16896]{0:T(1024)} %reshape.416.index, bf16[8,104,1024]{2,1,0:T(8,128)(2,1)} %all-to-all-done.got, bf16[10,186,1536]{2,1,0:T(8,128)(2,1)} %bitcast.227, bf16[10,186,1536]{2,1,0:T(8,128)(2,1)} %bitcast.228, ...), custom_call_target="tpu_custom_call" | custom-call | flops 8999999488 | bytes 20000000 | tf_op jit(solution)/shard_map/pallas_call | solution.py:1028
  168.6 5.1 %all-to-all-start.3 = ((bf16[8,104,1024]{2,1,0:T(8,128)(2,1)}), bf16[8,104,1024]{2,1,0:T(8,128)(2,1)S(1)}, u32[]{:S(2)}, u32[]{:S(2)}) async-start(bf16[8,104,1024]{2,1,0:T(8,128)(2,1)} %get-tuple-element.106), calls=%async_computation.3 | async-start | bytes 3407872 | tf_op jit(solution)/shard_map/all_to_all | solution.py:1328
  173.7 2.7 fusion
  178.5 0.8 slice_bitcast_fusion.1
  179.3 0.6 copy.62
  180.5 1.3 reshape.422.stamps
  181.8 5.3 %shard_map.281 = bf16[8,104,1024]{2,1,0:T(8,128)(2,1)} custom-call(s32[1024]{0:T(1024)S(1)} %copy-done.10, bf16[8,112,1024]{2,1,0:T(8,128)(2,1)S(1)} %all-to-all-done.2.got), custom_call_target="tpu_custom_call" | custom-call | flops 2000000 | bytes 2000000 | tf_op jit(solution)/shard_map/pallas_call | solution.py:526
  187.2 13.1 %shard_map.282 = (bf16[386,8192]{1,0:T(8,128)(2,1)}, s32[1,8192]{1,0:T(1,128)}) custom-call(s32[16]{0:T(128)} %reshape.419.starts, s32[8192]{0:T(1024)} %bitcast.198, s32[8192]{0:T(1024)} %bitcast.204, bf16[8,186,512]{2,1,0:T(8,128)(2,1)} %copy-done.12, s32[8,1,512]{2,1,0:T(1,128)} %reshape.422.stamps, bf16[100,8192]{1,0:T(8,128)(2,1)} %get-tuple-element.81.s_cols.own, ...), custom_call_target="tpu_custom_call" | custom-call | flops 20000000 | bytes 16000000 | tf_op jit(solution)/shard_map/pallas_call | solution.py:1168
  200.3 15.4 %shard_map.280 = (bf16[5,112,8192]{2,1,0:T(8,128)(2,1)}, f32[100,64,128]{2,1,0:T(8,128)}, s32[1,8192]{1,0:T(1,128)}) custom-call(bf16[386,8192]{1,0:T(8,128)(2,1)} %bitcast.186, bf16[112,8192]{1,0:T(8,128)(2,1)} %bitcast.181, bf16[112,8192]{1,0:T(8,128)(2,1)} %get-tuple-element.107.low.low_in, f32[100,64,128]{2,1,0:T(8,128)} %bitcast.191, ...), custom_call_target="tpu_custom_call" | custom-call | flops 3000000000 | bytes 34000000 | tf_op jit(solution)/shard_map/pallas_call | solution.py:595
  215.7 6.5 %all-to-all-start.4 = ((bf16[8,104,1024]{2,1,0:T(8,128)(2,1)}), bf16[8,104,1024]{2,1,0:T(8,128)(2,1)}, u32[]{:S(2)}, u32[]{:S(2)}) async-start(bf16[8,104,1024]{2,1,0:T(8,128)(2,1)} %shard_map.281), calls=%async_computation.4 | async-start | bytes 3407872 | tf_op jit(solution)/shard_map/all_to_all | solution.py:1328
  222.3 23.8 %shard_map.283 = (f32[2176,128]{1,0:T(8,128)}, f32[8,128]{1,0:T(8,128)}, f32[100,64,128]{2,1,0:T(8,128)}) custom-call(s32[8192]{0:T(1024)} %get-tuple-element.191.index, bf16[8,104,1024]{2,1,0:T(8,128)(2,1)} %copy-done.11, bf16[448,112]{1,0:T(8,128)(2,1)} %get-tuple-element.116.w_hid, bf16[5,112,8192]{2,1,0:T(8,128)(2,1)} %get-tuple-element.117.factors_in, ...), custom_call_target="tpu_custom_call" | custom-call | flops 5000000000 | bytes 36000000 | tf_op jit(solution)/shard_map/pallas_call | solution.py:729
  246.1 1.2 copy-done.4
  247.4 0.7 copy-done.9
  248.0 1.8 shard_map.284
  250.6 1.8 collective-permute-done.8
  252.5 1.7 collective-permute-start.9
  254.2 1.3 collective-permute-start.10
  255.5 1.2 collective-permute-start.11
  256.7 6.3 %all-to-all-done.4.partner = bf16[8,104,1024]{2,1,0:T(8,128)(2,1)} async-done(((bf16[8,104,1024]{2,1,0:T(8,128)(2,1)}), bf16[8,104,1024]{2,1,0:T(8,128)(2,1)}, u32[]{:S(2)}, u32[]{:S(2)}) %all-to-all-start.4) | async-done | bytes 1703968 | tf_op jit(solution)/shard_map/all_to_all | solution.py:1328
  263.0 9.9 %shard_map.285 = bf16[386,8192]{1,0:T(8,128)(2,1)} custom-call(s32[16]{0:T(128)} %reshape.419.starts, s32[8192]{0:T(1024)} %bitcast.199, bf16[8,104,1024]{2,1,0:T(8,128)(2,1)} %all-to-all-done.4.partner, bf16[386,8192]{1,0:T(8,128)(2,1)} %get-tuple-element.126.mailbox), custom_call_target="tpu_custom_call", output_to_operand_aliasing={{}: (3, {})} | custom-call | flops 10000000 | bytes 8000000 | tf_op jit(solution)/shard_map/pallas_call | solution.py:1223
  273.1 1.5 collective-permute-start.14
  274.6 2.0 collective-permute-start.12
  276.7 2.8 collective-permute-done.13
  279.5 0.7 collective-permute-done.12
  280.5 1.1 collective-permute-done.15
  281.6 2.6 collective-permute-start.17
  284.8 0.9 collective-permute-start.16
  285.8 2.9 collective-permute-done.18
  288.8 0.9 collective-permute-start.20
  289.6 2.3 collective-permute-start.21
  292.3 1.0 collective-permute-done.20
  293.3 1.8 collective-permute-done.21
  297.0 0.7 fusion.35
  (138 shorter events, 9.8 us)
Async XLA Ops:
  2.4 7.5 %collective-permute-start = (bf16[216,128]{1,0:T(8,128)(2,1)S(1)}, bf16[216,128]{1,0:T(8,128)(2,1)S(1)}, u32[]{:S(2)}, u32[]{:S(2)}) collective-permute-start(bf16[216,128]{1,0:T(8,128)(2,1)S(1)} %pad_maximum_fusion), channel_id=1, source_target_pairs={{0,2},{1,3},{2,0},{3,1},{4,6},{5,7},{6,4},{7,5},{8,10},{9,11},{10,... | collective-permute-start | bytes 165896 | tf_op jit(solution)/shard_map/ppermute | solution.py:1241
  5.4 6.1 %collective-permute-start.1 = (bf16[216,128]{1,0:T(8,128)(2,1)S(1)}, bf16[216,128]{1,0:T(8,128)(2,1)S(1)}, u32[]{:S(2)}, u32[]{:S(2)}) collective-permute-start(bf16[216,128]{1,0:T(8,128)(2,1)S(1)} %pad_maximum_fusion), channel_id=1, source_target_pairs={{0,4},{1,5},{2,6},{3,7},{4,0},{5,1},{6,2},{7,3},{8,12},{9,13},{10,... | collective-permute-start | bytes 165896 | tf_op jit(solution)/shard_map/ppermute | solution.py:1241
  8.0 6.0 %collective-permute-start.2 = (bf16[216,128]{1,0:T(8,128)(2,1)S(1)}, bf16[216,128]{1,0:T(8,128)(2,1)S(1)}, u32[]{:S(2)}, u32[]{:S(2)}) collective-permute-start(bf16[216,128]{1,0:T(8,128)(2,1)S(1)} %pad_maximum_fusion), channel_id=1, source_target_pairs={{0,6},{1,7},{2,4},{3,5},{4,2},{5,3},{6,0},{7,1},{8,14},{9,15},{10,... | collective-permute-start | bytes 165896 | tf_op jit(solution)/shard_map/ppermute | solution.py:1241
  14.0 14.4 %collective-permute-start.4 = (bf16[4,88,128]{2,1,0:T(8,128)(2,1)S(1)}, bf16[4,88,128]{2,1,0:T(8,128)(2,1)S(1)}, u32[]{:S(2)}, u32[]{:S(2)}) collective-permute-start(bf16[4,88,128]{2,1,0:T(8,128)(2,1)S(1)} %fusion.24), channel_id=1, source_target_pairs={{0,8},{8,0},{16,24},{24,16},{1,9},{9,1},{17,25},{25,17},{2,10},{10... | collective-permute-start | bytes 270344 | tf_op jit(solution)/shard_map/ppermute | solution.py:1241
  15.5 12.9 %collective-permute-start.5 = (bf16[4,88,128]{2,1,0:T(8,128)(2,1)S(1)}, bf16[4,88,128]{2,1,0:T(8,128)(2,1)S(1)}, u32[]{:S(2)}, u32[]{:S(2)}) collective-permute-start(bf16[4,88,128]{2,1,0:T(8,128)(2,1)S(1)} %fusion.24), channel_id=1, source_target_pairs={{0,16},{8,24},{16,0},{24,8},{1,17},{9,25},{17,1},{25,9},{2,18},{10... | collective-permute-start | bytes 270344 | tf_op jit(solution)/shard_map/ppermute | solution.py:1241
  17.0 11.4 %collective-permute-start.6 = (bf16[4,88,128]{2,1,0:T(8,128)(2,1)S(1)}, bf16[4,88,128]{2,1,0:T(8,128)(2,1)S(1)}, u32[]{:S(2)}, u32[]{:S(2)}) collective-permute-start(bf16[4,88,128]{2,1,0:T(8,128)(2,1)S(1)} %fusion.24), channel_id=1, source_target_pairs={{0,24},{8,16},{16,8},{24,0},{1,25},{9,17},{17,9},{25,1},{2,26},{10... | collective-permute-start | bytes 270344 | tf_op jit(solution)/shard_map/ppermute | solution.py:1241
  17.5 11.7 %collective-permute-start.3 = (bf16[4,128,128]{2,1,0:T(8,128)(2,1)S(1)}, bf16[4,128,128]{2,1,0:T(8,128)(2,1)S(1)}, u32[]{:S(2)}, u32[]{:S(2)}) collective-permute-start(bf16[4,128,128]{2,1,0:T(8,128)(2,1)S(1)} %fusion.19), channel_id=1, source_target_pairs={{0,1},{1,0},{2,3},{3,2},{4,5},{5,4},{6,7},{7,6},{8,9},{9,8},{10,11... | collective-permute-start | bytes 393224 | tf_op jit(solution)/shard_map/ppermute | solution.py:1241
  19.8 3.8 %copy-start.7 = (f32[100,128]{1,0:T(8,128)S(1)}, f32[100,128]{1,0:T(8,128)}, u32[]{:S(2)}) copy-start(f32[100,128]{1,0:T(8,128)} %constant.208.clone.freq) | copy-start | bytes 153604
  19.8 41.5 %all-to-all-start.1 = ((bf16[8,186,512]{2,1,0:T(8,128)(2,1)}), bf16[8,186,512]{2,1,0:T(8,128)(2,1)S(1)}, u32[]{:S(2)}, u32[]{:S(2)}) async-start(bf16[8,186,512]{2,1,0:T(8,128)(2,1)} %broadcast_in_dim.137), calls=%async_computation.1 | async-start | bytes 3145728 | tf_op jit(solution)/shard_map/all_to_all | solution.py:1328
  27.1 1.2 copy-start
  28.5 1.9 collective-permute-start.7
  31.5 0.9 copy-start.13
  60.0 5.8 %copy-start.22 = (s32[1,1,3,512]{3,1,2,0:T(1,128)S(1)}, s32[1,1,3,512]{3,1,2,0:T(1,128)}, u32[]{:S(2)}) copy-start(s32[1,1,3,512]{3,1,2,0:T(1,128)} %param.29) | copy-start | bytes 18436
  60.0 5.8 %copy-start.24 = (s32[1,1,8]{2,1,0:T(1,128)S(1)}, s32[1,1,8]{2,1,0:T(1,128)}, u32[]{:S(2)}) copy-start(s32[1,1,8]{2,1,0:T(1,128)} %param.28) | copy-start | bytes 100
  60.0 6.1 %copy-start.17 = (s32[1,1,8,1024]{3,2,1,0:T(8,128)S(1)}, s32[1,1,8,1024]{3,2,1,0:T(8,128)}, u32[]{:S(2)}) copy-start(s32[1,1,8,1024]{3,2,1,0:T(8,128)} %param.27) | copy-start | bytes 98308
  60.0 18.3 %copy-start.23 = (s32[1,1,512]{2,1,0:T(1,128)S(1)}, s32[1,1,512]{2,1,0:T(1,128)}, u32[]{:S(2)}) copy-start(s32[1,1,512]{2,1,0:T(1,128)} %param.34) | copy-start | bytes 6148
  61.3 17.8 %copy-start.12 = (bf16[8,186,512]{2,1,0:T(8,128)(2,1)}, bf16[8,186,512]{2,1,0:T(8,128)(2,1)S(1)}, u32[]{:S(2)}) copy-start(bf16[8,186,512]{2,1,0:T(8,128)(2,1)S(1)} %all-to-all-done.1.edges) | copy-start | bytes 4571140
  61.3 17.8 %copy-start.18 = (s32[1,1,1536,10]{2,1,3,0:T(1,128)S(1)}, s32[1,1,1536,10]{2,1,3,0:T(1,128)}, u32[]{:S(2)}) copy-start(s32[1,1,1536,10]{2,1,3,0:T(1,128)} %param.31) | copy-start | bytes 184324
  61.3 17.8 %copy-start.16 = (s32[1,1,1536,10]{2,1,3,0:T(1,128)S(1)}, s32[1,1,1536,10]{2,1,3,0:T(1,128)}, u32[]{:S(2)}) copy-start(s32[1,1,1536,10]{2,1,3,0:T(1,128)} %param.30) | copy-start | bytes 184324
  61.3 45.1 %all-to-all-start = ((bf16[8,104,1024]{2,1,0:T(8,128)(2,1)}), bf16[8,104,1024]{2,1,0:T(8,128)(2,1)}, u32[]{:S(2)}, u32[]{:S(2)}) async-start(bf16[8,104,1024]{2,1,0:T(8,128)(2,1)} %get-tuple-element.80), calls=%async_computation | async-start | bytes 3407872 | tf_op jit(solution)/shard_map/all_to_all | solution.py:1328
  66.1 5.0 %copy-start.21 = (s32[1,4,2,128]{3,1,2,0:T(4,128)}, s32[1,4,2,128]{3,1,2,0:T(4,128)S(1)}, u32[]{:S(2)}) copy-start(s32[1,4,2,128]{3,1,2,0:T(4,128)S(1)} %copy.46) | copy-start | bytes 12292
  79.4 8.8 %copy-start.2 = (bf16[100,8192]{1,0:T(8,128)(2,1)S(1)}, bf16[100,8192]{1,0:T(8,128)(2,1)}, u32[]{:S(2)}) copy-start(bf16[100,8192]{1,0:T(8,128)(2,1)} %get-tuple-element.81.s_cols.own) | copy-start | bytes 4915204
  79.4 8.8 %copy-start.6 = (s32[8192]{0:T(1024)S(1)}, s32[8192]{0:T(1024)}, u32[]{:S(2)}) copy-start(s32[8192]{0:T(1024)} %get-tuple-element.191.index) | copy-start | bytes 98308
  86.5 1.7 copy-start.3
  99.2 1.2 copy-start.1
  106.4 62.2 %all-to-all-start.2 = ((bf16[8,112,1024]{2,1,0:T(8,128)(2,1)}), bf16[8,112,1024]{2,1,0:T(8,128)(2,1)S(1)}, u32[]{:S(2)}, u32[]{:S(2)}) async-start(bf16[8,112,1024]{2,1,0:T(8,128)(2,1)} %copy-done.1), calls=%async_computation.2 | async-start | bytes 3670016 | tf_op jit(solution)/shard_map/all_to_all | solution.py:1328
  168.6 47.1 %all-to-all-start.3 = ((bf16[8,104,1024]{2,1,0:T(8,128)(2,1)}), bf16[8,104,1024]{2,1,0:T(8,128)(2,1)S(1)}, u32[]{:S(2)}, u32[]{:S(2)}) async-start(bf16[8,104,1024]{2,1,0:T(8,128)(2,1)} %get-tuple-element.106), calls=%async_computation.3 | async-start | bytes 3407872 | tf_op jit(solution)/shard_map/all_to_all | solution.py:1328
  173.7 8.1 %copy-start.10 = (s32[1024]{0:T(1024)S(1)}, s32[1024]{0:T(1024)}, u32[]{:S(2)}) copy-start(s32[1024]{0:T(1024)} %get-tuple-element.111.index) | copy-start | bytes 12292
  176.6 0.6 copy-start.15
  215.7 6.6 %copy-start.11 = (bf16[8,104,1024]{2,1,0:T(8,128)(2,1)}, bf16[8,104,1024]{2,1,0:T(8,128)(2,1)S(1)}, u32[]{:S(2)}) copy-start(bf16[8,104,1024]{2,1,0:T(8,128)(2,1)S(1)} %all-to-all-done.3.got) | copy-start | bytes 5111812
  215.7 47.3 %all-to-all-start.4 = ((bf16[8,104,1024]{2,1,0:T(8,128)(2,1)}), bf16[8,104,1024]{2,1,0:T(8,128)(2,1)}, u32[]{:S(2)}, u32[]{:S(2)}) async-start(bf16[8,104,1024]{2,1,0:T(8,128)(2,1)} %shard_map.281), calls=%async_computation.4 | async-start | bytes 3407872 | tf_op jit(solution)/shard_map/all_to_all | solution.py:1328
  222.3 23.8 %copy-start.5 = (f32[1448,128]{1,0:T(8,128)S(1)}, f32[1448,128]{1,0:T(8,128)}, u32[]{:S(2)}) copy-start(f32[1448,128]{1,0:T(8,128)} %get-tuple-element.120.att) | copy-start | bytes 2224132
  222.3 23.8 %copy-start.8 = (f32[8,128]{1,0:T(8,128)S(1)}, f32[8,128]{1,0:T(8,128)}, u32[]{:S(2)}) copy-start(f32[8,128]{1,0:T(8,128)} %get-tuple-element.121.losses) | copy-start | bytes 12292
  246.1 1.2 copy-start.4
  247.4 0.7 copy-start.9
  250.0 2.4 collective-permute-start.8
  252.5 20.4 %collective-permute-start.9 = (f32[1,4,1,88,128]{4,3,2,1,0:T(8,128)S(1)}, f32[1,4,1,88,128]{4,3,2,1,0:T(8,128)S(1)}, u32[]{:S(2)}, u32[]{:S(2)}) collective-permute-start(f32[1,4,1,88,128]{4,3,2,1,0:T(8,128)S(1)} %get-tuple-element.180), channel_id=1, source_target_pairs={{0,8},{8,0},{16,24},{24,16},{1,9},{9,1},{17,25},{25,17},{2,10},{10... | collective-permute-start | bytes 540680 | tf_op jit(solution)/shard_map/ppermute | solution.py:1241
  254.2 18.8 %collective-permute-start.10 = (f32[1,4,1,88,128]{4,3,2,1,0:T(8,128)S(1)}, f32[1,4,1,88,128]{4,3,2,1,0:T(8,128)S(1)}, u32[]{:S(2)}, u32[]{:S(2)}) collective-permute-start(f32[1,4,1,88,128]{4,3,2,1,0:T(8,128)S(1)} %get-tuple-element.179), channel_id=1, source_target_pairs={{0,16},{8,24},{16,0},{24,8},{1,17},{9,25},{17,1},{25,9},{2,18},{10... | collective-permute-start | bytes 540680 | tf_op jit(solution)/shard_map/ppermute | solution.py:1241
  255.5 41.5 %copy-start.14 = (f32[11264]{0:T(1024)S(1)}, f32[11264]{0:T(1024)}, u32[]{:S(2)}) copy-start(f32[11264]{0:T(1024)} %param.19) | copy-start | bytes 135172
  255.5 41.5 %copy-start.19 = (f32[11264]{0:T(1024)S(1)}, f32[11264]{0:T(1024)}, u32[]{:S(2)}) copy-start(f32[11264]{0:T(1024)} %param.20) | copy-start | bytes 135172
  255.5 41.5 %copy-start.20 = (f32[11264]{0:T(1024)S(1)}, f32[11264]{0:T(1024)}, u32[]{:S(2)}) copy-start(f32[11264]{0:T(1024)} %param.21) | copy-start | bytes 135172
  255.5 17.4 %collective-permute-start.11 = (f32[1,4,1,88,128]{4,3,2,1,0:T(8,128)S(1)}, f32[1,4,1,88,128]{4,3,2,1,0:T(8,128)S(1)}, u32[]{:S(2)}, u32[]{:S(2)}) collective-permute-start(f32[1,4,1,88,128]{4,3,2,1,0:T(8,128)S(1)} %get-tuple-element.178), channel_id=1, source_target_pairs={{0,24},{8,16},{16,8},{24,0},{1,25},{9,17},{17,9},{25,1},{2,26},{10... | collective-permute-start | bytes 540680 | tf_op jit(solution)/shard_map/ppermute | solution.py:1241
  273.1 6.5 %collective-permute-start.13 = (f32[1,1,1,88,128]{4,3,2,1,0:T(8,128)S(1)}, f32[1,1,1,88,128]{4,3,2,1,0:T(8,128)S(1)}, u32[]{:S(2)}, u32[]{:S(2)}) collective-permute-start(f32[1,1,1,88,128]{4,3,2,1,0:T(8,128)S(1)} %get-tuple-element.183), channel_id=1, source_target_pairs={{0,4},{1,5},{2,6},{3,7},{4,0},{5,1},{6,2},{7,3},{8,12},{9,13},{10,... | collective-permute-start | bytes 135176 | tf_op jit(solution)/shard_map/ppermute | solution.py:1241
  273.1 6.4 %collective-permute-start.14 = (f32[1,1,1,88,128]{4,3,2,1,0:T(8,128)S(1)}, f32[1,1,1,88,128]{4,3,2,1,0:T(8,128)S(1)}, u32[]{:S(2)}, u32[]{:S(2)}) collective-permute-start(f32[1,1,1,88,128]{4,3,2,1,0:T(8,128)S(1)} %get-tuple-element.182), channel_id=1, source_target_pairs={{0,6},{1,7},{2,4},{3,5},{4,2},{5,3},{6,0},{7,1},{8,14},{9,15},{10,... | collective-permute-start | bytes 135176 | tf_op jit(solution)/shard_map/ppermute | solution.py:1241
  274.6 5.6 %collective-permute-start.12 = (f32[1,1,1,88,128]{4,3,2,1,0:T(8,128)S(1)}, f32[1,1,1,88,128]{4,3,2,1,0:T(8,128)S(1)}, u32[]{:S(2)}, u32[]{:S(2)}) collective-permute-start(f32[1,1,1,88,128]{4,3,2,1,0:T(8,128)S(1)} %get-tuple-element.181), channel_id=1, source_target_pairs={{0,2},{1,3},{2,0},{3,1},{4,6},{5,7},{6,4},{7,5},{8,10},{9,11},{10,... | collective-permute-start | bytes 135176 | tf_op jit(solution)/shard_map/ppermute | solution.py:1241
  280.3 1.2 collective-permute-start.15
  281.6 4.2 %collective-permute-start.17 = (f32[8,128]{1,0:T(8,128)S(1)}, f32[8,128]{1,0:T(8,128)S(1)}, u32[]{:S(2)}, u32[]{:S(2)}) collective-permute-start(f32[8,128]{1,0:T(8,128)S(1)} %fusion.34), channel_id=1, source_target_pairs={{0,16},{8,24},{16,0},{24,8},{1,17},{9,25},{17,1},{25,9},{2,18},{10... | collective-permute-start | bytes 12296 | tf_op jit(solution)/shard_map/ppermute | solution.py:1241
  284.2 4.5 %collective-permute-start.18 = (f32[8,128]{1,0:T(8,128)S(1)}, f32[8,128]{1,0:T(8,128)S(1)}, u32[]{:S(2)}, u32[]{:S(2)}) collective-permute-start(f32[8,128]{1,0:T(8,128)S(1)} %fusion.34), channel_id=1, source_target_pairs={{0,24},{8,16},{16,8},{24,0},{1,25},{9,17},{17,9},{25,1},{2,26},{10... | collective-permute-start | bytes 12296 | tf_op jit(solution)/shard_map/ppermute | solution.py:1241
  284.8 3.9 %collective-permute-start.16 = (f32[8,128]{1,0:T(8,128)S(1)}, f32[8,128]{1,0:T(8,128)S(1)}, u32[]{:S(2)}, u32[]{:S(2)}) collective-permute-start(f32[8,128]{1,0:T(8,128)S(1)} %fusion.34), channel_id=1, source_target_pairs={{0,8},{8,0},{16,24},{24,16},{1,9},{9,1},{17,25},{25,17},{2,10},{10... | collective-permute-start | bytes 12296 | tf_op jit(solution)/shard_map/ppermute | solution.py:1241
  288.8 4.5 %collective-permute-start.20 = (f32[8,128]{1,0:T(8,128)S(1)}, f32[8,128]{1,0:T(8,128)S(1)}, u32[]{:S(2)}, u32[]{:S(2)}) collective-permute-start(f32[8,128]{1,0:T(8,128)S(1)} %add_add_fusion.3), channel_id=1, source_target_pairs={{0,4},{1,5},{2,6},{3,7},{4,0},{5,1},{6,2},{7,3},{8,12},{9,13},{10,... | collective-permute-start | bytes 12296 | tf_op jit(solution)/shard_map/ppermute | solution.py:1241
  289.6 5.4 %collective-permute-start.21 = (f32[8,128]{1,0:T(8,128)S(1)}, f32[8,128]{1,0:T(8,128)S(1)}, u32[]{:S(2)}, u32[]{:S(2)}) collective-permute-start(f32[8,128]{1,0:T(8,128)S(1)} %add_add_fusion.3), channel_id=1, source_target_pairs={{0,6},{1,7},{2,4},{3,5},{4,2},{5,3},{6,0},{7,1},{8,14},{9,15},{10,... | collective-permute-start | bytes 12296 | tf_op jit(solution)/shard_map/ppermute | solution.py:1241
  292.0 3.6 %collective-permute-start.19 = (f32[8,128]{1,0:T(8,128)S(1)}, f32[8,128]{1,0:T(8,128)S(1)}, u32[]{:S(2)}, u32[]{:S(2)}) collective-permute-start(f32[8,128]{1,0:T(8,128)S(1)} %add_add_fusion.3), channel_id=1, source_target_pairs={{0,2},{1,3},{2,0},{3,1},{4,6},{5,7},{6,4},{7,5},{8,10},{9,11},{10,... | collective-permute-start | bytes 12296 | tf_op jit(solution)/shard_map/ppermute | solution.py:1241

commit v4 on v3

--- a/solution.py
+++ b/solution.py
@@ -179,20 +179,10 @@
     w_mail,
     w_two,
     w_hid,
+    kv_e,
+    att,
+    cols,
     w_feat,
-    kv_h,
-    kv_e,
-    kv_t,
-    q_h,
-    q_one,
-    o_att,
-    o_att_n,
-    o_h,
-    src_t,
-    src_n,
-    dst_t,
-    dst_n,
-    cols,
     wide,
     rows,
 ):
@@ -244,23 +234,28 @@
             block = spread_heads(rows[pl.ds(ROW_KV + 2 * start + part, size, stride=2), :])
             return jnp.where(row_of((size, LANES)) < count, block, 0.0).T[:PAD]
 
-        kv_h[to, :] = heads(0, MEM).astype(BF16)
+        att[to, :] = heads(0, MEM).astype(BF16)
         kv_e[to, :] = heads(MEM, EDGE)[:, :EDGE].astype(BF16)
-        kv_t[to, :] = heads(MEM + EDGE, TENC)[:, :TENC].astype(BF16)
+        att[KV + PAD * part : KV + PAD * part + PAD, :] = heads(MEM + EDGE, TENC).astype(BF16)
     q_rows = spread_heads(rows[ROW_Q : ROW_Q + LANES, :])
     keep = row_of((LANES, LANES)) < 100
-    q_h[...] = jnp.where(keep, q_rows, 0.0).T[:PAD].astype(BF16)
     q_two = spread_heads(rows[ROW_Q + 100 : ROW_Q + 100 + LANES, :])
     q_sum = jnp.sum(jnp.where(keep, q_two, 0.0), 0, keepdims=True)
-    q_one[...] = jnp.broadcast_to(q_sum, (LANES, LANES)).T[:PAD]
-    att = spread_heads(turned(ROW_O, 100))
-    o_att[...] = att[:PAD, :PAD].astype(BF16)
-    o_att_n[...] = att.T[:PAD, :PAD].astype(BF16)
-    o_h[...] = turned(ROW_O + 100, 100)[:PAD].astype(BF16)
-    for start, out_t, out_n in ((ROW_SRC, src_t, src_n), (ROW_DST, dst_t, dst_n)):
-        block = turned(start, 100)
-        out_t[...] = block[:PAD, :PAD].astype(BF16)
-        out_n[...] = block.T[:PAD, :PAD].astype(BF16)
+    cols[6, :, :] = jnp.broadcast_to(q_sum, (LANES, LANES)).T[:PAD]
+    o_att = spread_heads(turned(ROW_O, 100))
+    src, dst = turned(ROW_SRC, 100), turned(ROW_DST, 100)
+    blocks = (
+        jnp.where(keep, q_rows, 0.0).T,
+        o_att,
+        o_att.T,
+        turned(ROW_O + 100, 100),
+        src,
+        src.T,
+        dst,
+        dst.T,
+    )
+    for i, block in enumerate(blocks):
+        att[2 * KV + PAD * i : 2 * KV + PAD * i + PAD, :] = block[:PAD].astype(BF16)
     for i, r in enumerate((ROW_BO, ROW_GAIN, ROW_SHIFT, ROW_BPRED, ROW_OUT)):
         cols[i, :, :] = column(r)
     first = rows[ROW_BOUT : ROW_BOUT + 1, :]
@@ -272,20 +267,9 @@
     ((GATES, MAIL), BF16),
     ((4 * PAD, 2 * PAD), BF16),
     ((4 * PAD, PAD), BF16),
-    ((PAD, NFEAT), BF16),
-    ((KV, LANES), BF16),
     ((KV, EDGE), BF16),
-    ((KV, TENC), BF16),
-    ((PAD, LANES), BF16),
-    ((PAD, LANES), F32),
-    ((PAD, PAD), BF16),
-    ((PAD, PAD), BF16),
-    ((PAD, LANES), BF16),
-    ((PAD, PAD), BF16),
-    ((PAD, PAD), BF16),
-    ((PAD, PAD), BF16),
-    ((PAD, PAD), BF16),
-    ((6, PAD, LANES), F32),
+    ((2 * KV + 8 * PAD, LANES), BF16),
+    ((7, PAD, LANES), F32),
 ]
 
 
@@ -368,8 +352,8 @@
 def gru_kernel(index, flat, mail_in, phi_in, mem_in, feat_in, *refs):
     wts, rest = refs[: len(WEIGHTS)], refs[len(WEIGHTS) :]
     sent_out, low_out, s_out = rest[:3]
-    wide, rows, mail, two, mem, feat, s_cols, table, sent, in_sems, out_sems, sent_sems = rest[3:]
-    w_mail, w_two, w_hid, w_feat = wts[:4]
+    w_feat, wide, rows, mail, two, mem, feat, s_cols, table, sent, in_sems, out_sems, sent_sems = rest[3:]
+    w_mail, w_two = wts[:2]
     nodes = mail.shape[1]
     half = nodes // 2
     copies = []
@@ -382,7 +366,7 @@
         copies.append([pltpu.make_async_copy(r, v, in_sems.at[part, i]) for i, (r, v) in enumerate(pairs)])
         for copy in copies[-1]:
             copy.start()
-    unpack_weights(flat, *wts, wide, rows)
+    unpack_weights(flat, *wts, w_feat, wide, rows)
     sub = 256
     real = row_of((PAD, sub)) < MEM
     ones = (row_of((PAD, sub)) == MEM).astype(F32)
@@ -462,6 +446,7 @@
         in_specs=[SMEM, VMEM] + [HBM] * 4,
         out_specs=[VMEM] * len(WEIGHTS) + [HBM] * 3,
         scratch_shapes=[
+            pltpu.VMEM((PAD, NFEAT), BF16),
             pltpu.VMEM((FLAT_ROWS + 16, LANES), F32),
             pltpu.VMEM((WROWS + 512, LANES), F32),
             pltpu.VMEM((MAIL, rows), BF16),
@@ -766,18 +751,8 @@
     p1,
     p2,
     weight,
-    kv_h,
     kv_e,
-    kv_t,
-    q_h,
-    q_one,
-    o_att,
-    o_att_n,
-    o_h,
-    src_t,
-    src_n,
-    dst_t,
-    dst_n,
+    att_wts,
     cols,
     sent,
     grads,
@@ -801,6 +776,11 @@
 ):
     lanes, picks = rest[:STREAMS], rest[STREAMS:]
     step = pl.program_id(0)
+    kv_h, kv_t = att_wts.at[0:KV, :], att_wts.at[KV : 2 * KV, 0:TENC]
+    q_h, o_att, o_att_n, o_h, src_t, src_n, dst_t, dst_n = (
+        att_wts.at[2 * KV + PAD * i : 2 * KV + PAD * i + PAD, 0 : LANES if i in (0, 3) else PAD]
+        for i in range(8)
+    )
     near = NBR * SECT
     total = near + SECT
     scale = 50 ** (-0.5)
@@ -842,7 +822,7 @@
     queries, probs, atts, pres, embs, norms = [], [], [], [], [], []
     for t in range(3):
         at = slice(t * EB, t * EB + EB)
-        q = query[:, at] + q_one[...]
+        q = query[:, at] + cols[6]
         scores = [[], []]
         for k in range(NBR):
             both = q * kv[k, 0:PAD, at]
@@ -1037,7 +1017,7 @@
         + [section(EDGE, t) for t in range(3)]
         + [section(TENC, t) for t in range(3)]
         + [pl.BlockSpec((1, EB), lambda b: (0, b))]
-        + [VMEM] * 13,
+        + [VMEM] * 3,
         out_specs=(VMEM, VMEM, VMEM),
         scratch_shapes=[
             pltpu.VMEM((slots, LANES), F32),
@@ -1060,7 +1040,7 @@
         + [pltpu.VMEM((SECT, LANES), BF16) for _ in range(NBR + 1)],
         compiler_params=params_of(),
         cost_estimate=pl.CostEstimate(flops=9_000_000_000, bytes_accessed=20_000_000, transcendentals=1_000_000),
-    )(index, got, edges, edges, edges, codes, codes, codes, weight, *wts[4:])
+    )(index, got, edges, edges, edges, codes, codes, codes, weight, *wts[3:])
 
 
 def pack_kernel(gru, bias, att, losses, out, rows):

time: 300 us -> 300 us (level)
  transfers between devices with their start and end apart: 27 -> 27, of which waited for: 14 -> 15; matrix products, arithmetic and copies ran while one was open for 7% -> 7% of each run, Pallas kernels for 61% -> 61%
where the time goes in v4:
time: 300 us; the launch traced here: 297 us
  Pallas kernels  183 us (61%)
  starting transfers between devices  47.5 us (16%)
  waiting for transfers between devices  30.7 us (10%)
  local copies, waits for them, and re-layouts  18.4 us (6%)
  other arithmetic  11.9 us (4%)
  between operations  3.37 us (1%)
    pallas_call x1, Pallas kernels, attention(): pl.pallas_call(attention_kernel, grid=(blocks,), out_shape=(jax.ShapeDtyp...  58.4 us
    pallas_call x1, Pallas kernels, gru_forward(): pl.pallas_call(gru_kernel, out_shape=shapes, in_specs=[SMEM, VMEM] + [HBM...  27.2 us
    ppermute x22, starting transfers between devices, flip(): lax.ppermute(x, axis, [(i, i ^ mask) for i in range(lax.axis_size(axis))])  24.7 us
    pallas_call x1, Pallas kernels, gru_backward(): pl.pallas_call(gru_back_kernel, out_shape=(jax.ShapeDtypeStruct((GRU_ROWS...  23.8 us
    all_to_all x5, starting transfers between devices, swap(): return lax.all_to_all(x, 'node', split_axis=0, concat_axis=0, tiled=True)  22.8 us
    ppermute x22, waiting for transfers between devices, flip(): lax.ppermute(x, axis, [(i, i ^ mask) for i in range(lax.axis_size(axis))])  16.2 us
    pallas_call x1, Pallas kernels, gru_factors(): pl.pallas_call(factor_kernel, grid=(rows // BLOCK,), out_shape=(jax.Shape...  15.4 us
    all_to_all x5, waiting for transfers between devices, swap(): return lax.all_to_all(x, 'node', split_axis=0, concat_axis=0, tiled=True)  14.5 us
  transfers between devices with their start and end apart: 27, of which 15 were waited for; matrix products, arithmetic and copies ran while one was open for 7% of the time, Pallas kernels for 61%

profile of v4, /device:TPU:0, one launch (start us, length us, event | category | flops | bytes accessed | tf_op | source)
XLA Modules:
  0.0 297.5 jit_solution(996250913854038778)
XLA Ops:
  0.6 0.9 add_select_fusion.4
  1.6 0.8 convert_bitcast_fusion
  2.4 3.1 %collective-permute-start = (bf16[216,128]{1,0:T(8,128)(2,1)S(1)}, bf16[216,128]{1,0:T(8,128)(2,1)S(1)}, u32[]{:S(2)}, u32[]{:S(2)}) collective-permute-start(bf16[216,128]{1,0:T(8,128)(2,1)S(1)} %pad_maximum_fusion), channel_id=1, source_target_pairs={{0,2},{1,3},{2,0},{3,1},{4,6},{5,7},{6,4},{7,5},{8,10},{9,11},{10,... | collective-permute-start | bytes 165896 | tf_op jit(solution)/shard_map/ppermute | solution.py:1221
  5.4 2.6 collective-permute-start.1
  8.1 0.8 bitcast_dynamic-update-slice_fusion.8
  9.0 0.8 sub.43.delta
  9.9 1.7 collective-permute-done.1
  11.6 2.4 collective-permute-done.2
  14.0 1.5 collective-permute-start.4
  15.5 1.5 collective-permute-start.5
  17.6 2.2 broadcast_in_dim.137
  19.8 3.7 %all-to-all-start.1 = ((bf16[8,186,512]{2,1,0:T(8,128)(2,1)}), bf16[8,186,512]{2,1,0:T(8,128)(2,1)S(1)}, u32[]{:S(2)}, u32[]{:S(2)}) async-start(bf16[8,186,512]{2,1,0:T(8,128)(2,1)} %broadcast_in_dim.137), calls=%async_computation.1 | async-start | bytes 3145728 | tf_op jit(solution)/shard_map/all_to_all | solution.py:1308
  23.6 3.5 %shard_map.274 = bf16[1,112,8192]{2,1,0:T(8,128)(2,1)S(1)} custom-call(s32[1,8192]{1,0:T(1,128)S(1)} %sub.43.delta, f32[100,128]{1,0:T(8,128)S(1)} %copy-done.7), custom_call_target="tpu_custom_call" | custom-call | flops 24576000 | bytes 1638400 | tf_op jit(solution)/shard_map/pallas_call | solution.py:165
  27.1 1.2 copy-done
  29.5 0.7 add_select_fusion.1
  30.5 1.0 bitcast_dynamic-update-slice_fusion.1
  31.5 0.8 copy-done.13
  32.4 27.2 %shard_map.275 = (bf16[336,386]{1,0:T(8,128)(2,1)}, bf16[448,224]{1,0:T(8,128)(2,1)}, bf16[448,112]{1,0:T(8,128)(2,1)}, bf16[224,186]{1,0:T(8,128)(2,1)}, bf16[1...) custom-call(s32[8192]{0:T(1024)} %get-tuple-element.171.index, ...), custom_call_target="tpu_custom_call" | custom-call | flops 4000000000 | bytes 24000000 | tf_op jit(solution)/shard_map/pallas_call | solution.py:443
  59.7 1.6 all-to-all-done.1.edges
  61.3 4.4 %all-to-all-start = ((bf16[8,104,1024]{2,1,0:T(8,128)(2,1)}), bf16[8,104,1024]{2,1,0:T(8,128)(2,1)}, u32[]{:S(2)}, u32[]{:S(2)}) async-start(bf16[8,104,1024]{2,1,0:T(8,128)(2,1)} %get-tuple-element.70), calls=%async_computation | async-start | bytes 3407872 | tf_op jit(solution)/shard_map/all_to_all | solution.py:1308
  66.8 4.4 %sort.10 = (s32[1024]{0:T(1024)}, s32[1024]{0:T(1024)}) sort(s32[1024]{0:T(1024)S(1)} %iota_add_fusion, s32[1024]{0:T(1024)S(1)} %iota.44), dimensions={0}, to_apply=%region_2.3 | sort | flops 10240 | bytes 16384 | tf_op jit(solution)/shard_map/sort | solution.py:1390
  71.1 6.3 %shard_map.276 = (s32[1024]{0:T(1024)}, s32[1024]{0:T(1024)}, s32[1024]{0:T(1024)}) custom-call(s32[1024]{0:T(1024)} %get-tuple-element.72.ordered, s32[1024]{0:T(1024)} %bitcast.210, s32[8192]{0:T(1024)} %bitcast.206), custom_call_target="tpu_custom_call" | custom-call | flops 4000000 | bytes 60000 | tf_op jit(solution)/shard_map/pallas_call | solution.py:543
  77.5 0.9 convert_reduce_fusion
  78.3 0.7 fusion.30
  79.5 0.6 reshape.416.index
  80.2 6.4 %shard_map.278.p0.p1.p2 = bf16[10,100,1536]{2,1,0:T(8,128)(2,1)S(1)} custom-call(s32[10,1536]{1,0:T(8,128)S(1)} %bitcast.183, f32[100,128]{1,0:T(8,128)S(1)} %copy-done.7), custom_call_target="tpu_custom_call" | custom-call | flops 46080000 | bytes 3072000 | tf_op jit(solution)/shard_map/pallas_call | solution.py:165
  86.6 1.7 copy-done.3
  88.2 10.9 %shard_map.277 = bf16[8,112,1024]{2,1,0:T(8,128)(2,1)S(1)} custom-call(s32[8192]{0:T(1024)S(1)} %copy-done.6, bf16[100,8192]{1,0:T(8,128)(2,1)S(1)} %copy-done.2, bf16[8,1024]{1,0:T(8,128)(2,1)S(1)} %reshape.412.notes), custom_call_target="tpu_custom_call" | custom-call | flops 8000000 | bytes 6000000 | tf_op jit(solution)/shard_map/pallas_call | solution.py:484
  99.2 1.2 copy-done.1
  100.4 6.0 %all-to-all-done.got = bf16[8,104,1024]{2,1,0:T(8,128)(2,1)} async-done(((bf16[8,104,1024]{2,1,0:T(8,128)(2,1)}), bf16[8,104,1024]{2,1,0:T(8,128)(2,1)}, u32[]{:S(2)}, u32[]{:S(2)}) %all-to-all-start) | async-done | bytes 1703968 | tf_op jit(solution)/shard_map/all_to_all | solution.py:1308
  106.4 3.6 %all-to-all-start.2 = ((bf16[8,112,1024]{2,1,0:T(8,128)(2,1)}), bf16[8,112,1024]{2,1,0:T(8,128)(2,1)S(1)}, u32[]{:S(2)}, u32[]{:S(2)}) async-start(bf16[8,112,1024]{2,1,0:T(8,128)(2,1)} %copy-done.1), calls=%async_computation.2 | async-start | bytes 3670016 | tf_op jit(solution)/shard_map/all_to_all | solution.py:1308
  110.0 58.4 %shard_map.279 = (bf16[8,104,1024]{2,1,0:T(8,128)(2,1)}, f32[1448,128]{1,0:T(8,128)}, f32[8,128]{1,0:T(8,128)}) custom-call(s32[16896]{0:T(1024)} %reshape.416.index, bf16[8,104,1024]{2,1,0:T(8,128)(2,1)} %all-to-all-done.got, bf16[10,186,1536]{2,1,0:T(8,128)(2,1)} %bitcast.227, bf16[10,186,1536]{2,1,0:T(8,128)(2,1)} %bitcast.228, ...), custom_call_target="tpu_custom_call" | custom-call | flops 8999999488 | bytes 20000000 | tf_op jit(solution)/shard_map/pallas_call | solution.py:1008
  168.4 5.0 %all-to-all-start.3 = ((bf16[8,104,1024]{2,1,0:T(8,128)(2,1)}), bf16[8,104,1024]{2,1,0:T(8,128)(2,1)S(1)}, u32[]{:S(2)}, u32[]{:S(2)}) async-start(bf16[8,104,1024]{2,1,0:T(8,128)(2,1)} %get-tuple-element.86), calls=%async_computation.3 | async-start | bytes 3407872 | tf_op jit(solution)/shard_map/all_to_all | solution.py:1308
  173.4 2.7 fusion
  178.2 0.8 slice_bitcast_fusion.1
  179.0 0.6 copy.62
  180.2 1.3 reshape.422.stamps
  181.6 5.3 %shard_map.281 = bf16[8,104,1024]{2,1,0:T(8,128)(2,1)} custom-call(s32[1024]{0:T(1024)S(1)} %copy-done.10, bf16[8,112,1024]{2,1,0:T(8,128)(2,1)S(1)} %all-to-all-done.2.got), custom_call_target="tpu_custom_call" | custom-call | flops 2000000 | bytes 2000000 | tf_op jit(solution)/shard_map/pallas_call | solution.py:511
  186.9 13.5 %shard_map.282 = (bf16[386,8192]{1,0:T(8,128)(2,1)}, s32[1,8192]{1,0:T(1,128)}) custom-call(s32[16]{0:T(128)} %reshape.419.starts, s32[8192]{0:T(1024)} %bitcast.198, s32[8192]{0:T(1024)} %bitcast.204, bf16[8,186,512]{2,1,0:T(8,128)(2,1)} %copy-done.12, s32[8,1,512]{2,1,0:T(1,128)} %reshape.422.stamps, bf16[100,8192]{1,0:T(8,128)(2,1)} %get-tuple-element.71.s_cols.own, ...), custom_call_target="tpu_custom_call" | custom-call | flops 20000000 | bytes 16000000 | tf_op jit(solution)/shard_map/pallas_call | solution.py:1148
  200.4 15.4 %shard_map.280 = (bf16[5,112,8192]{2,1,0:T(8,128)(2,1)}, f32[100,64,128]{2,1,0:T(8,128)}, s32[1,8192]{1,0:T(1,128)}) custom-call(bf16[386,8192]{1,0:T(8,128)(2,1)} %bitcast.186, bf16[112,8192]{1,0:T(8,128)(2,1)} %bitcast.181, bf16[112,8192]{1,0:T(8,128)(2,1)} %get-tuple-element.87.low.low_in, f32[100,64,128]{2,1,0:T(8,128)} %bitcast.191, ...), custom_call_target="tpu_custom_call" | custom-call | flops 3000000000 | bytes 34000000 | tf_op jit(solution)/shard_map/pallas_call | solution.py:580
  215.8 6.0 %all-to-all-start.4 = ((bf16[8,104,1024]{2,1,0:T(8,128)(2,1)}), bf16[8,104,1024]{2,1,0:T(8,128)(2,1)}, u32[]{:S(2)}, u32[]{:S(2)}) async-start(bf16[8,104,1024]{2,1,0:T(8,128)(2,1)} %shard_map.281), calls=%async_computation.4 | async-start | bytes 3407872 | tf_op jit(solution)/shard_map/all_to_all | solution.py:1308
  221.8 23.8 %shard_map.283 = (f32[2176,128]{1,0:T(8,128)}, f32[8,128]{1,0:T(8,128)}, f32[100,64,128]{2,1,0:T(8,128)}) custom-call(s32[8192]{0:T(1024)} %get-tuple-element.171.index, bf16[8,104,1024]{2,1,0:T(8,128)(2,1)} %copy-done.11, bf16[448,112]{1,0:T(8,128)(2,1)} %get-tuple-element.96.w_hid, bf16[5,112,8192]{2,1,0:T(8,128)(2,1)} %get-tuple-element.97.factors_in, ...), custom_call_target="tpu_custom_call" | custom-call | flops 5000000000 | bytes 36000000 | tf_op jit(solution)/shard_map/pallas_call | solution.py:714
  245.6 1.2 copy-done.4
  246.9 0.7 copy-done.9
  247.6 1.8 shard_map.284
  250.1 1.8 collective-permute-done.8
  252.1 0.9 collective-permute-start.9
  252.9 1.6 collective-permute-start.10
  254.5 1.1 collective-permute-start.11
  255.6 6.9 %all-to-all-done.4.partner = bf16[8,104,1024]{2,1,0:T(8,128)(2,1)} async-done(((bf16[8,104,1024]{2,1,0:T(8,128)(2,1)}), bf16[8,104,1024]{2,1,0:T(8,128)(2,1)}, u32[]{:S(2)}, u32[]{:S(2)}) %all-to-all-start.4) | async-done | bytes 1703968 | tf_op jit(solution)/shard_map/all_to_all | solution.py:1308
  262.5 10.3 %shard_map.285 = bf16[386,8192]{1,0:T(8,128)(2,1)} custom-call(s32[16]{0:T(128)} %reshape.419.starts, s32[8192]{0:T(1024)} %bitcast.199, bf16[8,104,1024]{2,1,0:T(8,128)(2,1)} %all-to-all-done.4.partner, bf16[386,8192]{1,0:T(8,128)(2,1)} %get-tuple-element.106.mailbox), custom_call_target="tpu_custom_call", output_to_operand_aliasing={{}: (3, {})} | custom-call | flops 10000000 | bytes 8000000 | tf_op jit(solution)/shard_map/pallas_call | solution.py:1203
  273.1 1.9 collective-permute-start.14
  275.1 1.4 collective-permute-start.12
  276.5 1.9 collective-permute-done.13
  278.4 0.6 collective-permute-done.14
  279.6 1.2 collective-permute-done.15
  280.8 2.2 collective-permute-start.17
  283.2 1.4 collective-permute-start.16
  284.7 2.9 collective-permute-done.18
  287.7 1.0 collective-permute-start.20
  288.7 1.9 collective-permute-start.21
  291.2 1.0 collective-permute-done.20
  292.2 1.9 collective-permute-done.21
  295.6 0.7 fusion.35
  (138 shorter events, 9.6 us)
Async XLA Ops:
  2.4 7.5 %collective-permute-start = (bf16[216,128]{1,0:T(8,128)(2,1)S(1)}, bf16[216,128]{1,0:T(8,128)(2,1)S(1)}, u32[]{:S(2)}, u32[]{:S(2)}) collective-permute-start(bf16[216,128]{1,0:T(8,128)(2,1)S(1)} %pad_maximum_fusion), channel_id=1, source_target_pairs={{0,2},{1,3},{2,0},{3,1},{4,6},{5,7},{6,4},{7,5},{8,10},{9,11},{10,... | collective-permute-start | bytes 165896 | tf_op jit(solution)/shard_map/ppermute | solution.py:1221
  5.4 6.1 %collective-permute-start.1 = (bf16[216,128]{1,0:T(8,128)(2,1)S(1)}, bf16[216,128]{1,0:T(8,128)(2,1)S(1)}, u32[]{:S(2)}, u32[]{:S(2)}) collective-permute-start(bf16[216,128]{1,0:T(8,128)(2,1)S(1)} %pad_maximum_fusion), channel_id=1, source_target_pairs={{0,4},{1,5},{2,6},{3,7},{4,0},{5,1},{6,2},{7,3},{8,12},{9,13},{10,... | collective-permute-start | bytes 165896 | tf_op jit(solution)/shard_map/ppermute | solution.py:1221
  8.0 6.0 %collective-permute-start.2 = (bf16[216,128]{1,0:T(8,128)(2,1)S(1)}, bf16[216,128]{1,0:T(8,128)(2,1)S(1)}, u32[]{:S(2)}, u32[]{:S(2)}) collective-permute-start(bf16[216,128]{1,0:T(8,128)(2,1)S(1)} %pad_maximum_fusion), channel_id=1, source_target_pairs={{0,6},{1,7},{2,4},{3,5},{4,2},{5,3},{6,0},{7,1},{8,14},{9,15},{10,... | collective-permute-start | bytes 165896 | tf_op jit(solution)/shard_map/ppermute | solution.py:1221
  14.0 14.4 %collective-permute-start.4 = (bf16[4,88,128]{2,1,0:T(8,128)(2,1)S(1)}, bf16[4,88,128]{2,1,0:T(8,128)(2,1)S(1)}, u32[]{:S(2)}, u32[]{:S(2)}) collective-permute-start(bf16[4,88,128]{2,1,0:T(8,128)(2,1)S(1)} %fusion.24), channel_id=1, source_target_pairs={{0,8},{8,0},{16,24},{24,16},{1,9},{9,1},{17,25},{25,17},{2,10},{10... | collective-permute-start | bytes 270344 | tf_op jit(solution)/shard_map/ppermute | solution.py:1221
  15.5 12.9 %collective-permute-start.5 = (bf16[4,88,128]{2,1,0:T(8,128)(2,1)S(1)}, bf16[4,88,128]{2,1,0:T(8,128)(2,1)S(1)}, u32[]{:S(2)}, u32[]{:S(2)}) collective-permute-start(bf16[4,88,128]{2,1,0:T(8,128)(2,1)S(1)} %fusion.24), channel_id=1, source_target_pairs={{0,16},{8,24},{16,0},{24,8},{1,17},{9,25},{17,1},{25,9},{2,18},{10... | collective-permute-start | bytes 270344 | tf_op jit(solution)/shard_map/ppermute | solution.py:1221
  17.0 11.4 %collective-permute-start.6 = (bf16[4,88,128]{2,1,0:T(8,128)(2,1)S(1)}, bf16[4,88,128]{2,1,0:T(8,128)(2,1)S(1)}, u32[]{:S(2)}, u32[]{:S(2)}) collective-permute-start(bf16[4,88,128]{2,1,0:T(8,128)(2,1)S(1)} %fusion.24), channel_id=1, source_target_pairs={{0,24},{8,16},{16,8},{24,0},{1,25},{9,17},{17,9},{25,1},{2,26},{10... | collective-permute-start | bytes 270344 | tf_op jit(solution)/shard_map/ppermute | solution.py:1221
  17.5 11.7 %collective-permute-start.3 = (bf16[4,128,128]{2,1,0:T(8,128)(2,1)S(1)}, bf16[4,128,128]{2,1,0:T(8,128)(2,1)S(1)}, u32[]{:S(2)}, u32[]{:S(2)}) collective-permute-start(bf16[4,128,128]{2,1,0:T(8,128)(2,1)S(1)} %fusion.19), channel_id=1, source_target_pairs={{0,1},{1,0},{2,3},{3,2},{4,5},{5,4},{6,7},{7,6},{8,9},{9,8},{10,11... | collective-permute-start | bytes 393224 | tf_op jit(solution)/shard_map/ppermute | solution.py:1221
  19.8 3.8 %copy-start.7 = (f32[100,128]{1,0:T(8,128)S(1)}, f32[100,128]{1,0:T(8,128)}, u32[]{:S(2)}) copy-start(f32[100,128]{1,0:T(8,128)} %constant.208.clone.freq) | copy-start | bytes 153604
  19.8 41.5 %all-to-all-start.1 = ((bf16[8,186,512]{2,1,0:T(8,128)(2,1)}), bf16[8,186,512]{2,1,0:T(8,128)(2,1)S(1)}, u32[]{:S(2)}, u32[]{:S(2)}) async-start(bf16[8,186,512]{2,1,0:T(8,128)(2,1)} %broadcast_in_dim.137), calls=%async_computation.1 | async-start | bytes 3145728 | tf_op jit(solution)/shard_map/all_to_all | solution.py:1308
  27.1 1.2 copy-start
  28.5 1.9 collective-permute-start.7
  31.5 0.9 copy-start.13
  59.6 6.1 %copy-start.22 = (s32[1,1,3,512]{3,1,2,0:T(1,128)S(1)}, s32[1,1,3,512]{3,1,2,0:T(1,128)}, u32[]{:S(2)}) copy-start(s32[1,1,3,512]{3,1,2,0:T(1,128)} %param.29) | copy-start | bytes 18436
  59.7 6.1 %copy-start.24 = (s32[1,1,8]{2,1,0:T(1,128)S(1)}, s32[1,1,8]{2,1,0:T(1,128)}, u32[]{:S(2)}) copy-start(s32[1,1,8]{2,1,0:T(1,128)} %param.28) | copy-start | bytes 100
  59.7 6.4 %copy-start.17 = (s32[1,1,8,1024]{3,2,1,0:T(8,128)S(1)}, s32[1,1,8,1024]{3,2,1,0:T(8,128)}, u32[]{:S(2)}) copy-start(s32[1,1,8,1024]{3,2,1,0:T(8,128)} %param.27) | copy-start | bytes 98308
  59.7 18.7 %copy-start.23 = (s32[1,1,512]{2,1,0:T(1,128)S(1)}, s32[1,1,512]{2,1,0:T(1,128)}, u32[]{:S(2)}) copy-start(s32[1,1,512]{2,1,0:T(1,128)} %param.34) | copy-start | bytes 6148
  61.3 17.8 %copy-start.12 = (bf16[8,186,512]{2,1,0:T(8,128)(2,1)}, bf16[8,186,512]{2,1,0:T(8,128)(2,1)S(1)}, u32[]{:S(2)}) copy-start(bf16[8,186,512]{2,1,0:T(8,128)(2,1)S(1)} %all-to-all-done.1.edges) | copy-start | bytes 4571140
  61.3 17.8 %copy-start.18 = (s32[1,1,1536,10]{2,1,3,0:T(1,128)S(1)}, s32[1,1,1536,10]{2,1,3,0:T(1,128)}, u32[]{:S(2)}) copy-start(s32[1,1,1536,10]{2,1,3,0:T(1,128)} %param.31) | copy-start | bytes 184324
  61.3 17.9 %copy-start.16 = (s32[1,1,1536,10]{2,1,3,0:T(1,128)S(1)}, s32[1,1,1536,10]{2,1,3,0:T(1,128)}, u32[]{:S(2)}) copy-start(s32[1,1,1536,10]{2,1,3,0:T(1,128)} %param.30) | copy-start | bytes 184324
  61.3 45.1 %all-to-all-start = ((bf16[8,104,1024]{2,1,0:T(8,128)(2,1)}), bf16[8,104,1024]{2,1,0:T(8,128)(2,1)}, u32[]{:S(2)}, u32[]{:S(2)}) async-start(bf16[8,104,1024]{2,1,0:T(8,128)(2,1)} %get-tuple-element.70), calls=%async_computation | async-start | bytes 3407872 | tf_op jit(solution)/shard_map/all_to_all | solution.py:1308
  66.1 5.0 %copy-start.21 = (s32[1,4,2,128]{3,1,2,0:T(4,128)}, s32[1,4,2,128]{3,1,2,0:T(4,128)S(1)}, u32[]{:S(2)}) copy-start(s32[1,4,2,128]{3,1,2,0:T(4,128)S(1)} %copy.46) | copy-start | bytes 12292
  79.5 8.8 %copy-start.2 = (bf16[100,8192]{1,0:T(8,128)(2,1)S(1)}, bf16[100,8192]{1,0:T(8,128)(2,1)}, u32[]{:S(2)}) copy-start(bf16[100,8192]{1,0:T(8,128)(2,1)} %get-tuple-element.71.s_cols.own) | copy-start | bytes 4915204
  79.5 8.8 %copy-start.6 = (s32[8192]{0:T(1024)S(1)}, s32[8192]{0:T(1024)}, u32[]{:S(2)}) copy-start(s32[8192]{0:T(1024)} %get-tuple-element.171.index) | copy-start | bytes 98308
  86.5 1.7 copy-start.3
  99.2 1.2 copy-start.1
  106.4 62.0 %all-to-all-start.2 = ((bf16[8,112,1024]{2,1,0:T(8,128)(2,1)}), bf16[8,112,1024]{2,1,0:T(8,128)(2,1)S(1)}, u32[]{:S(2)}, u32[]{:S(2)}) async-start(bf16[8,112,1024]{2,1,0:T(8,128)(2,1)} %copy-done.1), calls=%async_computation.2 | async-start | bytes 3670016 | tf_op jit(solution)/shard_map/all_to_all | solution.py:1308
  168.4 47.4 %all-to-all-start.3 = ((bf16[8,104,1024]{2,1,0:T(8,128)(2,1)}), bf16[8,104,1024]{2,1,0:T(8,128)(2,1)S(1)}, u32[]{:S(2)}, u32[]{:S(2)}) async-start(bf16[8,104,1024]{2,1,0:T(8,128)(2,1)} %get-tuple-element.86), calls=%async_computation.3 | async-start | bytes 3407872 | tf_op jit(solution)/shard_map/all_to_all | solution.py:1308
  173.4 8.1 %copy-start.10 = (s32[1024]{0:T(1024)S(1)}, s32[1024]{0:T(1024)}, u32[]{:S(2)}) copy-start(s32[1024]{0:T(1024)} %get-tuple-element.91.index) | copy-start | bytes 12292
  176.3 0.6 copy-start.15
  215.8 6.0 %copy-start.11 = (bf16[8,104,1024]{2,1,0:T(8,128)(2,1)}, bf16[8,104,1024]{2,1,0:T(8,128)(2,1)S(1)}, u32[]{:S(2)}) copy-start(bf16[8,104,1024]{2,1,0:T(8,128)(2,1)S(1)} %all-to-all-done.3.got) | copy-start | bytes 5111812
  215.8 46.7 %all-to-all-start.4 = ((bf16[8,104,1024]{2,1,0:T(8,128)(2,1)}), bf16[8,104,1024]{2,1,0:T(8,128)(2,1)}, u32[]{:S(2)}, u32[]{:S(2)}) async-start(bf16[8,104,1024]{2,1,0:T(8,128)(2,1)} %shard_map.281), calls=%async_computation.4 | async-start | bytes 3407872 | tf_op jit(solution)/shard_map/all_to_all | solution.py:1308
  221.8 23.8 %copy-start.5 = (f32[1448,128]{1,0:T(8,128)S(1)}, f32[1448,128]{1,0:T(8,128)}, u32[]{:S(2)}) copy-start(f32[1448,128]{1,0:T(8,128)} %get-tuple-element.100.att) | copy-start | bytes 2224132
  221.8 23.8 %copy-start.8 = (f32[8,128]{1,0:T(8,128)S(1)}, f32[8,128]{1,0:T(8,128)}, u32[]{:S(2)}) copy-start(f32[8,128]{1,0:T(8,128)} %get-tuple-element.101.losses) | copy-start | bytes 12292
  245.6 1.2 copy-start.4
  246.9 0.7 copy-start.9
  249.5 2.4 collective-permute-start.8
  252.1 20.7 %collective-permute-start.9 = (f32[1,4,1,88,128]{4,3,2,1,0:T(8,128)S(1)}, f32[1,4,1,88,128]{4,3,2,1,0:T(8,128)S(1)}, u32[]{:S(2)}, u32[]{:S(2)}) collective-permute-start(f32[1,4,1,88,128]{4,3,2,1,0:T(8,128)S(1)} %get-tuple-element.160), channel_id=1, source_target_pairs={{0,8},{8,0},{16,24},{24,16},{1,9},{9,1},{17,25},{25,17},{2,10},{10... | collective-permute-start | bytes 540680 | tf_op jit(solution)/shard_map/ppermute | solution.py:1221
  252.9 19.9 %collective-permute-start.10 = (f32[1,4,1,88,128]{4,3,2,1,0:T(8,128)S(1)}, f32[1,4,1,88,128]{4,3,2,1,0:T(8,128)S(1)}, u32[]{:S(2)}, u32[]{:S(2)}) collective-permute-start(f32[1,4,1,88,128]{4,3,2,1,0:T(8,128)S(1)} %get-tuple-element.159), channel_id=1, source_target_pairs={{0,16},{8,24},{16,0},{24,8},{1,17},{9,25},{17,1},{25,9},{2,18},{10... | collective-permute-start | bytes 540680 | tf_op jit(solution)/shard_map/ppermute | solution.py:1221
  254.5 41.1 %copy-start.14 = (f32[11264]{0:T(1024)S(1)}, f32[11264]{0:T(1024)}, u32[]{:S(2)}) copy-start(f32[11264]{0:T(1024)} %param.19) | copy-start | bytes 135172
  254.5 41.1 %copy-start.19 = (f32[11264]{0:T(1024)S(1)}, f32[11264]{0:T(1024)}, u32[]{:S(2)}) copy-start(f32[11264]{0:T(1024)} %param.20) | copy-start | bytes 135172
  254.5 41.1 %copy-start.20 = (f32[11264]{0:T(1024)S(1)}, f32[11264]{0:T(1024)}, u32[]{:S(2)}) copy-start(f32[11264]{0:T(1024)} %param.21) | copy-start | bytes 135172
  254.5 18.3 %collective-permute-start.11 = (f32[1,4,1,88,128]{4,3,2,1,0:T(8,128)S(1)}, f32[1,4,1,88,128]{4,3,2,1,0:T(8,128)S(1)}, u32[]{:S(2)}, u32[]{:S(2)}) collective-permute-start(f32[1,4,1,88,128]{4,3,2,1,0:T(8,128)S(1)} %get-tuple-element.158), channel_id=1, source_target_pairs={{0,24},{8,16},{16,8},{24,0},{1,25},{9,17},{17,9},{25,1},{2,26},{10... | collective-permute-start | bytes 540680 | tf_op jit(solution)/shard_map/ppermute | solution.py:1221
  272.9 5.5 %collective-permute-start.13 = (f32[1,1,1,88,128]{4,3,2,1,0:T(8,128)S(1)}, f32[1,1,1,88,128]{4,3,2,1,0:T(8,128)S(1)}, u32[]{:S(2)}, u32[]{:S(2)}) collective-permute-start(f32[1,1,1,88,128]{4,3,2,1,0:T(8,128)S(1)} %get-tuple-element.163), channel_id=1, source_target_pairs={{0,4},{1,5},{2,6},{3,7},{4,0},{5,1},{6,2},{7,3},{8,12},{9,13},{10,... | collective-permute-start | bytes 135176 | tf_op jit(solution)/shard_map/ppermute | solution.py:1221
  273.1 5.9 %collective-permute-start.14 = (f32[1,1,1,88,128]{4,3,2,1,0:T(8,128)S(1)}, f32[1,1,1,88,128]{4,3,2,1,0:T(8,128)S(1)}, u32[]{:S(2)}, u32[]{:S(2)}) collective-permute-start(f32[1,1,1,88,128]{4,3,2,1,0:T(8,128)S(1)} %get-tuple-element.162), channel_id=1, source_target_pairs={{0,6},{1,7},{2,4},{3,5},{4,2},{5,3},{6,0},{7,1},{8,14},{9,15},{10,... | collective-permute-start | bytes 135176 | tf_op jit(solution)/shard_map/ppermute | solution.py:1221
  275.1 4.4 %collective-permute-start.12 = (f32[1,1,1,88,128]{4,3,2,1,0:T(8,128)S(1)}, f32[1,1,1,88,128]{4,3,2,1,0:T(8,128)S(1)}, u32[]{:S(2)}, u32[]{:S(2)}) collective-permute-start(f32[1,1,1,88,128]{4,3,2,1,0:T(8,128)S(1)} %get-tuple-element.161), channel_id=1, source_target_pairs={{0,2},{1,3},{2,0},{3,1},{4,6},{5,7},{6,4},{7,5},{8,10},{9,11},{10,... | collective-permute-start | bytes 135176 | tf_op jit(solution)/shard_map/ppermute | solution.py:1221
  279.6 1.2 collective-permute-start.15
  280.8 3.8 %collective-permute-start.17 = (f32[8,128]{1,0:T(8,128)S(1)}, f32[8,128]{1,0:T(8,128)S(1)}, u32[]{:S(2)}, u32[]{:S(2)}) collective-permute-start(f32[8,128]{1,0:T(8,128)S(1)} %fusion.34), channel_id=1, source_target_pairs={{0,16},{8,24},{16,0},{24,8},{1,17},{9,25},{17,1},{25,9},{2,18},{10... | collective-permute-start | bytes 12296 | tf_op jit(solution)/shard_map/ppermute | solution.py:1221
  283.1 4.5 %collective-permute-start.18 = (f32[8,128]{1,0:T(8,128)S(1)}, f32[8,128]{1,0:T(8,128)S(1)}, u32[]{:S(2)}, u32[]{:S(2)}) collective-permute-start(f32[8,128]{1,0:T(8,128)S(1)} %fusion.34), channel_id=1, source_target_pairs={{0,24},{8,16},{16,8},{24,0},{1,25},{9,17},{17,9},{25,1},{2,26},{10... | collective-permute-start | bytes 12296 | tf_op jit(solution)/shard_map/ppermute | solution.py:1221
  283.2 4.4 %collective-permute-start.16 = (f32[8,128]{1,0:T(8,128)S(1)}, f32[8,128]{1,0:T(8,128)S(1)}, u32[]{:S(2)}, u32[]{:S(2)}) collective-permute-start(f32[8,128]{1,0:T(8,128)S(1)} %fusion.34), channel_id=1, source_target_pairs={{0,8},{8,0},{16,24},{24,16},{1,9},{9,1},{17,25},{25,17},{2,10},{10... | collective-permute-start | bytes 12296 | tf_op jit(solution)/shard_map/ppermute | solution.py:1221
  287.7 4.5 %collective-permute-start.20 = (f32[8,128]{1,0:T(8,128)S(1)}, f32[8,128]{1,0:T(8,128)S(1)}, u32[]{:S(2)}, u32[]{:S(2)}) collective-permute-start(f32[8,128]{1,0:T(8,128)S(1)} %add_add_fusion.3), channel_id=1, source_target_pairs={{0,4},{1,5},{2,6},{3,7},{4,0},{5,1},{6,2},{7,3},{8,12},{9,13},{10,... | collective-permute-start | bytes 12296 | tf_op jit(solution)/shard_map/ppermute | solution.py:1221
  288.7 5.4 %collective-permute-start.21 = (f32[8,128]{1,0:T(8,128)S(1)}, f32[8,128]{1,0:T(8,128)S(1)}, u32[]{:S(2)}, u32[]{:S(2)}) collective-permute-start(f32[8,128]{1,0:T(8,128)S(1)} %add_add_fusion.3), channel_id=1, source_target_pairs={{0,6},{1,7},{2,4},{3,5},{4,2},{5,3},{6,0},{7,1},{8,14},{9,15},{10,... | collective-permute-start | bytes 12296 | tf_op jit(solution)/shard_map/ppermute | solution.py:1221
  290.5 3.6 %collective-permute-start.19 = (f32[8,128]{1,0:T(8,128)S(1)}, f32[8,128]{1,0:T(8,128)S(1)}, u32[]{:S(2)}, u32[]{:S(2)}) collective-permute-start(f32[8,128]{1,0:T(8,128)S(1)} %add_add_fusion.3), channel_id=1, source_target_pairs={{0,2},{1,3},{2,0},{3,1},{4,6},{5,7},{6,4},{7,5},{8,10},{9,11},{10,... | collective-permute-start | bytes 12296 | tf_op jit(solution)/shard_map/ppermute | solution.py:1221
